TPU v7x, 256 devices: a whole 4x4x8 slice. The times are simulated.
256 devices in a mesh: seq: 32 (over y, x, core), fsdp: 8 (over z).
Axes of the slice: x: 4, y: 4, z: 8, core: 2. Of those that a mesh axis runs over, the one named last changes fastest.
Arguments:
- self_q: bfloat16 [8, 4096, 4096], P('fsdp', 'seq'), may hold values from -128 to 128
- self_k: bfloat16 [8, 4096, 4096], P('fsdp', 'seq'), may hold values from -32 to 32
- self_v: bfloat16 [8, 4096, 4096], P('fsdp', 'seq'), may hold values from -6 to 6
- cross_q: bfloat16 [8, 4096, 4096], P('fsdp', 'seq'), may hold values from -160 to 160
- audio: bfloat16 [8, 1024, 768], P('fsdp', 'seq'), may hold values from -6 to 6
- key_weight: bfloat16 [768, 4096], P('fsdp', 'seq'), may hold values from -0.21875 to 0.21875
- value_weight: bfloat16 [768, 4096], P('fsdp', 'seq'), may hold values from -0.21875 to 0.21875
- intersection: int32 [8, 64, 4], P('fsdp', 'seq'), may hold values from 0 to 63, as said below
- counts: int32 [8, 64], P('fsdp', 'seq'), may hold values from 1 to 4, as said below
- cotangent: bfloat16 [8, 4096, 4096], P('fsdp', 'seq'), may hold values from -6 to 6
Outputs:
- block_out: bfloat16 [8, 4096, 4096], P('fsdp', 'seq')
- audio_grad: float32 [8, 1024, 768], P('fsdp', 'seq')
Inputs may be any that keep to these rules, and one draw needn't show every extreme that they name: `intersection`: the first counts entries of a frame's list are distinct consecutive blocks, each within 3 blocks of block f for frame f; later entries are padding and are ignored. `counts`: every clip has a frame whose window holds 4 blocks.
All inputs are finite; a program needn't handle non-finite values.
Results may differ from a plain program's by a relative error of at most 0.015.
The roundings to bfloat16 on the way count: a program that leaves them out, or rounds other values in their place, can miss the bound.
Values may be sent and summed in bfloat16 or wider, within the bound.
No kernel may reach another device: no remote copies, remote signals or barrier semaphores. Data moves between devices by JAX's collectives and lax.ppermute only.
A program may use at most 128 MiB of HBM per device.

v0:
```python
import functools

import jax
import jax.numpy as jnp
from jax import lax
from jax.experimental import pallas as pl
from jax.experimental.pallas import tpu as pltpu
from jax.sharding import PartitionSpec as P

HD = 128
AB = 16
MAXB = 4
REACH = 3
SCALING = HD ** (-0.5)
EXP2_SCALING = SCALING * 1.4426950408889634
F32 = jnp.float32
BF16 = jnp.bfloat16
VMEM_BYTES = 48 * 1024 * 1024


def passed_along(block, axis, distance):
    devices = range(lax.axis_size(axis))
    route = [(i - distance, i) for i in devices if i - distance in devices]
    return lax.ppermute(block, axis, route)


def gathered_by_doubling(block, axis):
    size = lax.axis_size(axis)
    here = lax.axis_index(axis)
    step = 1
    while step < size:
        other = lax.ppermute(block, axis, [(i, i ^ step) for i in range(size)])
        upper = (here & step) != 0
        block = jnp.concatenate(
            [jnp.where(upper, other, block), jnp.where(upper, block, other)], axis=0
        )
        step *= 2
    return block


def heads_first_kernel(group, q_ref, k_ref, v_ref, out_ref):
    rows = q_ref.shape[0]
    for head in range(group):
        cols = slice(head * HD, (head + 1) * HD)
        out_ref[head, 0:rows] = q_ref[:, cols]
        out_ref[head, rows : 2 * rows] = k_ref[:, cols]
        out_ref[head, 2 * rows : 3 * rows] = v_ref[:, cols]


def heads_first(q_local, k_local, v_local):
    _, rows, width = q_local.shape
    heads = width // HD
    group = 8
    block = pl.BlockSpec((None, rows, group * HD), lambda i: (0, 0, i))
    return pl.pallas_call(
        functools.partial(heads_first_kernel, group),
        grid=(heads // group,),
        in_specs=[block] * 3,
        out_specs=pl.BlockSpec((group, 3 * rows, HD), lambda i: (i, 0, 0)),
        out_shape=jax.ShapeDtypeStruct((heads, 3 * rows, HD), BF16),
        compiler_params=pltpu.CompilerParams(vmem_limit_bytes=VMEM_BYTES),
        cost_estimate=pl.CostEstimate(
            flops=0, bytes_accessed=6 * rows * width * 2, transcendentals=0
        ),
        name="heads_first",
    )(q_local, k_local, v_local)


def self_attention_kernel(
    block_rows, block_keys, q_ref, k_ref, v_ref, out_ref, keys_t, values_x, scores, tops
):
    length = out_ref.shape[0]
    key_blocks = length // block_keys
    query_blocks = length // block_rows
    chunk = q_ref.shape[1]
    for piece in range(length // chunk):
        keys_t[:, piece * chunk : (piece + 1) * chunk] = k_ref[piece].T
        values_x[piece * chunk : (piece + 1) * chunk, :HD] = v_ref[piece]
    values_x[:, HD:] = jnp.ones((length, HD), BF16)
    per_block = block_rows // chunk

    def queries_of(block):
        rows = q_ref[pl.ds(block * per_block, per_block)]
        return rows.reshape(block_rows, HD)

    def highest(top, part):
        for group in range(part.shape[1] // HD):
            lanes = part[:, group * HD : (group + 1) * HD]
            top = lanes if top is None else jnp.maximum(top, lanes)
        return top

    def row_max(top):
        return jnp.broadcast_to(jnp.max(top, axis=1, keepdims=True), (block_rows, HD))

    first = queries_of(0)
    top = None
    for j in range(key_blocks):
        keys = slice(j * block_keys, (j + 1) * block_keys)
        part = jnp.dot(first, keys_t[:, keys], preferred_element_type=F32)
        scores[0, :, keys] = part
        top = highest(top, part)
    tops[0] = row_max(top)

    def body(i, carry):
        slot = lax.rem(i, 2)
        later = 1 - slot
        queries = queries_of(jnp.minimum(i + 1, query_blocks - 1))
        top_here = tops[slot][:, :1]
        top = None
        total = None
        for j in range(key_blocks):
            keys = slice(j * block_keys, (j + 1) * block_keys)
            part = jnp.dot(queries, keys_t[:, keys], preferred_element_type=F32)
            scores[later, :, keys] = part
            top = highest(top, part)
            raised = jnp.exp2((scores[slot, :, keys] - top_here) * EXP2_SCALING).astype(BF16)
            mixed = jnp.dot(raised, values_x[keys, :], preferred_element_type=F32)
            total = mixed if total is None else total + mixed
        tops[later] = row_max(top)
        rows = pl.ds(pl.multiple_of(i * block_rows, block_rows), block_rows)
        out_ref[rows, :] = (total[:, :HD] / total[:, HD:]).astype(BF16)
        return carry

    lax.fori_loop(0, query_blocks, body, 0)


def attend_self(qkv):
    sources, _, rows, _ = qkv.shape
    length = sources * rows
    block_rows, block_keys = 512, 512

    def part(which):
        return pl.BlockSpec((sources, None, rows, HD), lambda i: (0, which, 0, 0))

    return pl.pallas_call(
        functools.partial(self_attention_kernel, block_rows, block_keys),
        grid=(1,),
        in_specs=[part(0), part(1), part(2)],
        out_specs=pl.BlockSpec((length, HD), lambda i: (0, 0)),
        out_shape=jax.ShapeDtypeStruct((length, HD), BF16),
        scratch_shapes=[
            pltpu.VMEM((HD, length), BF16),
            pltpu.VMEM((length, 2 * HD), BF16),
            pltpu.VMEM((2, block_rows, length), F32),
            pltpu.VMEM((2, block_rows, HD), F32),
        ],
        compiler_params=pltpu.CompilerParams(vmem_limit_bytes=VMEM_BYTES),
        cost_estimate=pl.CostEstimate(
            flops=8 * length * length * HD,
            bytes_accessed=8 * length * HD,
            transcendentals=length * length,
        ),
        name="self_attention",
    )(qkv, qkv, qkv)


def contract(a, b, dim_a, dim_b):
    return lax.dot_general(a, b, (((dim_a,), (dim_b,)), ((), ())), preferred_element_type=F32)


def cross_kernel(
    group, near_ref, live_ref, proj_ref, q_ref, grad_ref, own_ref, out_ref, audio_grad_ref
):
    @pl.when(pl.program_id(0) == 0)
    def _():
        audio_grad_ref[...] = jnp.zeros_like(audio_grad_ref)

    near = near_ref[...]
    live = live_ref[...] > 0
    sent = None
    for head in range(group):
        cols = slice(head * HD, (head + 1) * HD)
        proj = proj_ref[head]
        both = jnp.dot(near, proj, preferred_element_type=F32).astype(BF16)
        keys = both[:, :HD]
        values = both[:, HD:]
        queries = q_ref[:, cols]
        grads = grad_ref[:, cols]
        scores = contract(queries, keys, 1, 1) * SCALING
        scores = jnp.where(live, scores, -1e30)
        raised = jnp.exp(scores - jnp.max(scores, axis=1, keepdims=True))
        weights = raised / jnp.sum(raised, axis=1, keepdims=True)
        weights_b = weights.astype(BF16)
        mixed = jnp.dot(weights_b, values, preferred_element_type=F32)
        out_ref[:, cols] = (own_ref[head].astype(F32) + mixed).astype(BF16)
        d_values = contract(weights_b, grads, 0, 0).astype(BF16)
        d_probs = contract(grads, values, 1, 1)
        weighed = weights * d_probs
        d_scores = (
            weighed - weights * jnp.sum(weighed, axis=1, keepdims=True)
        ).astype(BF16)
        d_keys = (contract(d_scores, queries, 0, 0) * SCALING).astype(BF16)
        d_both = jnp.concatenate([d_keys, d_values], axis=1)
        term = contract(d_both, proj, 1, 1)
        sent = term if sent is None else sent + term
    audio_grad_ref[...] += sent


def cross_attention(near, live, proj, queries, grads, own):
    heads, features, _ = proj.shape
    rows, width = queries.shape
    band = near.shape[0]
    group = 4
    return pl.pallas_call(
        functools.partial(cross_kernel, group),
        grid=(heads // group,),
        in_specs=[
            pl.BlockSpec((band, features), lambda i: (0, 0)),
            pl.BlockSpec((rows, band), lambda i: (0, 0)),
            pl.BlockSpec((group, features, 2 * HD), lambda i: (i, 0, 0)),
            pl.BlockSpec((rows, group * HD), lambda i: (0, i)),
            pl.BlockSpec((rows, group * HD), lambda i: (0, i)),
            pl.BlockSpec((group, rows, HD), lambda i: (i, 0, 0)),
        ],
        out_specs=[
            pl.BlockSpec((rows, group * HD), lambda i: (0, i)),
            pl.BlockSpec((band, features), lambda i: (0, 0)),
        ],
        out_shape=[
            jax.ShapeDtypeStruct((rows, width), BF16),
            jax.ShapeDtypeStruct((band, features), F32),
        ],
        compiler_params=pltpu.CompilerParams(vmem_limit_bytes=VMEM_BYTES),
        cost_estimate=pl.CostEstimate(
            flops=8 * band * features * 2 * width,
            bytes_accessed=proj.size * 2 + 8 * rows * width,
            transcendentals=rows * band * heads,
        ),
        name="cross_attention",
    )(near, live, proj, queries, grads, own)


def live_band(window_ids, live_counts, band_first, band_blocks, frame_rows):
    slots = jnp.arange(window_ids.shape[1], dtype=jnp.int32)
    blocks = band_first + jnp.arange(band_blocks, dtype=jnp.int32)
    hits = (window_ids[:, :, None] == blocks[None, None, :]) & (
        slots[None, :, None] < live_counts[:, None, None]
    )
    live = jnp.any(hits, axis=1).astype(F32)
    return jnp.repeat(jnp.repeat(live, AB, axis=1), frame_rows, axis=0)


def local(
    self_q,
    self_k,
    self_v,
    cross_q,
    audio,
    key_weight,
    value_weight,
    intersection,
    counts,
    cotangent,
):
    both = jnp.concatenate([key_weight, value_weight], axis=1)
    cols = gathered_by_doubling(both[None], "fsdp")
    cols = cols.reshape(1, -1, 2 * HD)
    proj = lax.all_gather(cols, "seq", axis=0, tiled=True)

    rows = self_q.shape[1]
    qkv = heads_first(self_q, self_k, self_v)
    qkv = lax.all_to_all(qkv, "seq", split_axis=0, concat_axis=0, tiled=True)
    qkv = qkv.reshape(qkv.shape[0], 3, rows, HD)
    own_heads = attend_self(qkv)
    own_heads = own_heads.reshape(-1, rows, HD)
    own_tokens = lax.all_to_all(own_heads, "seq", split_axis=0, concat_axis=0, tiled=True)

    owned = audio.shape[1]
    half = owned // 2
    here = lax.axis_index("seq")
    frames = intersection.shape[1]
    mine = audio[0]
    near = jnp.concatenate(
        [
            passed_along(mine[half:], "seq", 2),
            passed_along(mine, "seq", 1),
            mine,
            passed_along(mine, "seq", -1),
            passed_along(mine[:half], "seq", -2),
        ],
        axis=0,
    )
    band_blocks = near.shape[0] // AB
    band_first = here * (owned // AB) - REACH
    live = live_band(intersection[0], counts[0], band_first, band_blocks, rows // frames)
    block_out, band = cross_attention(
        near, live, proj, cross_q[0], cotangent[0], own_tokens
    )

    total = band[half + owned : half + 2 * owned]
    band_b = band.astype(BF16)
    before = passed_along(band_b[half : half + owned], "seq", -1)
    after = passed_along(band_b[half + 2 * owned : half + 3 * owned], "seq", 1)
    far_before = passed_along(band_b[:half], "seq", -2)
    far_after = passed_along(band_b[half + 3 * owned :], "seq", 2)
    far = jnp.concatenate([far_after, far_before], axis=0)
    total = total + before.astype(F32) + after.astype(F32) + far.astype(F32)
    return (block_out[None], total[None])


def solution(mesh):
    in_specs = (
        P("fsdp", "seq", None),
        P("fsdp", "seq", None),
        P("fsdp", "seq", None),
        P("fsdp", "seq", None),
        P("fsdp", "seq", None),
        P("fsdp", "seq"),
        P("fsdp", "seq"),
        P("fsdp", "seq", None),
        P("fsdp", "seq"),
        P("fsdp", "seq", None),
    )
    out_specs = (P("fsdp", "seq", None), P("fsdp", "seq", None))
    return jax.shard_map(local, mesh=mesh, in_specs=in_specs, out_specs=out_specs, check_vma=False)
```

profile of v0, /device:TPU:1, one launch (start us, length us, event | category | flops | bytes accessed | tf_op | source)
XLA Modules:
  0.0 202.9 jit_solution(14503026544806872692)
XLA Ops:
  7.2 0.9 maximum_bitcast_fusion
  8.2 2.5 %collective-permute-start.4 = (bf16[1,96,256]{2,1,0:T(8,128)(2,1)S(1)}, bf16[1,96,256]{2,1,0:T(8,128)(2,1)S(1)}, u32[]{:S(2)}, u32[]{:S(2)}) collective-permute-start(bf16[1,96,256]{2,1,0:T(8,128)(2,1)S(1)} %maximum_bitcast_fusion), channel_id=1, source_target_pairs={{0,1},{1,0},{2,3},{3,2},{4,5},{5,4},{6,7},{7,6},{8,9},{9,8},{10,11... | collective-permute-start | bytes 147464 | tf_op jit(solution)/shard_map/ppermute | solution.py:32
  10.7 1.5 collective-permute-done.4
  12.2 0.8 broadcast_select_fusion.5
  13.0 3.1 %collective-permute-start.5 = (bf16[2,96,256]{2,1,0:T(8,128)(2,1)S(1)}, bf16[2,96,256]{2,1,0:T(8,128)(2,1)S(1)}, u32[]{:S(2)}, u32[]{:S(2)}) collective-permute-start(bf16[2,96,256]{2,1,0:T(8,128)(2,1)S(1)} %pad_maximum_fusion.2), channel_id=1, source_target_pairs={{0,2},{1,3},{2,0},{3,1},{4,6},{5,7},{6,4},{7,5},{8,10},{9,11},{10,... | collective-permute-start | bytes 294920 | tf_op jit(solution)/shard_map/ppermute | solution.py:32
  16.1 2.0 collective-permute-done.5
  18.1 7.2 %collective-permute-start.6 = (bf16[4,96,256]{2,1,0:T(8,128)(2,1)S(1)}, bf16[4,96,256]{2,1,0:T(8,128)(2,1)}, u32[]{:S(2)}, u32[]{:S(2)}) collective-permute-start(bf16[4,96,256]{2,1,0:T(8,128)(2,1)S(1)} %pad_maximum_fusion.1), channel_id=1, source_target_pairs={{0,4},{1,5},{2,6},{3,7},{4,0},{5,1},{6,2},{7,3},{8,12},{9,13},{10,... | collective-permute-start | bytes 589832 | tf_op jit(solution)/shard_map/ppermute | solution.py:32
  25.3 3.2 %collective-permute-done.6 = bf16[4,96,256]{2,1,0:T(8,128)(2,1)} collective-permute-done((bf16[4,96,256]{2,1,0:T(8,128)(2,1)S(1)}, bf16[4,96,256]{2,1,0:T(8,128)(2,1)}, u32[]{:S(2)}, u32[]{:S(2)}) %collective-permute-start.6) | collective-permute-done | bytes 196640 | tf_op jit(solution)/shard_map/ppermute | solution.py:32
  28.5 1.0 broadcast_select_fusion.1
  29.5 0.8 pad_maximum_fusion
  30.3 2.6 %heads_first.1 = bf16[32,384,128]{2,1,0:T(8,128)(2,1)} custom-call(bf16[1,128,4096]{2,1,0:T(8,128)(2,1)S(1)} %copy-done.1, bf16[1,128,4096]{2,1,0:T(8,128)(2,1)S(1)} %copy-done.2, bf16[1,128,4096]{2,1,0:T(8,128)(2,1)S(1)} %copy-done.3), custom_call_target="tpu_custom_call" | custom-call | bytes 6291456 | tf_op jit(solution)/shard_map/heads_first/pallas_call | solution.py:55
  32.9 15.4 %all-to-all-start = ((bf16[32,384,128]{2,1,0:T(8,128)(2,1)}), bf16[32,384,128]{2,1,0:T(8,128)(2,1)S(1)}, u32[]{:S(2)}, u32[]{:S(2)}) async-start(bf16[32,384,128]{2,1,0:T(8,128)(2,1)} %heads_first.1), calls=%async_computation | async-start | bytes 6291456 | tf_op jit(solution)/shard_map/all_to_all | solution.py:262
  48.3 2.1 %collective-permute-start.2 = (bf16[32,768]{1,0:T(8,128)(2,1)S(1)}, bf16[32,768]{1,0:T(8,128)(2,1)S(1)}, u32[]{:S(2)}, u32[]{:S(2)}) collective-permute-start(bf16[32,768]{1,0:T(8,128)(2,1)S(1)} %bitcast.31), channel_id=1, source_target_pairs={{8,0},{16,8},{24,16},{32,24},{40,32},{48,40},{56,48},{64,56},{72,6... | collective-permute-start | bytes 147464 | tf_op jit(solution)/shard_map/ppermute | solution.py:24
  50.5 3.4 %collective-permute-start.1 = (bf16[32,768]{1,0:T(8,128)(2,1)S(1)}, bf16[32,768]{1,0:T(8,128)(2,1)S(1)}, u32[]{:S(2)}, u32[]{:S(2)}) collective-permute-start(bf16[32,768]{1,0:T(8,128)(2,1)S(1)} %bitcast.32), channel_id=1, source_target_pairs={{0,8},{8,16},{16,24},{24,32},{32,40},{40,48},{48,56},{56,64},{64,7... | collective-permute-start | bytes 147464 | tf_op jit(solution)/shard_map/ppermute | solution.py:24
  53.9 1.3 collective-permute-start.3
  55.2 4.0 %collective-permute-start = (bf16[16,768]{1,0:T(8,128)(2,1)S(1)}, bf16[16,768]{1,0:T(8,128)(2,1)S(1)}, u32[]{:S(2)}, u32[]{:S(2)}) collective-permute-start(bf16[16,768]{1,0:T(8,128)(2,1)S(1)} %get-tuple-element.17), channel_id=1, source_target_pairs={{0,16},{8,24},{16,32},{24,40},{32,48},{40,56},{48,64},{56,72},{64,... | collective-permute-start | bytes 73736 | tf_op jit(solution)/shard_map/ppermute | solution.py:24
  59.2 34.5 %all-to-all-done = bf16[32,384,128]{2,1,0:T(8,128)(2,1)S(1)} async-done(((bf16[32,384,128]{2,1,0:T(8,128)(2,1)}), bf16[32,384,128]{2,1,0:T(8,128)(2,1)S(1)}, u32[]{:S(2)}, u32[]{:S(2)}) %all-to-all-start) | async-done | bytes 3145760 | tf_op jit(solution)/shard_map/all_to_all | solution.py:262
  93.7 30.2 %self_attention.1 = bf16[4096,128]{1,0:T(8,128)(2,1)S(1)} custom-call(bf16[32,3,128,128]{3,2,1,0:T(8,128)(2,1)S(1)} %bitcast.23, bf16[32,3,128,128]{3,2,1,0:T(8,128)(2,1)S(1)} %bitcast.24, bf16[32,3,128,128]{3,2,1,0:T(8,128)(2,1)S(1)} %bitcast.25), custom_call_target="tpu_custom_call" | custom-call | flops 17179869184 | bytes 4194304 | tf_op jit(solution)/shard_map/self_attention/pallas_call | solution.py:135
  123.9 1.0 copy-done
  124.9 5.9 %all-to-all-start.1 = ((bf16[32,128,128]{2,1,0:T(8,128)(2,1)}), bf16[32,128,128]{2,1,0:T(8,128)(2,1)S(1)}, u32[]{:S(2)}, u32[]{:S(2)}) async-start(bf16[32,128,128]{2,1,0:T(8,128)(2,1)} %bitcast.26), calls=%async_computation.1 | async-start | bytes 2097152 | tf_op jit(solution)/shard_map/all_to_all | solution.py:266
  130.9 0.1 and_reduce_fusion
  131.0 0.1 reshape.54
  131.2 16.8 %all-to-all-done.1.own_ref = bf16[32,128,128]{2,1,0:T(8,128)(2,1)S(1)} async-done(((bf16[32,128,128]{2,1,0:T(8,128)(2,1)}), bf16[32,128,128]{2,1,0:T(8,128)(2,1)S(1)}, u32[]{:S(2)}, u32[]{:S(2)}) %all-to-all-start.1) | async-done | bytes 1048608 | tf_op jit(solution)/shard_map/all_to_all | solution.py:266
  148.1 1.2 copy-done.4
  149.3 1.2 copy-done.5
  150.5 32.4 %cross_attention.1 = (bf16[128,4096]{1,0:T(8,128)(2,1)}, f32[128,768]{1,0:T(8,128)S(1)}) custom-call(bf16[128,768]{1,0:T(8,128)(2,1)S(1)} %constant_dynamic-update-slice_fusion.near_ref, f32[128,128]{1,0:T(8,128)S(1)} %bitcast.27, bf16[32,768,256]{2,1,0:T(8,128)(2,1)} %all-gather.2.cloned.1.call-done.proj_ref, bf16[128,4096]{1,0:T(8,128)(2,1)S(1)} %bitcast.28, ...), custom_call_target="tpu_custom_call" | custom-call | flops 6442450944 | bytes 16777216 | tf_op jit(solution)/shard_map/cross_attention/pallas_call | solution.py:204
  183.0 2.3 %collective-permute-start.7 = (bf16[32,768]{1,0:T(8,128)(2,1)S(1)}, bf16[32,768]{1,0:T(8,128)(2,1)S(1)}, u32[]{:S(2)}, u32[]{:S(2)}) collective-permute-start(bf16[32,768]{1,0:T(8,128)(2,1)S(1)} %get-tuple-element.10), channel_id=1, source_target_pairs={{8,0},{16,8},{24,16},{32,24},{40,32},{48,40},{56,48},{64,56},{72,6... | collective-permute-start | bytes 147464 | tf_op jit(solution)/shard_map/ppermute | solution.py:24
  185.3 3.3 %collective-permute-start.8 = (bf16[32,768]{1,0:T(8,128)(2,1)S(1)}, bf16[32,768]{1,0:T(8,128)(2,1)S(1)}, u32[]{:S(2)}, u32[]{:S(2)}) collective-permute-start(bf16[32,768]{1,0:T(8,128)(2,1)S(1)} %get-tuple-element.11), channel_id=1, source_target_pairs={{0,8},{8,16},{16,24},{24,32},{32,40},{40,48},{48,56},{56,64},{64,7... | collective-permute-start | bytes 147464 | tf_op jit(solution)/shard_map/ppermute | solution.py:24
  188.6 2.3 %collective-permute-start.9 = (bf16[16,768]{1,0:T(8,128)(2,1)S(1)}, bf16[16,768]{1,0:T(8,128)(2,1)S(1)}, u32[]{:S(2)}, u32[]{:S(2)}) collective-permute-start(bf16[16,768]{1,0:T(8,128)(2,1)S(1)} %get-tuple-element.8), channel_id=1, source_target_pairs={{0,16},{8,24},{16,32},{24,40},{32,48},{40,56},{48,64},{56,72},{64,... | collective-permute-start | bytes 73736 | tf_op jit(solution)/shard_map/ppermute | solution.py:24
  190.8 1.3 collective-permute-start.10
  192.1 3.3 %collective-permute-done.10 = bf16[16,768]{1,0:T(8,128)(2,1)S(1)} collective-permute-done((bf16[16,768]{1,0:T(8,128)(2,1)S(1)}, bf16[16,768]{1,0:T(8,128)(2,1)S(1)}, u32[]{:S(2)}, u32[]{:S(2)}) %collective-permute-start.10) | collective-permute-done | bytes 24608 | tf_op jit(solution)/shard_map/ppermute | solution.py:24
  195.4 0.7 add_bitcast_fusion
  (42 shorter events, 0.4 us)
Async XLA Ops:
  7.2 23.1 %copy-start.3 = (bf16[1,128,4096]{2,1,0:T(8,128)(2,1)S(1)}, bf16[1,128,4096]{2,1,0:T(8,128)(2,1)}, u32[]{:S(2)}) copy-start(bf16[1,128,4096]{2,1,0:T(8,128)(2,1)} %v_ref.1) | copy-start | bytes 3145732
  7.2 23.1 %copy-start.2 = (bf16[1,128,4096]{2,1,0:T(8,128)(2,1)S(1)}, bf16[1,128,4096]{2,1,0:T(8,128)(2,1)}, u32[]{:S(2)}) copy-start(bf16[1,128,4096]{2,1,0:T(8,128)(2,1)} %k_ref.1) | copy-start | bytes 3145732
  7.2 23.1 %copy-start.1 = (bf16[1,128,4096]{2,1,0:T(8,128)(2,1)S(1)}, bf16[1,128,4096]{2,1,0:T(8,128)(2,1)}, u32[]{:S(2)}) copy-start(bf16[1,128,4096]{2,1,0:T(8,128)(2,1)} %q_ref.1) | copy-start | bytes 3145732
  7.2 140.9 %all-gather.2.cloned.1.call-start = ((), (), s32[]{:S(2)}) async-start(), calls=%async_computation.2 | async-start | bytes 12976128 | tf_op jit(solution)/shard_map/all_gather | solution.py:258
  8.2 4.0 %collective-permute-start.4 = (bf16[1,96,256]{2,1,0:T(8,128)(2,1)S(1)}, bf16[1,96,256]{2,1,0:T(8,128)(2,1)S(1)}, u32[]{:S(2)}, u32[]{:S(2)}) collective-permute-start(bf16[1,96,256]{2,1,0:T(8,128)(2,1)S(1)} %maximum_bitcast_fusion), channel_id=1, source_target_pairs={{0,1},{1,0},{2,3},{3,2},{4,5},{5,4},{6,7},{7,6},{8,9},{9,8},{10,11... | collective-permute-start | bytes 147464 | tf_op jit(solution)/shard_map/ppermute | solution.py:32
  13.0 5.1 %collective-permute-start.5 = (bf16[2,96,256]{2,1,0:T(8,128)(2,1)S(1)}, bf16[2,96,256]{2,1,0:T(8,128)(2,1)S(1)}, u32[]{:S(2)}, u32[]{:S(2)}) collective-permute-start(bf16[2,96,256]{2,1,0:T(8,128)(2,1)S(1)} %pad_maximum_fusion.2), channel_id=1, source_target_pairs={{0,2},{1,3},{2,0},{3,1},{4,6},{5,7},{6,4},{7,5},{8,10},{9,11},{10,... | collective-permute-start | bytes 294920 | tf_op jit(solution)/shard_map/ppermute | solution.py:32
  18.1 10.4 %collective-permute-start.6 = (bf16[4,96,256]{2,1,0:T(8,128)(2,1)S(1)}, bf16[4,96,256]{2,1,0:T(8,128)(2,1)}, u32[]{:S(2)}, u32[]{:S(2)}) collective-permute-start(bf16[4,96,256]{2,1,0:T(8,128)(2,1)S(1)} %pad_maximum_fusion.1), channel_id=1, source_target_pairs={{0,4},{1,5},{2,6},{3,7},{4,0},{5,1},{6,2},{7,3},{8,12},{9,13},{10,... | collective-permute-start | bytes 589832 | tf_op jit(solution)/shard_map/ppermute | solution.py:32
  32.9 15.4 %copy-start.6 = (bf16[1,32,768]{2,1,0:T(8,128)(2,1)S(1)}, bf16[1,32,768]{2,1,0:T(8,128)(2,1)}, u32[]{:S(2)}) copy-start(bf16[1,32,768]{2,1,0:T(8,128)(2,1)} %param.14) | copy-start | bytes 147460
  32.9 60.8 %all-to-all-start = ((bf16[32,384,128]{2,1,0:T(8,128)(2,1)}), bf16[32,384,128]{2,1,0:T(8,128)(2,1)S(1)}, u32[]{:S(2)}, u32[]{:S(2)}) async-start(bf16[32,384,128]{2,1,0:T(8,128)(2,1)} %heads_first.1), calls=%async_computation | async-start | bytes 6291456 | tf_op jit(solution)/shard_map/all_to_all | solution.py:262
  48.3 82.8 %collective-permute-start.2 = (bf16[32,768]{1,0:T(8,128)(2,1)S(1)}, bf16[32,768]{1,0:T(8,128)(2,1)S(1)}, u32[]{:S(2)}, u32[]{:S(2)}) collective-permute-start(bf16[32,768]{1,0:T(8,128)(2,1)S(1)} %bitcast.31), channel_id=1, source_target_pairs={{8,0},{16,8},{24,16},{32,24},{40,32},{48,40},{56,48},{64,56},{72,6... | collective-permute-start | bytes 147464 | tf_op jit(solution)/shard_map/ppermute | solution.py:24
  50.5 80.7 %collective-permute-start.1 = (bf16[32,768]{1,0:T(8,128)(2,1)S(1)}, bf16[32,768]{1,0:T(8,128)(2,1)S(1)}, u32[]{:S(2)}, u32[]{:S(2)}) collective-permute-start(bf16[32,768]{1,0:T(8,128)(2,1)S(1)} %bitcast.32), channel_id=1, source_target_pairs={{0,8},{8,16},{16,24},{24,32},{32,40},{40,48},{48,56},{56,64},{64,7... | collective-permute-start | bytes 147464 | tf_op jit(solution)/shard_map/ppermute | solution.py:24
  53.9 77.3 %collective-permute-start.3 = (bf16[16,768]{1,0:T(8,128)(2,1)S(1)}, bf16[16,768]{1,0:T(8,128)(2,1)S(1)}, u32[]{:S(2)}, u32[]{:S(2)}) collective-permute-start(bf16[16,768]{1,0:T(8,128)(2,1)S(1)} %get-tuple-element.16), channel_id=1, source_target_pairs={{16,0},{24,8},{32,16},{40,24},{48,32},{56,40},{64,48},{72,56},{80,... | collective-permute-start | bytes 73736 | tf_op jit(solution)/shard_map/ppermute | solution.py:24
  55.2 75.9 %collective-permute-start = (bf16[16,768]{1,0:T(8,128)(2,1)S(1)}, bf16[16,768]{1,0:T(8,128)(2,1)S(1)}, u32[]{:S(2)}, u32[]{:S(2)}) collective-permute-start(bf16[16,768]{1,0:T(8,128)(2,1)S(1)} %get-tuple-element.17), channel_id=1, source_target_pairs={{0,16},{8,24},{16,32},{24,40},{32,48},{40,56},{48,64},{56,72},{64,... | collective-permute-start | bytes 73736 | tf_op jit(solution)/shard_map/ppermute | solution.py:24
  93.7 37.1 %copy-start.8 = (s32[1,2]{1,0:T(1,128)S(1)}, s32[1,2]{1,0:T(1,128)}, u32[]{:S(2)}) copy-start(s32[1,2]{1,0:T(1,128)} %param.18) | copy-start | bytes 28
  93.7 37.2 %copy-start.7 = (s32[1,2,4]{2,1,0:T(2,128)S(1)}, s32[1,2,4]{2,1,0:T(2,128)}, u32[]{:S(2)}) copy-start(s32[1,2,4]{2,1,0:T(2,128)} %param.17) | copy-start | bytes 100
  123.9 1.0 copy-start
  124.9 23.2 %all-to-all-start.1 = ((bf16[32,128,128]{2,1,0:T(8,128)(2,1)}), bf16[32,128,128]{2,1,0:T(8,128)(2,1)S(1)}, u32[]{:S(2)}, u32[]{:S(2)}) async-start(bf16[32,128,128]{2,1,0:T(8,128)(2,1)} %bitcast.26), calls=%async_computation.1 | async-start | bytes 2097152 | tf_op jit(solution)/shard_map/all_to_all | solution.py:266
  148.1 1.2 copy-start.4
  149.3 1.2 copy-start.5
  183.0 12.4 %collective-permute-start.7 = (bf16[32,768]{1,0:T(8,128)(2,1)S(1)}, bf16[32,768]{1,0:T(8,128)(2,1)S(1)}, u32[]{:S(2)}, u32[]{:S(2)}) collective-permute-start(bf16[32,768]{1,0:T(8,128)(2,1)S(1)} %get-tuple-element.10), channel_id=1, source_target_pairs={{8,0},{16,8},{24,16},{32,24},{40,32},{48,40},{56,48},{64,56},{72,6... | collective-permute-start | bytes 147464 | tf_op jit(solution)/shard_map/ppermute | solution.py:24
  185.3 10.1 %collective-permute-start.8 = (bf16[32,768]{1,0:T(8,128)(2,1)S(1)}, bf16[32,768]{1,0:T(8,128)(2,1)S(1)}, u32[]{:S(2)}, u32[]{:S(2)}) collective-permute-start(bf16[32,768]{1,0:T(8,128)(2,1)S(1)} %get-tuple-element.11), channel_id=1, source_target_pairs={{0,8},{8,16},{16,24},{24,32},{32,40},{40,48},{48,56},{56,64},{64,7... | collective-permute-start | bytes 147464 | tf_op jit(solution)/shard_map/ppermute | solution.py:24
  188.6 3.6 %collective-permute-start.9 = (bf16[16,768]{1,0:T(8,128)(2,1)S(1)}, bf16[16,768]{1,0:T(8,128)(2,1)S(1)}, u32[]{:S(2)}, u32[]{:S(2)}) collective-permute-start(bf16[16,768]{1,0:T(8,128)(2,1)S(1)} %get-tuple-element.8), channel_id=1, source_target_pairs={{0,16},{8,24},{16,32},{24,40},{32,48},{40,56},{48,64},{56,72},{64,... | collective-permute-start | bytes 73736 | tf_op jit(solution)/shard_map/ppermute | solution.py:24
  190.8 4.6 %collective-permute-start.10 = (bf16[16,768]{1,0:T(8,128)(2,1)S(1)}, bf16[16,768]{1,0:T(8,128)(2,1)S(1)}, u32[]{:S(2)}, u32[]{:S(2)}) collective-permute-start(bf16[16,768]{1,0:T(8,128)(2,1)S(1)} %get-tuple-element.9), channel_id=1, source_target_pairs={{16,0},{24,8},{32,16},{40,24},{48,32},{56,40},{64,48},{72,56},{80,... | collective-permute-start | bytes 73736 | tf_op jit(solution)/shard_map/ppermute | solution.py:24
Sparse Core Ops, SparseCore 0:
  30.4 101.2 all-gather.1
where the time goes:
time: 206 us; the launch traced here: 203 us
  Pallas kernels  65.2 us (32%)
  waiting for transfers between devices  61.3 us (30%)
  starting transfers between devices  54.1 us (26%)
  between operations  14.3 us (7%)
  other arithmetic  4.34 us (2%)
  local copies, waits for them, and re-layouts  3.64 us (2%)
    all_to_all x1, waiting for transfers between devices, local(): qkv = lax.all_to_all(qkv, 'seq', split_axis=0, concat_axis=0, tiled=True)  34.5 us
    pallas_call x1, Pallas kernels, cross_attention(): pl.pallas_call(functools.partial(cross_kernel, group), grid=(heads // gro...  32.4 us
    pallas_call x1, Pallas kernels, attend_self(): pl.pallas_call(functools.partial(self_attention_kernel, block_rows, block...  30.2 us
    ppermute x8, starting transfers between devices, passed_along(): return lax.ppermute(block, axis, route)  20 us
    all_to_all x1, waiting for transfers between devices, local(): lax.all_to_all(own_heads, 'seq', split_axis=0, concat_axis=0, tiled=True)  16.8 us
    all_to_all x1, starting transfers between devices, local(): qkv = lax.all_to_all(qkv, 'seq', split_axis=0, concat_axis=0, tiled=True)  15.4 us
    ppermute x3, starting transfers between devices, gathered_by_doubling(): other = lax.ppermute(block, axis, [(i, i ^ step) for i in range(size)])  12.9 us
    ppermute x3, waiting for transfers between devices, gathered_by_doubling(): other = lax.ppermute(block, axis, [(i, i ^ step) for i in range(size)])  6.66 us
  transfers between devices with their start and end apart: 14, of which 6 were waited for; matrix products, arithmetic and copies ran while one was open for 0% of the time, Pallas kernels for 16%

commit v1 on v0

--- a/solution.py
+++ b/solution.py
@@ -16,6 +16,7 @@
 F32 = jnp.float32
 BF16 = jnp.bfloat16
 VMEM_BYTES = 48 * 1024 * 1024
+CROSS_GROUP = 8
 
 
 def passed_along(block, axis, distance):
@@ -24,18 +25,14 @@
     return lax.ppermute(block, axis, route)
 
 
-def gathered_by_doubling(block, axis):
+def round_ring(block, axis, distance):
     size = lax.axis_size(axis)
-    here = lax.axis_index(axis)
-    step = 1
-    while step < size:
-        other = lax.ppermute(block, axis, [(i, i ^ step) for i in range(size)])
-        upper = (here & step) != 0
-        block = jnp.concatenate(
-            [jnp.where(upper, other, block), jnp.where(upper, block, other)], axis=0
-        )
-        step *= 2
-    return block
+    return lax.ppermute(block, axis, [(i, (i + distance) % size) for i in range(size)])
+
+
+def from_other_core(block):
+    size = lax.axis_size("seq")
+    return lax.ppermute(block, "seq", [(i, i ^ 1) for i in range(size)])
 
 
 def heads_first_kernel(group, q_ref, k_ref, v_ref, out_ref):
@@ -66,13 +63,13 @@
     )(q_local, k_local, v_local)
 
 
-def self_attention_kernel(
-    block_rows, block_keys, q_ref, k_ref, v_ref, out_ref, keys_t, values_x, scores, tops
-):
-    length = out_ref.shape[0]
+def self_attention_kernel(block_rows, block_keys, operands, *refs):
+    q_ref, k_ref, v_ref = refs[:3]
+    out_ref, keys_t, values_x, scores, tops = refs[operands:]
+    chunk = q_ref.shape[1]
+    length = k_ref.shape[0] * chunk
     key_blocks = length // block_keys
-    query_blocks = length // block_rows
-    chunk = q_ref.shape[1]
+    query_blocks = out_ref.shape[0] // block_rows
     for piece in range(length // chunk):
         keys_t[:, piece * chunk : (piece + 1) * chunk] = k_ref[piece].T
         values_x[piece * chunk : (piece + 1) * chunk, :HD] = v_ref[piece]
@@ -124,19 +121,31 @@
     lax.fori_loop(0, query_blocks, body, 0)
 
 
-def attend_self(qkv):
+def attend_self(qkv, part, parts, so_far=None):
     sources, _, rows, _ = qkv.shape
     length = sources * rows
     block_rows, block_keys = 512, 512
-
-    def part(which):
+    q_sources = sources // parts
+
+    def whole(which):
         return pl.BlockSpec((sources, None, rows, HD), lambda i: (0, which, 0, 0))
 
+    operands = [qkv, qkv, qkv]
+    in_specs = [
+        pl.BlockSpec((q_sources, None, rows, HD), lambda i: (part, 0, 0, 0)),
+        whole(1),
+        whole(2),
+    ]
+    aliases = {}
+    if so_far is not None:
+        operands.append(so_far)
+        in_specs.append(pl.BlockSpec(memory_space=pl.ANY))
+        aliases = {3: 0}
     return pl.pallas_call(
-        functools.partial(self_attention_kernel, block_rows, block_keys),
+        functools.partial(self_attention_kernel, block_rows, block_keys, len(operands)),
         grid=(1,),
-        in_specs=[part(0), part(1), part(2)],
-        out_specs=pl.BlockSpec((length, HD), lambda i: (0, 0)),
+        in_specs=in_specs,
+        out_specs=pl.BlockSpec((length // parts, HD), lambda i: (part, 0)),
         out_shape=jax.ShapeDtypeStruct((length, HD), BF16),
         scratch_shapes=[
             pltpu.VMEM((HD, length), BF16),
@@ -144,14 +153,15 @@
             pltpu.VMEM((2, block_rows, length), F32),
             pltpu.VMEM((2, block_rows, HD), F32),
         ],
+        input_output_aliases=aliases,
         compiler_params=pltpu.CompilerParams(vmem_limit_bytes=VMEM_BYTES),
         cost_estimate=pl.CostEstimate(
-            flops=8 * length * length * HD,
+            flops=8 * length * length * HD // parts,
             bytes_accessed=8 * length * HD,
-            transcendentals=length * length,
+            transcendentals=length * length // parts,
         ),
         name="self_attention",
-    )(qkv, qkv, qkv)
+    )(*operands)
 
 
 def contract(a, b, dim_a, dim_b):
@@ -159,75 +169,131 @@
 
 
 def cross_kernel(
-    group, near_ref, live_ref, proj_ref, q_ref, grad_ref, own_ref, out_ref, audio_grad_ref
+    group,
+    pieces,
+    place_ref,
+    near_ref,
+    live_ref,
+    q_ref,
+    grad_ref,
+    *refs,
 ):
+    proj_refs = refs[: 2 * pieces]
+    out_ref, audio_grad_ref, proj = refs[2 * pieces :]
+
     @pl.when(pl.program_id(0) == 0)
     def _():
         audio_grad_ref[...] = jnp.zeros_like(audio_grad_ref)
 
+    depth = proj_refs[0].shape[1]
+    for kind in range(2):
+        lanes = pl.ds(pl.multiple_of(place_ref[pieces + kind], HD), HD)
+        for piece in range(pieces):
+            rows = pl.ds(pl.multiple_of(place_ref[piece], 32), depth)
+            proj[:, rows, lanes] = proj_refs[kind * pieces + piece][...]
+
     near = near_ref[...]
     live = live_ref[...] > 0
+    heads = range(group)
+    cols = [slice(head * HD, (head + 1) * HD) for head in heads]
+    both = [
+        jnp.dot(near, proj[head], preferred_element_type=F32).astype(BF16) for head in heads
+    ]
+    keys = [part[:, :HD] for part in both]
+    values = [part[:, HD:] for part in both]
+    scores = [contract(q_ref[:, cols[head]], keys[head], 1, 1) for head in heads]
+    d_probs = [contract(grad_ref[:, cols[head]], values[head], 1, 1) for head in heads]
+    weights = []
+    for head in heads:
+        masked = jnp.where(live, scores[head], -1e30)
+        top = jnp.max(masked, axis=1, keepdims=True)
+        raised = jnp.exp2((masked - top) * EXP2_SCALING)
+        weights.append(raised / jnp.sum(raised, axis=1, keepdims=True))
+    weights_b = [part.astype(BF16) for part in weights]
+    d_scores = []
+    for head in heads:
+        weighed = weights[head] * d_probs[head]
+        inner = jnp.sum(weighed, axis=1, keepdims=True)
+        d_scores.append((weighed - weights[head] * inner).astype(BF16))
+    for head in heads:
+        out_ref[:, cols[head]] = jnp.dot(
+            weights_b[head], values[head], preferred_element_type=F32
+        )
+    d_values = [
+        contract(weights_b[head], grad_ref[:, cols[head]], 0, 0).astype(BF16) for head in heads
+    ]
+    d_keys = [
+        (contract(d_scores[head], q_ref[:, cols[head]], 0, 0) * SCALING).astype(BF16)
+        for head in heads
+    ]
     sent = None
-    for head in range(group):
-        cols = slice(head * HD, (head + 1) * HD)
-        proj = proj_ref[head]
-        both = jnp.dot(near, proj, preferred_element_type=F32).astype(BF16)
-        keys = both[:, :HD]
-        values = both[:, HD:]
-        queries = q_ref[:, cols]
-        grads = grad_ref[:, cols]
-        scores = contract(queries, keys, 1, 1) * SCALING
-        scores = jnp.where(live, scores, -1e30)
-        raised = jnp.exp(scores - jnp.max(scores, axis=1, keepdims=True))
-        weights = raised / jnp.sum(raised, axis=1, keepdims=True)
-        weights_b = weights.astype(BF16)
-        mixed = jnp.dot(weights_b, values, preferred_element_type=F32)
-        out_ref[:, cols] = (own_ref[head].astype(F32) + mixed).astype(BF16)
-        d_values = contract(weights_b, grads, 0, 0).astype(BF16)
-        d_probs = contract(grads, values, 1, 1)
-        weighed = weights * d_probs
-        d_scores = (
-            weighed - weights * jnp.sum(weighed, axis=1, keepdims=True)
-        ).astype(BF16)
-        d_keys = (contract(d_scores, queries, 0, 0) * SCALING).astype(BF16)
-        d_both = jnp.concatenate([d_keys, d_values], axis=1)
-        term = contract(d_both, proj, 1, 1)
+    for head in heads:
+        d_both = jnp.concatenate([d_keys[head], d_values[head]], axis=1)
+        term = contract(d_both, proj[head], 1, 1)
         sent = term if sent is None else sent + term
     audio_grad_ref[...] += sent
 
 
-def cross_attention(near, live, proj, queries, grads, own):
-    heads, features, _ = proj.shape
+def cross_attention(place, near, live, queries, grads, own_pieces, other_pieces):
+    heads, depth, _ = own_pieces[0].shape
+    pieces = len(own_pieces)
+    features = depth * pieces
     rows, width = queries.shape
     band = near.shape[0]
-    group = 4
+    group = CROSS_GROUP
+    piece = pl.BlockSpec((group, depth, HD), lambda i: (i, 0, 0))
     return pl.pallas_call(
-        functools.partial(cross_kernel, group),
+        functools.partial(cross_kernel, group, pieces),
         grid=(heads // group,),
         in_specs=[
+            pl.BlockSpec(memory_space=pltpu.SMEM),
             pl.BlockSpec((band, features), lambda i: (0, 0)),
             pl.BlockSpec((rows, band), lambda i: (0, 0)),
-            pl.BlockSpec((group, features, 2 * HD), lambda i: (i, 0, 0)),
             pl.BlockSpec((rows, group * HD), lambda i: (0, i)),
             pl.BlockSpec((rows, group * HD), lambda i: (0, i)),
-            pl.BlockSpec((group, rows, HD), lambda i: (i, 0, 0)),
-        ],
+        ]
+        + [piece] * (2 * pieces),
         out_specs=[
             pl.BlockSpec((rows, group * HD), lambda i: (0, i)),
             pl.BlockSpec((band, features), lambda i: (0, 0)),
         ],
         out_shape=[
-            jax.ShapeDtypeStruct((rows, width), BF16),
+            jax.ShapeDtypeStruct((rows, width), F32),
             jax.ShapeDtypeStruct((band, features), F32),
         ],
+        scratch_shapes=[pltpu.VMEM((group, features, 2 * HD), BF16)],
         compiler_params=pltpu.CompilerParams(vmem_limit_bytes=VMEM_BYTES),
         cost_estimate=pl.CostEstimate(
             flops=8 * band * features * 2 * width,
-            bytes_accessed=proj.size * 2 + 8 * rows * width,
+            bytes_accessed=4 * features * width + 8 * rows * width,
             transcendentals=rows * band * heads,
         ),
         name="cross_attention",
-    )(near, live, proj, queries, grads, own)
+    )(place, near, live, queries, grads, *own_pieces, *other_pieces)
+
+
+def merge_kernel(group, own_ref, cross_ref, out_ref):
+    for head in range(group):
+        cols = slice(head * HD, (head + 1) * HD)
+        out_ref[:, cols] = (own_ref[head].astype(F32) + cross_ref[:, cols]).astype(BF16)
+
+
+def merged(own_tokens, cross_out):
+    heads, rows, _ = own_tokens.shape
+    group = 8
+    flat = pl.BlockSpec((rows, group * HD), lambda i: (0, i))
+    return pl.pallas_call(
+        functools.partial(merge_kernel, group),
+        grid=(heads // group,),
+        in_specs=[pl.BlockSpec((group, rows, HD), lambda i: (i, 0, 0)), flat],
+        out_specs=flat,
+        out_shape=jax.ShapeDtypeStruct(cross_out.shape, BF16),
+        compiler_params=pltpu.CompilerParams(vmem_limit_bytes=VMEM_BYTES),
+        cost_estimate=pl.CostEstimate(
+            flops=cross_out.size, bytes_accessed=8 * cross_out.size, transcendentals=0
+        ),
+        name="merge",
+    )(own_tokens, cross_out)
 
 
 def live_band(window_ids, live_counts, band_first, band_blocks, frame_rows):
@@ -252,23 +318,28 @@
     counts,
     cotangent,
 ):
-    both = jnp.concatenate([key_weight, value_weight], axis=1)
-    cols = gathered_by_doubling(both[None], "fsdp")
-    cols = cols.reshape(1, -1, 2 * HD)
-    proj = lax.all_gather(cols, "seq", axis=0, tiled=True)
-
+    here = lax.axis_index("seq")
+    layer = lax.axis_index("fsdp")
+    layers = lax.axis_size("fsdp")
     rows = self_q.shape[1]
+    members = lax.axis_size("seq")
+    depth = key_weight.shape[0]
+
+    even = (jnp.arange(members) % 2 == 0)[:, None, None]
+    handed = jnp.where(even, key_weight[None], value_weight[None])
+    start = lax.all_to_all(handed, "seq", split_axis=0, concat_axis=0, tiled=True)
     qkv = heads_first(self_q, self_k, self_v)
+    start, qkv = lax.optimization_barrier((start, qkv))
+
+    up, down = [start], [start]
+    for _ in range((layers - 1) // 2):
+        up.append(round_ring(up[-1], "fsdp", 1))
+        down.append(round_ring(down[-1], "fsdp", -1))
+    arrived = up[:-1] + down[1:-1]
+    other_arrived = [from_other_core(piece) for piece in arrived]
     qkv = lax.all_to_all(qkv, "seq", split_axis=0, concat_axis=0, tiled=True)
-    qkv = qkv.reshape(qkv.shape[0], 3, rows, HD)
-    own_heads = attend_self(qkv)
-    own_heads = own_heads.reshape(-1, rows, HD)
-    own_tokens = lax.all_to_all(own_heads, "seq", split_axis=0, concat_axis=0, tiled=True)
-
     owned = audio.shape[1]
     half = owned // 2
-    here = lax.axis_index("seq")
-    frames = intersection.shape[1]
     mine = audio[0]
     near = jnp.concatenate(
         [
@@ -280,12 +351,48 @@
         ],
         axis=0,
     )
+    qkv, other_arrived, near = lax.optimization_barrier((qkv, other_arrived, near))
+    qkv = qkv.reshape(qkv.shape[0], 3, rows, HD)
+
+    own_heads = attend_self(qkv, 0, 2)
+    last_up, last_down, own_heads, qkv = lax.optimization_barrier(
+        (up[-1], down[-1], own_heads, qkv)
+    )
+    middle = members // 2
+    opposite = [
+        round_ring(last_up[:middle], "fsdp", 1),
+        round_ring(last_down[middle:], "fsdp", -1),
+    ]
+    last = [last_up, last_down]
+    other_last = [from_other_core(piece) for piece in last]
+    own_heads = attend_self(qkv, 1, 2, own_heads)
+    opposite, other_last, own_heads = lax.optimization_barrier((opposite, other_last, own_heads))
+    opposite = jnp.concatenate(opposite, axis=0)
+    own_tokens = lax.all_to_all(
+        own_heads.reshape(-1, rows, HD), "seq", split_axis=0, concat_axis=0, tiled=True
+    )
+
+    own_pieces = arrived + last + [opposite]
+    other_pieces = other_arrived + other_last + [from_other_core(opposite)]
+    steps = len(up)
+    inner = steps - 1
+    shifts = [-i for i in range(inner)] + [i for i in range(1, inner)] + [-inner, inner, steps]
+    core = lax.rem(here, 2)
+    place = jnp.concatenate(
+        [
+            lax.rem(layer + jnp.array([shift % layers for shift in shifts]), layers) * depth,
+            jnp.stack([core * HD, (1 - core) * HD]),
+        ]
+    ).astype(jnp.int32)
+
+    frames = intersection.shape[1]
     band_blocks = near.shape[0] // AB
     band_first = here * (owned // AB) - REACH
     live = live_band(intersection[0], counts[0], band_first, band_blocks, rows // frames)
-    block_out, band = cross_attention(
-        near, live, proj, cross_q[0], cotangent[0], own_tokens
-    )
+    cross_out, band = cross_attention(
+        place, near, live, cross_q[0], cotangent[0], own_pieces, other_pieces
+    )
+    block_out = merged(own_tokens, cross_out)
 
     total = band[half + owned : half + 2 * owned]
     band_b = band.astype(BF16)

time: 206 us -> 170 us (0.83)
  the two profiles are of different devices: /device:TPU:1 before, /device:TPU:6 now
where the time goes in v1:
time: 170 us; the launch traced here: 169 us
  starting transfers between devices  63 us (37%)
  Pallas kernels  51 us (30%)
  waiting for transfers between devices  41 us (24%)
  local copies, waits for them, and re-layouts  10.2 us (6%)
  other arithmetic  2.73 us (2%)
    pallas_call x2, Pallas kernels, attend_self(): pl.pallas_call(functools.partial(self_attention_kernel, block_rows, block...  32.1 us
    ppermute x8, waiting for transfers between devices, round_ring(): lax.ppermute(block, axis, [(i, (i + distance) % size) for i in range(size)])  26 us
    ppermute x8, starting transfers between devices, passed_along(): return lax.ppermute(block, axis, route)  23.6 us
    ppermute x8, starting transfers between devices, round_ring(): lax.ppermute(block, axis, [(i, (i + distance) % size) for i in range(size)])  15.6 us
    pallas_call x1, Pallas kernels, cross_attention(): pl.pallas_call(functools.partial(cross_kernel, group, pieces), grid=(head...  14.5 us
    ppermute x8, waiting for transfers between devices, passed_along(): return lax.ppermute(block, axis, route)  9.31 us
    all_to_all x1, starting transfers between devices, local(): lax.all_to_all(own_heads.reshape(-1, rows, HD), 'seq', split_axis=0, conc...  8.26 us
    unnamed x33, local copies, waits for them, and re-layouts  7.94 us
  transfers between devices with their start and end apart: 27, of which 9 were waited for; matrix products, arithmetic and copies ran while one was open for 1% of the time, Pallas kernels for 29%

profile of v1, /device:TPU:6, one launch (start us, length us, event | category | flops | bytes accessed | tf_op | source)
XLA Modules:
  0.0 169.1 jit_solution(12371939613298306755)
XLA Ops:
  0.6 1.8 %broadcast_select_fusion = bf16[32,96,128]{2,1,0:T(8,128)(2,1)} fusion(pred[32]{0:T(512)(128)(4,1)S(1)} %fusion.2, bf16[96,128]{1,0:T(8,128)(2,1)} %param.17, bf16[96,128]{1,0:T(8,128)(2,1)} %param.16), kind=kLoop, calls=%fused_computation | loop fusion | flops 393216 | bytes 835616 | tf_op jit(solution)/shard_map/jit(_where)/select_n | solution.py:329
  2.4 7.6 %all-to-all-start = ((bf16[32,96,128]{2,1,0:T(8,128)(2,1)}), bf16[32,96,128]{2,1,0:T(8,128)(2,1)S(1)}, u32[]{:S(2)}, u32[]{:S(2)}) async-start(bf16[32,96,128]{2,1,0:T(8,128)(2,1)} %broadcast_select_fusion), calls=%async_computation | async-start | bytes 1572864 | tf_op jit(solution)/shard_map/all_to_all | solution.py:330
  11.2 1.2 copy-done.3
  12.4 1.2 copy-done.4
  13.7 2.6 %heads_first.1 = bf16[32,384,128]{2,1,0:T(8,128)(2,1)} custom-call(bf16[1,128,4096]{2,1,0:T(8,128)(2,1)S(1)} %copy-done.2, bf16[1,128,4096]{2,1,0:T(8,128)(2,1)S(1)} %copy-done.3, bf16[1,128,4096]{2,1,0:T(8,128)(2,1)S(1)} %copy-done.4), custom_call_target="tpu_custom_call" | custom-call | bytes 6291456 | tf_op jit(solution)/shard_map/heads_first/pallas_call | solution.py:52
  16.3 5.7 %all-to-all-done.refs_0_ = bf16[32,96,128]{2,1,0:T(8,128)(2,1)S(1)} async-done(((bf16[32,96,128]{2,1,0:T(8,128)(2,1)}), bf16[32,96,128]{2,1,0:T(8,128)(2,1)S(1)}, u32[]{:S(2)}, u32[]{:S(2)}) %all-to-all-start) | async-done | bytes 786464 | tf_op jit(solution)/shard_map/all_to_all | solution.py:330
  22.9 6.5 %all-to-all-start.1 = ((bf16[32,384,128]{2,1,0:T(8,128)(2,1)}), bf16[32,384,128]{2,1,0:T(8,128)(2,1)S(1)}, u32[]{:S(2)}, u32[]{:S(2)}) async-start(bf16[32,384,128]{2,1,0:T(8,128)(2,1)} %heads_first.1), calls=%async_computation.1 | async-start | bytes 6291456 | tf_op jit(solution)/shard_map/all_to_all | solution.py:340
  29.5 5.9 %collective-permute-start.3 = (bf16[32,96,128]{2,1,0:T(8,128)(2,1)}, bf16[32,96,128]{2,1,0:T(8,128)(2,1)}, u32[]{:S(2)}, u32[]{:S(2)}) collective-permute-start(bf16[32,96,128]{2,1,0:T(8,128)(2,1)} %copy-done.5), channel_id=1, source_target_pairs={{0,7},{1,0},{2,1},{3,2},{4,3},{5,4},{6,5},{7,6},{8,15},{9,8},{10,9... | collective-permute-start | bytes 2359304 | tf_op jit(solution)/shard_map/ppermute | solution.py:30
  35.4 17.4 %collective-permute-done.3.refs_3_ = bf16[32,96,128]{2,1,0:T(8,128)(2,1)} collective-permute-done((bf16[32,96,128]{2,1,0:T(8,128)(2,1)}, bf16[32,96,128]{2,1,0:T(8,128)(2,1)}, u32[]{:S(2)}, u32[]{:S(2)}) %collective-permute-start.3) | collective-permute-done | bytes 786464 | tf_op jit(solution)/shard_map/ppermute | solution.py:30
  52.8 3.7 %collective-permute-start.4 = (bf16[32,96,128]{2,1,0:T(8,128)(2,1)}, bf16[32,96,128]{2,1,0:T(8,128)(2,1)}, u32[]{:S(2)}, u32[]{:S(2)}) collective-permute-start(bf16[32,96,128]{2,1,0:T(8,128)(2,1)} %collective-permute-done.3.refs_3_), channel_id=1, source_target_pairs={{0,7},{1,0},{2,1},{3,2},{4,3},{5,4},{6,5},{7,6},{8,15},{9,8},{10,9... | collective-permute-start | bytes 2359304 | tf_op jit(solution)/shard_map/ppermute | solution.py:30
  56.5 2.8 %collective-permute-start.14 = (bf16[16,768]{1,0:T(8,128)(2,1)S(1)}, bf16[16,768]{1,0:T(8,128)(2,1)S(1)}, u32[]{:S(2)}, u32[]{:S(2)}) collective-permute-start(bf16[16,768]{1,0:T(8,128)(2,1)S(1)} %get-tuple-element.46), channel_id=1, source_target_pairs={{16,0},{24,8},{32,16},{40,24},{48,32},{56,40},{64,48},{72,56},{80,... | collective-permute-start | bytes 73736 | tf_op jit(solution)/shard_map/ppermute | solution.py:25
  59.3 1.9 %collective-permute-start.13 = (bf16[32,768]{1,0:T(8,128)(2,1)S(1)}, bf16[32,768]{1,0:T(8,128)(2,1)S(1)}, u32[]{:S(2)}, u32[]{:S(2)}) collective-permute-start(bf16[32,768]{1,0:T(8,128)(2,1)S(1)} %bitcast.27), channel_id=1, source_target_pairs={{8,0},{16,8},{24,16},{32,24},{40,32},{48,40},{56,48},{64,56},{72,6... | collective-permute-start | bytes 147464 | tf_op jit(solution)/shard_map/ppermute | solution.py:25
  61.2 2.4 %collective-permute-start.12 = (bf16[32,768]{1,0:T(8,128)(2,1)S(1)}, bf16[32,768]{1,0:T(8,128)(2,1)S(1)}, u32[]{:S(2)}, u32[]{:S(2)}) collective-permute-start(bf16[32,768]{1,0:T(8,128)(2,1)S(1)} %bitcast.28), channel_id=1, source_target_pairs={{0,8},{8,16},{16,24},{24,32},{32,40},{40,48},{48,56},{56,64},{64,7... | collective-permute-start | bytes 147464 | tf_op jit(solution)/shard_map/ppermute | solution.py:25
  63.6 1.9 %collective-permute-done.14 = bf16[16,768]{1,0:T(8,128)(2,1)S(1)} collective-permute-done((bf16[16,768]{1,0:T(8,128)(2,1)S(1)}, bf16[16,768]{1,0:T(8,128)(2,1)S(1)}, u32[]{:S(2)}, u32[]{:S(2)}) %collective-permute-start.14) | collective-permute-done | bytes 24608 | tf_op jit(solution)/shard_map/ppermute | solution.py:25
  65.5 5.0 %collective-permute-start.11 = (bf16[16,768]{1,0:T(8,128)(2,1)S(1)}, bf16[16,768]{1,0:T(8,128)(2,1)S(1)}, u32[]{:S(2)}, u32[]{:S(2)}) collective-permute-start(bf16[16,768]{1,0:T(8,128)(2,1)S(1)} %get-tuple-element.47), channel_id=1, source_target_pairs={{0,16},{8,24},{16,32},{24,40},{32,48},{40,56},{48,64},{56,72},{64,... | collective-permute-start | bytes 73736 | tf_op jit(solution)/shard_map/ppermute | solution.py:25
  70.6 1.5 collective-permute-done.11
  73.1 3.4 %collective-permute-done.1.refs_2_ = bf16[32,96,128]{2,1,0:T(8,128)(2,1)} collective-permute-done((bf16[32,96,128]{2,1,0:T(8,128)(2,1)}, bf16[32,96,128]{2,1,0:T(8,128)(2,1)}, u32[]{:S(2)}, u32[]{:S(2)}) %collective-permute-start.1) | collective-permute-done | bytes 786464 | tf_op jit(solution)/shard_map/ppermute | solution.py:30
  76.6 4.0 %collective-permute-start.5 = (bf16[32,96,128]{2,1,0:T(8,128)(2,1)}, bf16[32,96,128]{2,1,0:T(8,128)(2,1)}, u32[]{:S(2)}, u32[]{:S(2)}) collective-permute-start(bf16[32,96,128]{2,1,0:T(8,128)(2,1)} %collective-permute-done.4.refs_4_), channel_id=1, source_target_pairs={{0,7},{1,0},{2,1},{3,2},{4,3},{5,4},{6,5},{7,6},{8,15},{9,8},{10,9... | collective-permute-start | bytes 2359304 | tf_op jit(solution)/shard_map/ppermute | solution.py:30
  80.6 16.1 %self_attention.2.refs_3_ = bf16[4096,128]{1,0:T(8,128)(2,1)S(1)} custom-call(bf16[32,3,128,128]{3,2,1,0:T(8,128)(2,1)S(1)} %bitcast.18, bf16[32,3,128,128]{3,2,1,0:T(8,128)(2,1)S(1)} %bitcast.19, bf16[32,3,128,128]{3,2,1,0:T(8,128)(2,1)S(1)} %bitcast.20), custom_call_target="tpu_custom_call" | custom-call | flops 8589934592 | bytes 4194304 | tf_op jit(solution)/shard_map/self_attention/pallas_call | solution.py:144
  96.7 1.3 collective-permute-done.5.refs_6_
  98.0 3.4 %collective-permute-done.2.refs_5_ = bf16[32,96,128]{2,1,0:T(8,128)(2,1)} collective-permute-done((bf16[32,96,128]{2,1,0:T(8,128)(2,1)}, bf16[32,96,128]{2,1,0:T(8,128)(2,1)}, u32[]{:S(2)}, u32[]{:S(2)}) %collective-permute-start.2) | collective-permute-done | bytes 786464 | tf_op jit(solution)/shard_map/ppermute | solution.py:30
  104.4 1.7 %collective-permute-start.15 = (bf16[16,96,128]{2,1,0:T(8,128)(2,1)S(1)}, bf16[16,96,128]{2,1,0:T(8,128)(2,1)S(1)}, u32[]{:S(2)}, u32[]{:S(2)}) collective-permute-start(bf16[16,96,128]{2,1,0:T(8,128)(2,1)S(1)} %slice.37), channel_id=1, source_target_pairs={{0,1},{1,2},{2,3},{3,4},{4,5},{5,6},{6,7},{7,0},{8,9},{9,10},{10,1... | collective-permute-start | bytes 1179656 | tf_op jit(solution)/shard_map/ppermute | solution.py:30
  106.2 16.1 %self_attention.3 = bf16[4096,128]{1,0:T(8,128)(2,1)S(1)} custom-call(bf16[32,3,128,128]{3,2,1,0:T(8,128)(2,1)S(1)} %bitcast.21, bf16[32,3,128,128]{3,2,1,0:T(8,128)(2,1)S(1)} %bitcast.22, bf16[32,3,128,128]{3,2,1,0:T(8,128)(2,1)S(1)} %bitcast.23, bf16[4096,128]{1,0:T(8,128)(2,1)S(1)} %self_attention.2.refs_3_), custom_call_target="tpu_custom_call", output_to_operand_aliasing={{}: (3, {})} | custom-call | flops 8589934592 | bytes 4194304 | tf_op jit(solution)/shard_map/self_attention/pallas_call | solution.py:144
  124.7 8.3 %all-to-all-start.2 = ((bf16[32,128,128]{2,1,0:T(8,128)(2,1)}), bf16[32,128,128]{2,1,0:T(8,128)(2,1)S(1)}, u32[]{:S(2)}, u32[]{:S(2)}) async-start(bf16[32,128,128]{2,1,0:T(8,128)(2,1)} %bitcast.24), calls=%async_computation.2 | async-start | bytes 2097152 | tf_op jit(solution)/shard_map/all_to_all | solution.py:371
  133.0 14.5 %cross_attention.1 = (f32[128,4096]{1,0:T(8,128)}, f32[128,768]{1,0:T(8,128)S(1)}) custom-call(s32[10]{0:T(128)S(1)} %pad_add_fusion.place_ref, bf16[128,768]{1,0:T(8,128)(2,1)S(1)} %constant_dynamic-update-slice_fusion.near_ref, f32[128,128]{1,0:T(8,128)S(1)} %bitcast.25, bf16[128,4096]{1,0:T(8,128)(2,1)} %bitcast.30, bf16[128,4096]{1,0:T(8,128)(2,1)} %bitcast.31, ...), custom_call_target="tpu_custom_call" | custom-call | flops 6442450944 | bytes 16777216 | tf_op jit(solution)/shard_map/cross_attention/pallas_call | solution.py:245
  147.6 2.5 %collective-permute-start.20 = (bf16[32,768]{1,0:T(8,128)(2,1)S(1)}, bf16[32,768]{1,0:T(8,128)(2,1)S(1)}, u32[]{:S(2)}, u32[]{:S(2)}) collective-permute-start(bf16[32,768]{1,0:T(8,128)(2,1)S(1)} %get-tuple-element.44), channel_id=1, source_target_pairs={{8,0},{16,8},{24,16},{32,24},{40,32},{48,40},{56,48},{64,56},{72,6... | collective-permute-start | bytes 147464 | tf_op jit(solution)/shard_map/ppermute | solution.py:25
  150.1 1.9 %collective-permute-start.21 = (bf16[32,768]{1,0:T(8,128)(2,1)S(1)}, bf16[32,768]{1,0:T(8,128)(2,1)S(1)}, u32[]{:S(2)}, u32[]{:S(2)}) collective-permute-start(bf16[32,768]{1,0:T(8,128)(2,1)S(1)} %get-tuple-element.45), channel_id=1, source_target_pairs={{0,8},{8,16},{16,24},{24,32},{32,40},{40,48},{48,56},{56,64},{64,7... | collective-permute-start | bytes 147464 | tf_op jit(solution)/shard_map/ppermute | solution.py:25
  152.0 5.2 %collective-permute-start.22 = (bf16[16,768]{1,0:T(8,128)(2,1)S(1)}, bf16[16,768]{1,0:T(8,128)(2,1)S(1)}, u32[]{:S(2)}, u32[]{:S(2)}) collective-permute-start(bf16[16,768]{1,0:T(8,128)(2,1)S(1)} %get-tuple-element.42), channel_id=1, source_target_pairs={{0,16},{8,24},{16,32},{24,40},{32,48},{40,56},{48,64},{56,72},{64,... | collective-permute-start | bytes 73736 | tf_op jit(solution)/shard_map/ppermute | solution.py:25
  157.2 1.9 %collective-permute-start.23 = (bf16[16,768]{1,0:T(8,128)(2,1)S(1)}, bf16[16,768]{1,0:T(8,128)(2,1)S(1)}, u32[]{:S(2)}, u32[]{:S(2)}) collective-permute-start(bf16[16,768]{1,0:T(8,128)(2,1)S(1)} %get-tuple-element.43), channel_id=1, source_target_pairs={{16,0},{24,8},{32,16},{40,24},{48,32},{56,40},{64,48},{72,56},{80,... | collective-permute-start | bytes 73736 | tf_op jit(solution)/shard_map/ppermute | solution.py:25
  159.2 5.9 %collective-permute-done.23 = bf16[16,768]{1,0:T(8,128)(2,1)S(1)} collective-permute-done((bf16[16,768]{1,0:T(8,128)(2,1)S(1)}, bf16[16,768]{1,0:T(8,128)(2,1)S(1)}, u32[]{:S(2)}, u32[]{:S(2)}) %collective-permute-start.23) | collective-permute-done | bytes 24608 | tf_op jit(solution)/shard_map/ppermute | solution.py:25
  165.7 1.6 copy-done
  167.3 1.8 %merge.1 = bf16[128,4096]{1,0:T(8,128)(2,1)} custom-call(bf16[32,128,128]{2,1,0:T(8,128)(2,1)S(1)} %all-to-all-done.2.own_ref, f32[128,4096]{1,0:T(8,128)S(1)} %copy-done), custom_call_target="tpu_custom_call" | custom-call | flops 524288 | bytes 4194304 | tf_op jit(solution)/shard_map/merge/pallas_call | solution.py:285
  (80 shorter events, 9.3 us)
Async XLA Ops:
  2.4 19.6 %all-to-all-start = ((bf16[32,96,128]{2,1,0:T(8,128)(2,1)}), bf16[32,96,128]{2,1,0:T(8,128)(2,1)S(1)}, u32[]{:S(2)}, u32[]{:S(2)}) async-start(bf16[32,96,128]{2,1,0:T(8,128)(2,1)} %broadcast_select_fusion), calls=%async_computation | async-start | bytes 1572864 | tf_op jit(solution)/shard_map/all_to_all | solution.py:330
  16.3 40.3 %copy-start.8 = (bf16[1,32,768]{2,1,0:T(8,128)(2,1)S(1)}, bf16[1,32,768]{2,1,0:T(8,128)(2,1)}, u32[]{:S(2)}) copy-start(bf16[1,32,768]{2,1,0:T(8,128)(2,1)} %param.15) | copy-start | bytes 147460
  22.9 57.7 %all-to-all-start.1 = ((bf16[32,384,128]{2,1,0:T(8,128)(2,1)}), bf16[32,384,128]{2,1,0:T(8,128)(2,1)S(1)}, u32[]{:S(2)}, u32[]{:S(2)}) async-start(bf16[32,384,128]{2,1,0:T(8,128)(2,1)} %heads_first.1), calls=%async_computation.1 | async-start | bytes 6291456 | tf_op jit(solution)/shard_map/all_to_all | solution.py:340
  29.5 23.4 %collective-permute-start.3 = (bf16[32,96,128]{2,1,0:T(8,128)(2,1)}, bf16[32,96,128]{2,1,0:T(8,128)(2,1)}, u32[]{:S(2)}, u32[]{:S(2)}) collective-permute-start(bf16[32,96,128]{2,1,0:T(8,128)(2,1)} %copy-done.5), channel_id=1, source_target_pairs={{0,7},{1,0},{2,1},{3,2},{4,3},{5,4},{6,5},{7,6},{8,15},{9,8},{10,9... | collective-permute-start | bytes 2359304 | tf_op jit(solution)/shard_map/ppermute | solution.py:30
  35.4 21.1 %collective-permute-start = (bf16[32,96,128]{2,1,0:T(8,128)(2,1)}, bf16[32,96,128]{2,1,0:T(8,128)(2,1)}, u32[]{:S(2)}, u32[]{:S(2)}) collective-permute-start(bf16[32,96,128]{2,1,0:T(8,128)(2,1)} %copy-done.5), channel_id=1, source_target_pairs={{0,1},{1,2},{2,3},{3,4},{4,5},{5,6},{6,7},{7,0},{8,9},{9,10},{10,1... | collective-permute-start | bytes 2359304 | tf_op jit(solution)/shard_map/ppermute | solution.py:30
  52.8 20.3 %collective-permute-start.4 = (bf16[32,96,128]{2,1,0:T(8,128)(2,1)}, bf16[32,96,128]{2,1,0:T(8,128)(2,1)}, u32[]{:S(2)}, u32[]{:S(2)}) collective-permute-start(bf16[32,96,128]{2,1,0:T(8,128)(2,1)} %collective-permute-done.3.refs_3_), channel_id=1, source_target_pairs={{0,7},{1,0},{2,1},{3,2},{4,3},{5,4},{6,5},{7,6},{8,15},{9,8},{10,9... | collective-permute-start | bytes 2359304 | tf_op jit(solution)/shard_map/ppermute | solution.py:30
  56.5 20.0 %collective-permute-start.1 = (bf16[32,96,128]{2,1,0:T(8,128)(2,1)}, bf16[32,96,128]{2,1,0:T(8,128)(2,1)}, u32[]{:S(2)}, u32[]{:S(2)}) collective-permute-start(bf16[32,96,128]{2,1,0:T(8,128)(2,1)} %collective-permute-done.refs_1_), channel_id=1, source_target_pairs={{0,1},{1,2},{2,3},{3,4},{4,5},{5,6},{6,7},{7,0},{8,9},{9,10},{10,1... | collective-permute-start | bytes 2359304 | tf_op jit(solution)/shard_map/ppermute | solution.py:30
  56.5 9.0 %collective-permute-start.14 = (bf16[16,768]{1,0:T(8,128)(2,1)S(1)}, bf16[16,768]{1,0:T(8,128)(2,1)S(1)}, u32[]{:S(2)}, u32[]{:S(2)}) collective-permute-start(bf16[16,768]{1,0:T(8,128)(2,1)S(1)} %get-tuple-element.46), channel_id=1, source_target_pairs={{16,0},{24,8},{32,16},{40,24},{48,32},{56,40},{64,48},{72,56},{80,... | collective-permute-start | bytes 73736 | tf_op jit(solution)/shard_map/ppermute | solution.py:25
  59.3 12.8 %collective-permute-start.13 = (bf16[32,768]{1,0:T(8,128)(2,1)S(1)}, bf16[32,768]{1,0:T(8,128)(2,1)S(1)}, u32[]{:S(2)}, u32[]{:S(2)}) collective-permute-start(bf16[32,768]{1,0:T(8,128)(2,1)S(1)} %bitcast.27), channel_id=1, source_target_pairs={{8,0},{16,8},{24,16},{32,24},{40,32},{48,40},{56,48},{64,56},{72,6... | collective-permute-start | bytes 147464 | tf_op jit(solution)/shard_map/ppermute | solution.py:25
  61.2 11.4 %collective-permute-start.12 = (bf16[32,768]{1,0:T(8,128)(2,1)S(1)}, bf16[32,768]{1,0:T(8,128)(2,1)S(1)}, u32[]{:S(2)}, u32[]{:S(2)}) collective-permute-start(bf16[32,768]{1,0:T(8,128)(2,1)S(1)} %bitcast.28), channel_id=1, source_target_pairs={{0,8},{8,16},{16,24},{24,32},{32,40},{40,48},{48,56},{56,64},{64,7... | collective-permute-start | bytes 147464 | tf_op jit(solution)/shard_map/ppermute | solution.py:25
  65.5 6.5 %collective-permute-start.11 = (bf16[16,768]{1,0:T(8,128)(2,1)S(1)}, bf16[16,768]{1,0:T(8,128)(2,1)S(1)}, u32[]{:S(2)}, u32[]{:S(2)}) collective-permute-start(bf16[16,768]{1,0:T(8,128)(2,1)S(1)} %get-tuple-element.47), channel_id=1, source_target_pairs={{0,16},{8,24},{16,32},{24,40},{32,48},{40,56},{48,64},{56,72},{64,... | collective-permute-start | bytes 73736 | tf_op jit(solution)/shard_map/ppermute | solution.py:25
  72.1 4.5 %collective-permute-start.6 = (bf16[32,96,128]{2,1,0:T(8,128)(2,1)}, bf16[32,96,128]{2,1,0:T(8,128)(2,1)}, u32[]{:S(2)}, u32[]{:S(2)}) collective-permute-start(bf16[32,96,128]{2,1,0:T(8,128)(2,1)} %copy-done.5), channel_id=1, source_target_pairs={{0,8},{8,0},{16,24},{24,16},{32,40},{40,32},{48,56},{56,48},{64,72... | collective-permute-start | bytes 2359304 | tf_op jit(solution)/shard_map/ppermute | solution.py:35
  72.1 8.5 %collective-permute-start.9 = (bf16[32,96,128]{2,1,0:T(8,128)(2,1)}, bf16[32,96,128]{2,1,0:T(8,128)(2,1)}, u32[]{:S(2)}, u32[]{:S(2)}) collective-permute-start(bf16[32,96,128]{2,1,0:T(8,128)(2,1)} %collective-permute-done.3.refs_3_), channel_id=1, source_target_pairs={{0,8},{8,0},{16,24},{24,16},{32,40},{40,32},{48,56},{56,48},{64,72... | collective-permute-start | bytes 2359304 | tf_op jit(solution)/shard_map/ppermute | solution.py:35
  72.6 8.0 %collective-permute-start.7 = (bf16[32,96,128]{2,1,0:T(8,128)(2,1)}, bf16[32,96,128]{2,1,0:T(8,128)(2,1)}, u32[]{:S(2)}, u32[]{:S(2)}) collective-permute-start(bf16[32,96,128]{2,1,0:T(8,128)(2,1)} %collective-permute-done.refs_1_), channel_id=1, source_target_pairs={{0,8},{8,0},{16,24},{24,16},{32,40},{40,32},{48,56},{56,48},{64,72... | collective-permute-start | bytes 2359304 | tf_op jit(solution)/shard_map/ppermute | solution.py:35
  73.1 7.5 %collective-permute-start.10 = (bf16[32,96,128]{2,1,0:T(8,128)(2,1)}, bf16[32,96,128]{2,1,0:T(8,128)(2,1)}, u32[]{:S(2)}, u32[]{:S(2)}) collective-permute-start(bf16[32,96,128]{2,1,0:T(8,128)(2,1)} %collective-permute-done.4.refs_4_), channel_id=1, source_target_pairs={{0,8},{8,0},{16,24},{24,16},{32,40},{40,32},{48,56},{56,48},{64,72... | collective-permute-start | bytes 2359304 | tf_op jit(solution)/shard_map/ppermute | solution.py:35
  76.5 4.1 %collective-permute-start.8 = (bf16[32,96,128]{2,1,0:T(8,128)(2,1)}, bf16[32,96,128]{2,1,0:T(8,128)(2,1)}, u32[]{:S(2)}, u32[]{:S(2)}) collective-permute-start(bf16[32,96,128]{2,1,0:T(8,128)(2,1)} %collective-permute-done.1.refs_2_), channel_id=1, source_target_pairs={{0,8},{8,0},{16,24},{24,16},{32,40},{40,32},{48,56},{56,48},{64,72... | collective-permute-start | bytes 2359304 | tf_op jit(solution)/shard_map/ppermute | solution.py:35
  76.6 21.4 %collective-permute-start.5 = (bf16[32,96,128]{2,1,0:T(8,128)(2,1)}, bf16[32,96,128]{2,1,0:T(8,128)(2,1)}, u32[]{:S(2)}, u32[]{:S(2)}) collective-permute-start(bf16[32,96,128]{2,1,0:T(8,128)(2,1)} %collective-permute-done.4.refs_4_), channel_id=1, source_target_pairs={{0,7},{1,0},{2,1},{3,2},{4,3},{5,4},{6,5},{7,6},{8,15},{9,8},{10,9... | collective-permute-start | bytes 2359304 | tf_op jit(solution)/shard_map/ppermute | solution.py:30
  80.6 20.8 %collective-permute-start.2 = (bf16[32,96,128]{2,1,0:T(8,128)(2,1)}, bf16[32,96,128]{2,1,0:T(8,128)(2,1)}, u32[]{:S(2)}, u32[]{:S(2)}) collective-permute-start(bf16[32,96,128]{2,1,0:T(8,128)(2,1)} %collective-permute-done.1.refs_2_), channel_id=1, source_target_pairs={{0,1},{1,2},{2,3},{3,4},{4,5},{5,6},{6,7},{7,0},{8,9},{9,10},{10,1... | collective-permute-start | bytes 2359304 | tf_op jit(solution)/shard_map/ppermute | solution.py:30
  102.4 20.8 %collective-permute-start.17 = (bf16[32,96,128]{2,1,0:T(8,128)(2,1)}, bf16[32,96,128]{2,1,0:T(8,128)(2,1)S(1)}, u32[]{:S(2)}, u32[]{:S(2)}) collective-permute-start(bf16[32,96,128]{2,1,0:T(8,128)(2,1)} %collective-permute-done.2.refs_5_), channel_id=1, source_target_pairs={{0,8},{8,0},{16,24},{24,16},{32,40},{40,32},{48,56},{56,48},{64,72... | collective-permute-start | bytes 2359304 | tf_op jit(solution)/shard_map/ppermute | solution.py:35
  103.5 20.0 %copy-start.12 = (s32[1,2]{1,0:T(1,128)S(1)}, s32[1,2]{1,0:T(1,128)}, u32[]{:S(2)}) copy-start(s32[1,2]{1,0:T(1,128)} %param.19) | copy-start | bytes 28
  103.6 20.0 %copy-start.9 = (s32[1,2,4]{2,1,0:T(2,128)S(1)}, s32[1,2,4]{2,1,0:T(2,128)}, u32[]{:S(2)}) copy-start(s32[1,2,4]{2,1,0:T(2,128)} %param.18) | copy-start | bytes 100
  103.6 21.0 %copy-start.13 = (s32[8]{0:T(128)S(1)}, s32[8]{0:T(128)}, u32[]{:S(2)}) copy-start(s32[8]{0:T(128)} %constant.44.clone) | copy-start | bytes 100
  103.6 19.7 %collective-permute-start.18 = (bf16[32,96,128]{2,1,0:T(8,128)(2,1)}, bf16[32,96,128]{2,1,0:T(8,128)(2,1)S(1)}, u32[]{:S(2)}, u32[]{:S(2)}) collective-permute-start(bf16[32,96,128]{2,1,0:T(8,128)(2,1)} %collective-permute-done.5.refs_6_), channel_id=1, source_target_pairs={{0,8},{8,0},{16,24},{24,16},{32,40},{40,32},{48,56},{56,48},{64,72... | collective-permute-start | bytes 2359304 | tf_op jit(solution)/shard_map/ppermute | solution.py:35
  104.2 19.1 %collective-permute-start.16 = (bf16[16,96,128]{2,1,0:T(8,128)(2,1)S(1)}, bf16[16,96,128]{2,1,0:T(8,128)(2,1)S(1)}, u32[]{:S(2)}, u32[]{:S(2)}) collective-permute-start(bf16[16,96,128]{2,1,0:T(8,128)(2,1)S(1)} %slice.38), channel_id=1, source_target_pairs={{0,7},{1,0},{2,1},{3,2},{4,3},{5,4},{6,5},{7,6},{8,15},{9,8},{10,9... | collective-permute-start | bytes 1179656 | tf_op jit(solution)/shard_map/ppermute | solution.py:30
  104.4 18.8 %collective-permute-start.15 = (bf16[16,96,128]{2,1,0:T(8,128)(2,1)S(1)}, bf16[16,96,128]{2,1,0:T(8,128)(2,1)S(1)}, u32[]{:S(2)}, u32[]{:S(2)}) collective-permute-start(bf16[16,96,128]{2,1,0:T(8,128)(2,1)S(1)} %slice.37), channel_id=1, source_target_pairs={{0,1},{1,2},{2,3},{3,4},{4,5},{5,6},{6,7},{7,0},{8,9},{9,10},{10,1... | collective-permute-start | bytes 1179656 | tf_op jit(solution)/shard_map/ppermute | solution.py:30
  123.3 9.7 %copy-start.6 = (bf16[32,96,128]{2,1,0:T(8,128)(2,1)S(1)}, bf16[32,96,128]{2,1,0:T(8,128)(2,1)}, u32[]{:S(2)}) copy-start(bf16[32,96,128]{2,1,0:T(8,128)(2,1)} %copy-done.5) | copy-start | bytes 2359300
  123.4 9.5 %collective-permute-start.19 = (bf16[32,96,128]{2,1,0:T(8,128)(2,1)S(1)}, bf16[32,96,128]{2,1,0:T(8,128)(2,1)}, u32[]{:S(2)}, u32[]{:S(2)}) collective-permute-start(bf16[32,96,128]{2,1,0:T(8,128)(2,1)S(1)} %constant_dynamic-update-slice_fusion.5.refs_7_), channel_id=1, source_target_pairs={{0,8},{8,0},{16,24},{24,16},{32,40},{40,32},{48,56},{56,48},{64,72... | collective-permute-start | bytes 2359304 | tf_op jit(solution)/shard_map/ppermute | solution.py:35
  124.7 41.1 %all-to-all-start.2 = ((bf16[32,128,128]{2,1,0:T(8,128)(2,1)}), bf16[32,128,128]{2,1,0:T(8,128)(2,1)S(1)}, u32[]{:S(2)}, u32[]{:S(2)}) async-start(bf16[32,128,128]{2,1,0:T(8,128)(2,1)} %bitcast.24), calls=%async_computation.2 | async-start | bytes 2097152 | tf_op jit(solution)/shard_map/all_to_all | solution.py:371
  147.6 17.5 %collective-permute-start.20 = (bf16[32,768]{1,0:T(8,128)(2,1)S(1)}, bf16[32,768]{1,0:T(8,128)(2,1)S(1)}, u32[]{:S(2)}, u32[]{:S(2)}) collective-permute-start(bf16[32,768]{1,0:T(8,128)(2,1)S(1)} %get-tuple-element.44), channel_id=1, source_target_pairs={{8,0},{16,8},{24,16},{32,24},{40,32},{48,40},{56,48},{64,56},{72,6... | collective-permute-start | bytes 147464 | tf_op jit(solution)/shard_map/ppermute | solution.py:25
  150.1 15.0 %collective-permute-start.21 = (bf16[32,768]{1,0:T(8,128)(2,1)S(1)}, bf16[32,768]{1,0:T(8,128)(2,1)S(1)}, u32[]{:S(2)}, u32[]{:S(2)}) collective-permute-start(bf16[32,768]{1,0:T(8,128)(2,1)S(1)} %get-tuple-element.45), channel_id=1, source_target_pairs={{0,8},{8,16},{16,24},{24,32},{32,40},{40,48},{48,56},{56,64},{64,7... | collective-permute-start | bytes 147464 | tf_op jit(solution)/shard_map/ppermute | solution.py:25
  152.0 7.1 %collective-permute-start.22 = (bf16[16,768]{1,0:T(8,128)(2,1)S(1)}, bf16[16,768]{1,0:T(8,128)(2,1)S(1)}, u32[]{:S(2)}, u32[]{:S(2)}) collective-permute-start(bf16[16,768]{1,0:T(8,128)(2,1)S(1)} %get-tuple-element.42), channel_id=1, source_target_pairs={{0,16},{8,24},{16,32},{24,40},{32,48},{40,56},{48,64},{56,72},{64,... | collective-permute-start | bytes 73736 | tf_op jit(solution)/shard_map/ppermute | solution.py:25
  157.2 7.8 %collective-permute-start.23 = (bf16[16,768]{1,0:T(8,128)(2,1)S(1)}, bf16[16,768]{1,0:T(8,128)(2,1)S(1)}, u32[]{:S(2)}, u32[]{:S(2)}) collective-permute-start(bf16[16,768]{1,0:T(8,128)(2,1)S(1)} %get-tuple-element.43), channel_id=1, source_target_pairs={{16,0},{24,8},{32,16},{40,24},{48,32},{56,40},{64,48},{72,56},{80,... | collective-permute-start | bytes 73736 | tf_op jit(solution)/shard_map/ppermute | solution.py:25
  (9 other events, 18.7 us)

commit v2 on v1

--- a/solution.py
+++ b/solution.py
@@ -15,7 +15,7 @@
 EXP2_SCALING = SCALING * 1.4426950408889634
 F32 = jnp.float32
 BF16 = jnp.bfloat16
-VMEM_BYTES = 48 * 1024 * 1024
+VMEM_BYTES = 60 * 1024 * 1024
 CROSS_GROUP = 8
 
 
@@ -25,14 +25,22 @@
     return lax.ppermute(block, axis, route)
 
 
-def round_ring(block, axis, distance):
-    size = lax.axis_size(axis)
-    return lax.ppermute(block, axis, [(i, (i + distance) % size) for i in range(size)])
-
-
-def from_other_core(block):
-    size = lax.axis_size("seq")
-    return lax.ppermute(block, "seq", [(i, i ^ 1) for i in range(size)])
+def round_ring(block, distance, core=None):
+    layers = lax.axis_size("fsdp")
+    members = range(lax.axis_size("seq"))
+    route = [
+        (i * layers + z, i * layers + (z + distance) % layers)
+        for i in members
+        for z in range(layers)
+        if core is None or i % 2 == core
+    ]
+    return lax.ppermute(block, ("seq", "fsdp"), route)
+
+
+def from_other_core(block, core=None):
+    members = range(lax.axis_size("seq"))
+    route = [(i, i ^ 1) for i in members if core is None or i % 2 == core]
+    return lax.ppermute(block, "seq", route)
 
 
 def heads_first_kernel(group, q_ref, k_ref, v_ref, out_ref):
@@ -170,7 +178,7 @@
 
 def cross_kernel(
     group,
-    pieces,
+    common,
     place_ref,
     near_ref,
     live_ref,
@@ -178,19 +186,30 @@
     grad_ref,
     *refs,
 ):
-    proj_refs = refs[: 2 * pieces]
-    out_ref, audio_grad_ref, proj = refs[2 * pieces :]
+    piece_refs = refs[: 2 * common]
+    opposite_refs = refs[2 * common : 2 * common + 4]
+    out_ref, audio_grad_ref, proj = refs[2 * common + 4 :]
 
     @pl.when(pl.program_id(0) == 0)
     def _():
         audio_grad_ref[...] = jnp.zeros_like(audio_grad_ref)
 
-    depth = proj_refs[0].shape[1]
+    depth = piece_refs[0].shape[1]
+
+    def put(piece, kind, ref):
+        lanes = pl.ds(pl.multiple_of(place_ref[common + 1 + kind], HD), HD)
+        rows = pl.ds(pl.multiple_of(place_ref[piece], 32), depth)
+        proj[:, rows, lanes] = ref[...]
+
     for kind in range(2):
-        lanes = pl.ds(pl.multiple_of(place_ref[pieces + kind], HD), HD)
-        for piece in range(pieces):
-            rows = pl.ds(pl.multiple_of(place_ref[piece], 32), depth)
-            proj[:, rows, lanes] = proj_refs[kind * pieces + piece][...]
+        for piece in range(common):
+            put(piece, kind, piece_refs[kind * common + piece])
+    for core in range(2):
+
+        @pl.when(place_ref[common + 3] == core)
+        def _(core=core):
+            put(common, 0, opposite_refs[core])
+            put(common, 1, opposite_refs[2 + 1 - core])
 
     near = near_ref[...]
     live = live_ref[...] > 0
@@ -234,16 +253,16 @@
     audio_grad_ref[...] += sent
 
 
-def cross_attention(place, near, live, queries, grads, own_pieces, other_pieces):
-    heads, depth, _ = own_pieces[0].shape
-    pieces = len(own_pieces)
-    features = depth * pieces
+def cross_attention(place, near, live, queries, grads, pieces, opposite):
+    heads, depth, _ = pieces[0].shape
+    common = len(pieces) // 2
+    features = depth * (common + 1)
     rows, width = queries.shape
     band = near.shape[0]
     group = CROSS_GROUP
     piece = pl.BlockSpec((group, depth, HD), lambda i: (i, 0, 0))
     return pl.pallas_call(
-        functools.partial(cross_kernel, group, pieces),
+        functools.partial(cross_kernel, group, common),
         grid=(heads // group,),
         in_specs=[
             pl.BlockSpec(memory_space=pltpu.SMEM),
@@ -252,7 +271,7 @@
             pl.BlockSpec((rows, group * HD), lambda i: (0, i)),
             pl.BlockSpec((rows, group * HD), lambda i: (0, i)),
         ]
-        + [piece] * (2 * pieces),
+        + [piece] * (2 * common + 4),
         out_specs=[
             pl.BlockSpec((rows, group * HD), lambda i: (0, i)),
             pl.BlockSpec((band, features), lambda i: (0, 0)),
@@ -269,7 +288,7 @@
             transcendentals=rows * band * heads,
         ),
         name="cross_attention",
-    )(place, near, live, queries, grads, *own_pieces, *other_pieces)
+    )(place, near, live, queries, grads, *pieces, *opposite)
 
 
 def merge_kernel(group, own_ref, cross_ref, out_ref):
@@ -321,25 +340,18 @@
     here = lax.axis_index("seq")
     layer = lax.axis_index("fsdp")
     layers = lax.axis_size("fsdp")
+    members = lax.axis_size("seq")
+    core = lax.rem(here, 2)
     rows = self_q.shape[1]
-    members = lax.axis_size("seq")
     depth = key_weight.shape[0]
+    owned = audio.shape[1]
+    half = owned // 2
 
     even = (jnp.arange(members) % 2 == 0)[:, None, None]
     handed = jnp.where(even, key_weight[None], value_weight[None])
     start = lax.all_to_all(handed, "seq", split_axis=0, concat_axis=0, tiled=True)
+
     qkv = heads_first(self_q, self_k, self_v)
-    start, qkv = lax.optimization_barrier((start, qkv))
-
-    up, down = [start], [start]
-    for _ in range((layers - 1) // 2):
-        up.append(round_ring(up[-1], "fsdp", 1))
-        down.append(round_ring(down[-1], "fsdp", -1))
-    arrived = up[:-1] + down[1:-1]
-    other_arrived = [from_other_core(piece) for piece in arrived]
-    qkv = lax.all_to_all(qkv, "seq", split_axis=0, concat_axis=0, tiled=True)
-    owned = audio.shape[1]
-    half = owned // 2
     mine = audio[0]
     near = jnp.concatenate(
         [
@@ -351,46 +363,53 @@
         ],
         axis=0,
     )
-    qkv, other_arrived, near = lax.optimization_barrier((qkv, other_arrived, near))
+    frames = intersection.shape[1]
+    band_blocks = near.shape[0] // AB
+    band_first = here * (owned // AB) - REACH
+    live = live_band(intersection[0], counts[0], band_first, band_blocks, rows // frames)
+    steps = (layers - 1) // 2
+    shifts = [-i for i in range(steps)] + [i for i in range(1, steps)]
+    shifts += [-steps, steps, layers // 2]
+    place = jnp.concatenate(
+        [
+            lax.rem(layer + jnp.array([shift % layers for shift in shifts]), layers) * depth,
+            jnp.stack([core * HD, (1 - core) * HD, core]),
+        ]
+    ).astype(jnp.int32)
+    start, qkv, near, live, place = lax.optimization_barrier((start, qkv, near, live, place))
+
+    up, down = [start], [start]
+    for _ in range(steps):
+        up.append(round_ring(up[-1], 1))
+        down.append(round_ring(down[-1], -1))
+    arrived = up[:-1] + down[1:-1]
+    other_arrived = [from_other_core(piece) for piece in arrived]
+    qkv = lax.all_to_all(qkv, "seq", split_axis=0, concat_axis=0, tiled=True)
+    qkv, other_arrived = lax.optimization_barrier((qkv, other_arrived))
     qkv = qkv.reshape(qkv.shape[0], 3, rows, HD)
 
     own_heads = attend_self(qkv, 0, 2)
     last_up, last_down, own_heads, qkv = lax.optimization_barrier(
         (up[-1], down[-1], own_heads, qkv)
     )
-    middle = members // 2
-    opposite = [
-        round_ring(last_up[:middle], "fsdp", 1),
-        round_ring(last_down[middle:], "fsdp", -1),
-    ]
+    opposite = [round_ring(last_up, 1, 0), round_ring(last_down, -1, 1)]
     last = [last_up, last_down]
     other_last = [from_other_core(piece) for piece in last]
     own_heads = attend_self(qkv, 1, 2, own_heads)
     opposite, other_last, own_heads = lax.optimization_barrier((opposite, other_last, own_heads))
-    opposite = jnp.concatenate(opposite, axis=0)
     own_tokens = lax.all_to_all(
         own_heads.reshape(-1, rows, HD), "seq", split_axis=0, concat_axis=0, tiled=True
     )
-
-    own_pieces = arrived + last + [opposite]
-    other_pieces = other_arrived + other_last + [from_other_core(opposite)]
-    steps = len(up)
-    inner = steps - 1
-    shifts = [-i for i in range(inner)] + [i for i in range(1, inner)] + [-inner, inner, steps]
-    core = lax.rem(here, 2)
-    place = jnp.concatenate(
-        [
-            lax.rem(layer + jnp.array([shift % layers for shift in shifts]), layers) * depth,
-            jnp.stack([core * HD, (1 - core) * HD]),
-        ]
-    ).astype(jnp.int32)
-
-    frames = intersection.shape[1]
-    band_blocks = near.shape[0] // AB
-    band_first = here * (owned // AB) - REACH
-    live = live_band(intersection[0], counts[0], band_first, band_blocks, rows // frames)
+    other_opposite = [from_other_core(opposite[0], 0), from_other_core(opposite[1], 1)]
+
     cross_out, band = cross_attention(
-        place, near, live, cross_q[0], cotangent[0], own_pieces, other_pieces
+        place,
+        near,
+        live,
+        cross_q[0],
+        cotangent[0],
+        arrived + last + other_arrived + other_last,
+        opposite + other_opposite,
     )
     block_out = merged(own_tokens, cross_out)
 

time: 170 us -> 196 us (1.15)
  the two profiles are of different devices: /device:TPU:6 before, /device:TPU:1 now
where the time goes in v2:
time: 196 us; the launch traced here: 192 us
  starting transfers between devices  75.2 us (38%)
  Pallas kernels  60.1 us (31%)
  waiting for transfers between devices  42 us (21%)
  other arithmetic  7.07 us (4%)
  local copies, waits for them, and re-layouts  6.31 us (3%)
    pallas_call x2, Pallas kernels, attend_self(): pl.pallas_call(functools.partial(self_attention_kernel, block_rows, block...  36.8 us
    ppermute x8, waiting for transfers between devices, round_ring(): return lax.ppermute(block, ('seq', 'fsdp'), route)  31.6 us
    ppermute x8, starting transfers between devices, passed_along(): return lax.ppermute(block, axis, route)  22.5 us
    ppermute x8, starting transfers between devices, round_ring(): return lax.ppermute(block, ('seq', 'fsdp'), route)  15.6 us
    pallas_call x1, Pallas kernels, cross_attention(): pl.pallas_call(functools.partial(cross_kernel, group, common), grid=(head...  15.1 us
    ppermute x9, starting transfers between devices, from_other_core(): return lax.ppermute(block, 'seq', route)  15.1 us
    all_to_all x1, starting transfers between devices, local(): lax.all_to_all(handed, 'seq', split_axis=0, concat_axis=0, tiled=True)  10.5 us
    all_to_all x1, starting transfers between devices, local(): lax.all_to_all(own_heads.reshape(-1, rows, HD), 'seq', split_axis=0, conc...  7.24 us
  transfers between devices with their start and end apart: 28, of which 5 were waited for; matrix products, arithmetic and copies ran while one was open for 4% of the time, Pallas kernels for 29%

profile of v2, /device:TPU:1, one launch (start us, length us, event | category | flops | bytes accessed | tf_op | source)
XLA Modules:
  0.0 191.7 jit_solution(735907984095146648)
XLA Ops:
  0.6 5.2 %collective-permute-start.2 = (bf16[32,768]{1,0:T(8,128)(2,1)}, bf16[32,768]{1,0:T(8,128)(2,1)S(1)}, u32[]{:S(2)}, u32[]{:S(2)}) collective-permute-start(bf16[32,768]{1,0:T(8,128)(2,1)} %bitcast.27), channel_id=1, source_target_pairs={{8,0},{16,8},{24,16},{32,24},{40,32},{48,40},{56,48},{64,56},{72,6... | collective-permute-start | bytes 147464 | tf_op jit(solution)/shard_map/ppermute | solution.py:25
  5.8 1.9 %collective-permute-start.1 = (bf16[32,768]{1,0:T(8,128)(2,1)}, bf16[32,768]{1,0:T(8,128)(2,1)S(1)}, u32[]{:S(2)}, u32[]{:S(2)}) collective-permute-start(bf16[32,768]{1,0:T(8,128)(2,1)} %bitcast.28), channel_id=1, source_target_pairs={{0,8},{8,16},{16,24},{24,32},{32,40},{40,48},{48,56},{56,64},{64,7... | collective-permute-start | bytes 147464 | tf_op jit(solution)/shard_map/ppermute | solution.py:25
  9.8 4.0 %collective-permute-start = (bf16[16,768]{1,0:T(8,128)(2,1)S(1)}, bf16[16,768]{1,0:T(8,128)(2,1)S(1)}, u32[]{:S(2)}, u32[]{:S(2)}) collective-permute-start(bf16[16,768]{1,0:T(8,128)(2,1)S(1)} %get-tuple-element.51), channel_id=1, source_target_pairs={{0,16},{8,24},{16,32},{24,40},{32,48},{40,56},{48,64},{56,72},{64,... | collective-permute-start | bytes 73736 | tf_op jit(solution)/shard_map/ppermute | solution.py:25
  13.8 1.8 broadcast_select_fusion
  15.6 10.5 %all-to-all-start = ((bf16[32,96,128]{2,1,0:T(8,128)(2,1)}), bf16[32,96,128]{2,1,0:T(8,128)(2,1)S(1)}, u32[]{:S(2)}, u32[]{:S(2)}) async-start(bf16[32,96,128]{2,1,0:T(8,128)(2,1)} %broadcast_select_fusion), calls=%async_computation | async-start | bytes 1572864 | tf_op jit(solution)/shard_map/all_to_all | solution.py:352
  29.0 4.4 %heads_first.1 = bf16[32,384,128]{2,1,0:T(8,128)(2,1)} custom-call(bf16[1,128,4096]{2,1,0:T(8,128)(2,1)} %q_ref.1, bf16[1,128,4096]{2,1,0:T(8,128)(2,1)} %k_ref.1, bf16[1,128,4096]{2,1,0:T(8,128)(2,1)} %v_ref.1), custom_call_target="tpu_custom_call" | custom-call | bytes 6291456 | tf_op jit(solution)/shard_map/heads_first/pallas_call | solution.py:60
  33.5 6.8 %all-to-all-done.refs_0_ = bf16[32,96,128]{2,1,0:T(8,128)(2,1)S(1)} async-done(((bf16[32,96,128]{2,1,0:T(8,128)(2,1)}), bf16[32,96,128]{2,1,0:T(8,128)(2,1)S(1)}, u32[]{:S(2)}, u32[]{:S(2)}) %all-to-all-start) | async-done | bytes 786464 | tf_op jit(solution)/shard_map/all_to_all | solution.py:352
  41.2 4.3 %all-to-all-start.1 = ((bf16[32,384,128]{2,1,0:T(8,128)(2,1)}), bf16[32,384,128]{2,1,0:T(8,128)(2,1)S(1)}, u32[]{:S(2)}, u32[]{:S(2)}) async-start(bf16[32,384,128]{2,1,0:T(8,128)(2,1)} %heads_first.1), calls=%async_computation.1 | async-start | bytes 6291456 | tf_op jit(solution)/shard_map/all_to_all | solution.py:387
  45.5 5.7 %collective-permute-start.7 = (bf16[32,96,128]{2,1,0:T(8,128)(2,1)}, bf16[32,96,128]{2,1,0:T(8,128)(2,1)S(1)}, u32[]{:S(2)}, u32[]{:S(2)}) collective-permute-start(bf16[32,96,128]{2,1,0:T(8,128)(2,1)} %copy-done.2), channel_id=1, source_target_pairs={{0,7},{1,0},{2,1},{3,2},{4,3},{5,4},{6,5},{7,6},{8,15},{9,8},{10,9... | collective-permute-start | bytes 2359304 | tf_op jit(solution)/shard_map/ppermute | solution.py:37
  51.1 16.9 %collective-permute-done.7.refs_3_ = bf16[32,96,128]{2,1,0:T(8,128)(2,1)S(1)} collective-permute-done((bf16[32,96,128]{2,1,0:T(8,128)(2,1)}, bf16[32,96,128]{2,1,0:T(8,128)(2,1)S(1)}, u32[]{:S(2)}, u32[]{:S(2)}) %collective-permute-start.7) | collective-permute-done | bytes 786464 | tf_op jit(solution)/shard_map/ppermute | solution.py:37
  68.0 3.3 %collective-permute-start.8 = (bf16[32,96,128]{2,1,0:T(8,128)(2,1)S(1)}, bf16[32,96,128]{2,1,0:T(8,128)(2,1)}, u32[]{:S(2)}, u32[]{:S(2)}) collective-permute-start(bf16[32,96,128]{2,1,0:T(8,128)(2,1)S(1)} %collective-permute-done.7.refs_3_), channel_id=1, source_target_pairs={{0,7},{1,0},{2,1},{3,2},{4,3},{5,4},{6,5},{7,6},{8,15},{9,8},{10,9... | collective-permute-start | bytes 2359304 | tf_op jit(solution)/shard_map/ppermute | solution.py:37
  71.4 1.5 collective-permute-start.10
  73.4 13.6 %collective-permute-done.8.refs_4_ = bf16[32,96,128]{2,1,0:T(8,128)(2,1)} collective-permute-done((bf16[32,96,128]{2,1,0:T(8,128)(2,1)S(1)}, bf16[32,96,128]{2,1,0:T(8,128)(2,1)}, u32[]{:S(2)}, u32[]{:S(2)}) %collective-permute-start.8) | collective-permute-done | bytes 786464 | tf_op jit(solution)/shard_map/ppermute | solution.py:37
  87.0 2.1 %collective-permute-start.14 = (bf16[32,96,128]{2,1,0:T(8,128)(2,1)}, bf16[32,96,128]{2,1,0:T(8,128)(2,1)S(1)}, u32[]{:S(2)}, u32[]{:S(2)}) collective-permute-start(bf16[32,96,128]{2,1,0:T(8,128)(2,1)} %collective-permute-done.8.refs_4_), channel_id=1, source_target_pairs={{0,8},{8,0},{16,24},{24,16},{32,40},{40,32},{48,56},{56,48},{64,72... | collective-permute-start | bytes 2359304 | tf_op jit(solution)/shard_map/ppermute | solution.py:43
  90.2 2.4 %collective-permute-start.12 = (bf16[32,96,128]{2,1,0:T(8,128)(2,1)}, bf16[32,96,128]{2,1,0:T(8,128)(2,1)}, u32[]{:S(2)}, u32[]{:S(2)}) collective-permute-start(bf16[32,96,128]{2,1,0:T(8,128)(2,1)} %collective-permute-done.5.refs_2_), channel_id=1, source_target_pairs={{0,8},{8,0},{16,24},{24,16},{32,40},{40,32},{48,56},{56,48},{64,72... | collective-permute-start | bytes 2359304 | tf_op jit(solution)/shard_map/ppermute | solution.py:43
  92.7 1.4 collective-permute-start.6
  95.9 1.6 copy-done.1
  97.5 18.4 %self_attention.2.refs_3_ = bf16[4096,128]{1,0:T(8,128)(2,1)} custom-call(bf16[32,3,128,128]{3,2,1,0:T(8,128)(2,1)} %bitcast.19, bf16[32,3,128,128]{3,2,1,0:T(8,128)(2,1)} %bitcast.20, bf16[32,3,128,128]{3,2,1,0:T(8,128)(2,1)} %bitcast.21), custom_call_target="tpu_custom_call" | custom-call | flops 8589934592 | bytes 4194304 | tf_op jit(solution)/shard_map/self_attention/pallas_call | solution.py:152
  117.3 1.7 collective-permute-start.18
  119.1 4.4 %collective-permute-start.16 = (bf16[32,96,128]{2,1,0:T(8,128)(2,1)}, bf16[32,96,128]{2,1,0:T(8,128)(2,1)}, u32[]{:S(2)}, u32[]{:S(2)}) collective-permute-start(bf16[32,96,128]{2,1,0:T(8,128)(2,1)} %collective-permute-done.9.refs_6_), channel_id=1, source_target_pairs={{8,15},{9,8},{10,9},{11,10},{12,11},{13,12},{14,13},{15,14},{24,31... | collective-permute-start | bytes 2359304 | tf_op jit(solution)/shard_map/ppermute | solution.py:37
  123.5 18.4 %self_attention.3 = bf16[4096,128]{1,0:T(8,128)(2,1)} custom-call(bf16[32,3,128,128]{3,2,1,0:T(8,128)(2,1)} %bitcast.22, bf16[32,3,128,128]{3,2,1,0:T(8,128)(2,1)} %bitcast.23, bf16[32,3,128,128]{3,2,1,0:T(8,128)(2,1)} %bitcast.24, bf16[4096,128]{1,0:T(8,128)(2,1)} %self_attention.2.refs_3_), custom_call_target="tpu_custom_call", output_to_operand_aliasing={{}: (3, {})} | custom-call | flops 8589934592 | bytes 4194304 | tf_op jit(solution)/shard_map/self_attention/pallas_call | solution.py:152
  142.0 1.3 collective-permute-start.19
  143.3 4.8 %collective-permute-start.20 = (bf16[32,96,128]{2,1,0:T(8,128)(2,1)}, bf16[32,96,128]{2,1,0:T(8,128)(2,1)}, u32[]{:S(2)}, u32[]{:S(2)}) collective-permute-start(bf16[32,96,128]{2,1,0:T(8,128)(2,1)} %collective-permute-done.16.refs_15_), channel_id=1, source_target_pairs={{8,0},{24,16},{40,32},{56,48},{72,64},{88,80},{104,96},{120,112},{... | collective-permute-start | bytes 2359304 | tf_op jit(solution)/shard_map/ppermute | solution.py:43
  148.1 7.2 %all-to-all-start.2 = ((bf16[32,128,128]{2,1,0:T(8,128)(2,1)}), bf16[32,128,128]{2,1,0:T(8,128)(2,1)S(1)}, u32[]{:S(2)}, u32[]{:S(2)}) async-start(bf16[32,128,128]{2,1,0:T(8,128)(2,1)} %bitcast.25), calls=%async_computation.2 | async-start | bytes 2097152 | tf_op jit(solution)/shard_map/all_to_all | solution.py:400
  155.4 15.1 %cross_attention.1 = (f32[128,4096]{1,0:T(8,128)}, f32[128,768]{1,0:T(8,128)}) custom-call(s32[11]{0:T(128)} %pad_add_fusion.place_ref, bf16[128,768]{1,0:T(8,128)(2,1)} %copy-done.4, f32[128,128]{1,0:T(8,128)} %bitcast.29, bf16[128,4096]{1,0:T(8,128)(2,1)} %bitcast.31, bf16[128,4096]{1,0:T(8,128)(2,1)} %bitcast.32, bf16[32,96,128]{2,1,0:T(8,128)(2,1)} %copy-done.2, ...), custom_call_target="tpu_custom_call" | custom-call | flops 6442450944 | bytes 16777216 | tf_op jit(solution)/shard_map/cross_attention/pallas_call | solution.py:264
  171.6 2.2 %collective-permute-start.21 = (bf16[32,768]{1,0:T(8,128)(2,1)S(1)}, bf16[32,768]{1,0:T(8,128)(2,1)S(1)}, u32[]{:S(2)}, u32[]{:S(2)}) collective-permute-start(bf16[32,768]{1,0:T(8,128)(2,1)S(1)} %get-tuple-element.48), channel_id=1, source_target_pairs={{8,0},{16,8},{24,16},{32,24},{40,32},{48,40},{56,48},{64,56},{72,6... | collective-permute-start | bytes 147464 | tf_op jit(solution)/shard_map/ppermute | solution.py:25
  173.7 3.4 %collective-permute-start.22 = (bf16[32,768]{1,0:T(8,128)(2,1)S(1)}, bf16[32,768]{1,0:T(8,128)(2,1)S(1)}, u32[]{:S(2)}, u32[]{:S(2)}) collective-permute-start(bf16[32,768]{1,0:T(8,128)(2,1)S(1)} %get-tuple-element.49), channel_id=1, source_target_pairs={{0,8},{8,16},{16,24},{24,32},{32,40},{40,48},{48,56},{56,64},{64,7... | collective-permute-start | bytes 147464 | tf_op jit(solution)/shard_map/ppermute | solution.py:25
  177.1 3.3 %collective-permute-start.23 = (bf16[16,768]{1,0:T(8,128)(2,1)S(1)}, bf16[16,768]{1,0:T(8,128)(2,1)S(1)}, u32[]{:S(2)}, u32[]{:S(2)}) collective-permute-start(bf16[16,768]{1,0:T(8,128)(2,1)S(1)} %get-tuple-element.46), channel_id=1, source_target_pairs={{0,16},{8,24},{16,32},{24,40},{32,48},{40,56},{48,64},{56,72},{64,... | collective-permute-start | bytes 73736 | tf_op jit(solution)/shard_map/ppermute | solution.py:25
  180.4 1.3 collective-permute-start.24
  181.8 3.5 %collective-permute-done.24 = bf16[16,768]{1,0:T(8,128)(2,1)S(1)} collective-permute-done((bf16[16,768]{1,0:T(8,128)(2,1)S(1)}, bf16[16,768]{1,0:T(8,128)(2,1)S(1)}, u32[]{:S(2)}, u32[]{:S(2)}) %collective-permute-start.24) | collective-permute-done | bytes 24608 | tf_op jit(solution)/shard_map/ppermute | solution.py:25
  185.3 1.6 add_bitcast_fusion
  187.9 3.8 %merge.1 = bf16[128,4096]{1,0:T(8,128)(2,1)} custom-call(bf16[32,128,128]{2,1,0:T(8,128)(2,1)} %copy-done, f32[128,4096]{1,0:T(8,128)} %get-tuple-element.44.cross_ref), custom_call_target="tpu_custom_call" | custom-call | flops 524288 | bytes 4194304 | tf_op jit(solution)/shard_map/merge/pallas_call | solution.py:304
  (78 shorter events, 12.9 us)
Async XLA Ops:
  0.6 32.8 %collective-permute-start.2 = (bf16[32,768]{1,0:T(8,128)(2,1)}, bf16[32,768]{1,0:T(8,128)(2,1)S(1)}, u32[]{:S(2)}, u32[]{:S(2)}) collective-permute-start(bf16[32,768]{1,0:T(8,128)(2,1)} %bitcast.27), channel_id=1, source_target_pairs={{8,0},{16,8},{24,16},{32,24},{40,32},{48,40},{56,48},{64,56},{72,6... | collective-permute-start | bytes 147464 | tf_op jit(solution)/shard_map/ppermute | solution.py:25
  5.8 27.6 %collective-permute-start.1 = (bf16[32,768]{1,0:T(8,128)(2,1)}, bf16[32,768]{1,0:T(8,128)(2,1)S(1)}, u32[]{:S(2)}, u32[]{:S(2)}) collective-permute-start(bf16[32,768]{1,0:T(8,128)(2,1)} %bitcast.28), channel_id=1, source_target_pairs={{0,8},{8,16},{16,24},{24,32},{32,40},{40,48},{48,56},{56,64},{64,7... | collective-permute-start | bytes 147464 | tf_op jit(solution)/shard_map/ppermute | solution.py:25
  8.5 24.9 %collective-permute-start.3 = (bf16[16,768]{1,0:T(8,128)(2,1)S(1)}, bf16[16,768]{1,0:T(8,128)(2,1)S(1)}, u32[]{:S(2)}, u32[]{:S(2)}) collective-permute-start(bf16[16,768]{1,0:T(8,128)(2,1)S(1)} %get-tuple-element.50), channel_id=1, source_target_pairs={{16,0},{24,8},{32,16},{40,24},{48,32},{56,40},{64,48},{72,56},{80,... | collective-permute-start | bytes 73736 | tf_op jit(solution)/shard_map/ppermute | solution.py:25
  9.8 23.6 %collective-permute-start = (bf16[16,768]{1,0:T(8,128)(2,1)S(1)}, bf16[16,768]{1,0:T(8,128)(2,1)S(1)}, u32[]{:S(2)}, u32[]{:S(2)}) collective-permute-start(bf16[16,768]{1,0:T(8,128)(2,1)S(1)} %get-tuple-element.51), channel_id=1, source_target_pairs={{0,16},{8,24},{16,32},{24,40},{32,48},{40,56},{48,64},{56,72},{64,... | collective-permute-start | bytes 73736 | tf_op jit(solution)/shard_map/ppermute | solution.py:25
  15.6 24.7 %all-to-all-start = ((bf16[32,96,128]{2,1,0:T(8,128)(2,1)}), bf16[32,96,128]{2,1,0:T(8,128)(2,1)S(1)}, u32[]{:S(2)}, u32[]{:S(2)}) async-start(bf16[32,96,128]{2,1,0:T(8,128)(2,1)} %broadcast_select_fusion), calls=%async_computation | async-start | bytes 1572864 | tf_op jit(solution)/shard_map/all_to_all | solution.py:352
  33.5 82.4 %copy-start.4 = (bf16[128,768]{1,0:T(8,128)(2,1)}, bf16[128,768]{1,0:T(8,128)(2,1)S(1)}, u32[]{:S(2)}) copy-start(bf16[128,768]{1,0:T(8,128)(2,1)S(1)} %constant_dynamic-update-slice_fusion.near_ref) | copy-start | bytes 589828
  41.2 54.7 %all-to-all-start.1 = ((bf16[32,384,128]{2,1,0:T(8,128)(2,1)}), bf16[32,384,128]{2,1,0:T(8,128)(2,1)S(1)}, u32[]{:S(2)}, u32[]{:S(2)}) async-start(bf16[32,384,128]{2,1,0:T(8,128)(2,1)} %heads_first.1), calls=%async_computation.1 | async-start | bytes 6291456 | tf_op jit(solution)/shard_map/all_to_all | solution.py:387
  45.5 22.5 %collective-permute-start.7 = (bf16[32,96,128]{2,1,0:T(8,128)(2,1)}, bf16[32,96,128]{2,1,0:T(8,128)(2,1)S(1)}, u32[]{:S(2)}, u32[]{:S(2)}) collective-permute-start(bf16[32,96,128]{2,1,0:T(8,128)(2,1)} %copy-done.2), channel_id=1, source_target_pairs={{0,7},{1,0},{2,1},{3,2},{4,3},{5,4},{6,5},{7,6},{8,15},{9,8},{10,9... | collective-permute-start | bytes 2359304 | tf_op jit(solution)/shard_map/ppermute | solution.py:37
  51.1 20.2 %collective-permute-start.4 = (bf16[32,96,128]{2,1,0:T(8,128)(2,1)}, bf16[32,96,128]{2,1,0:T(8,128)(2,1)S(1)}, u32[]{:S(2)}, u32[]{:S(2)}) collective-permute-start(bf16[32,96,128]{2,1,0:T(8,128)(2,1)} %copy-done.2), channel_id=1, source_target_pairs={{0,1},{1,2},{2,3},{3,4},{4,5},{5,6},{6,7},{7,0},{8,9},{9,10},{10,1... | collective-permute-start | bytes 2359304 | tf_op jit(solution)/shard_map/ppermute | solution.py:37
  68.0 26.1 %copy-start.5 = (bf16[32,96,128]{2,1,0:T(8,128)(2,1)}, bf16[32,96,128]{2,1,0:T(8,128)(2,1)S(1)}, u32[]{:S(2)}) copy-start(bf16[32,96,128]{2,1,0:T(8,128)(2,1)S(1)} %collective-permute-done.7.refs_3_) | copy-start | bytes 2359300
  68.0 19.0 %collective-permute-start.8 = (bf16[32,96,128]{2,1,0:T(8,128)(2,1)S(1)}, bf16[32,96,128]{2,1,0:T(8,128)(2,1)}, u32[]{:S(2)}, u32[]{:S(2)}) collective-permute-start(bf16[32,96,128]{2,1,0:T(8,128)(2,1)S(1)} %collective-permute-done.7.refs_3_), channel_id=1, source_target_pairs={{0,7},{1,0},{2,1},{3,2},{4,3},{5,4},{6,5},{7,6},{8,15},{9,8},{10,9... | collective-permute-start | bytes 2359304 | tf_op jit(solution)/shard_map/ppermute | solution.py:37
  71.3 22.8 %copy-start.6 = (bf16[32,96,128]{2,1,0:T(8,128)(2,1)}, bf16[32,96,128]{2,1,0:T(8,128)(2,1)S(1)}, u32[]{:S(2)}) copy-start(bf16[32,96,128]{2,1,0:T(8,128)(2,1)S(1)} %collective-permute-done.4.refs_1_) | copy-start | bytes 2359300
  71.4 18.9 %collective-permute-start.5 = (bf16[32,96,128]{2,1,0:T(8,128)(2,1)S(1)}, bf16[32,96,128]{2,1,0:T(8,128)(2,1)}, u32[]{:S(2)}, u32[]{:S(2)}) collective-permute-start(bf16[32,96,128]{2,1,0:T(8,128)(2,1)S(1)} %collective-permute-done.4.refs_1_), channel_id=1, source_target_pairs={{0,1},{1,2},{2,3},{3,4},{4,5},{5,6},{6,7},{7,0},{8,9},{9,10},{10,1... | collective-permute-start | bytes 2359304 | tf_op jit(solution)/shard_map/ppermute | solution.py:37
  71.4 21.3 %collective-permute-start.10 = (bf16[32,96,128]{2,1,0:T(8,128)(2,1)}, bf16[32,96,128]{2,1,0:T(8,128)(2,1)S(1)}, u32[]{:S(2)}, u32[]{:S(2)}) collective-permute-start(bf16[32,96,128]{2,1,0:T(8,128)(2,1)} %copy-done.2), channel_id=1, source_target_pairs={{0,8},{8,0},{16,24},{24,16},{32,40},{40,32},{48,56},{56,48},{64,72... | collective-permute-start | bytes 2359304 | tf_op jit(solution)/shard_map/ppermute | solution.py:43
  72.9 19.8 %collective-permute-start.13 = (bf16[32,96,128]{2,1,0:T(8,128)(2,1)S(1)}, bf16[32,96,128]{2,1,0:T(8,128)(2,1)S(1)}, u32[]{:S(2)}, u32[]{:S(2)}) collective-permute-start(bf16[32,96,128]{2,1,0:T(8,128)(2,1)S(1)} %collective-permute-done.7.refs_3_), channel_id=1, source_target_pairs={{0,8},{8,0},{16,24},{24,16},{32,40},{40,32},{48,56},{56,48},{64,72... | collective-permute-start | bytes 2359304 | tf_op jit(solution)/shard_map/ppermute | solution.py:43
  73.0 21.1 %collective-permute-start.11 = (bf16[32,96,128]{2,1,0:T(8,128)(2,1)S(1)}, bf16[32,96,128]{2,1,0:T(8,128)(2,1)S(1)}, u32[]{:S(2)}, u32[]{:S(2)}) collective-permute-start(bf16[32,96,128]{2,1,0:T(8,128)(2,1)S(1)} %collective-permute-done.4.refs_1_), channel_id=1, source_target_pairs={{0,8},{8,0},{16,24},{24,16},{32,40},{40,32},{48,56},{56,48},{64,72... | collective-permute-start | bytes 2359304 | tf_op jit(solution)/shard_map/ppermute | solution.py:43
  87.0 7.1 %collective-permute-start.14 = (bf16[32,96,128]{2,1,0:T(8,128)(2,1)}, bf16[32,96,128]{2,1,0:T(8,128)(2,1)S(1)}, u32[]{:S(2)}, u32[]{:S(2)}) collective-permute-start(bf16[32,96,128]{2,1,0:T(8,128)(2,1)} %collective-permute-done.8.refs_4_), channel_id=1, source_target_pairs={{0,8},{8,0},{16,24},{24,16},{32,40},{40,32},{48,56},{56,48},{64,72... | collective-permute-start | bytes 2359304 | tf_op jit(solution)/shard_map/ppermute | solution.py:43
  90.2 5.6 %collective-permute-start.12 = (bf16[32,96,128]{2,1,0:T(8,128)(2,1)}, bf16[32,96,128]{2,1,0:T(8,128)(2,1)}, u32[]{:S(2)}, u32[]{:S(2)}) collective-permute-start(bf16[32,96,128]{2,1,0:T(8,128)(2,1)} %collective-permute-done.5.refs_2_), channel_id=1, source_target_pairs={{0,8},{8,0},{16,24},{24,16},{32,40},{40,32},{48,56},{56,48},{64,72... | collective-permute-start | bytes 2359304 | tf_op jit(solution)/shard_map/ppermute | solution.py:43
  92.6 23.3 %collective-permute-start.9 = (bf16[32,96,128]{2,1,0:T(8,128)(2,1)}, bf16[32,96,128]{2,1,0:T(8,128)(2,1)}, u32[]{:S(2)}, u32[]{:S(2)}) collective-permute-start(bf16[32,96,128]{2,1,0:T(8,128)(2,1)} %collective-permute-done.8.refs_4_), channel_id=1, source_target_pairs={{0,7},{1,0},{2,1},{3,2},{4,3},{5,4},{6,5},{7,6},{8,15},{9,8},{10,9... | collective-permute-start | bytes 2359304 | tf_op jit(solution)/shard_map/ppermute | solution.py:37
  92.7 23.2 %collective-permute-start.6 = (bf16[32,96,128]{2,1,0:T(8,128)(2,1)}, bf16[32,96,128]{2,1,0:T(8,128)(2,1)}, u32[]{:S(2)}, u32[]{:S(2)}) collective-permute-start(bf16[32,96,128]{2,1,0:T(8,128)(2,1)} %collective-permute-done.5.refs_2_), channel_id=1, source_target_pairs={{0,1},{1,2},{2,3},{3,4},{4,5},{5,6},{6,7},{7,0},{8,9},{9,10},{10,1... | collective-permute-start | bytes 2359304 | tf_op jit(solution)/shard_map/ppermute | solution.py:37
  115.9 26.0 %collective-permute-start.17 = (bf16[32,96,128]{2,1,0:T(8,128)(2,1)}, bf16[32,96,128]{2,1,0:T(8,128)(2,1)S(1)}, u32[]{:S(2)}, u32[]{:S(2)}) collective-permute-start(bf16[32,96,128]{2,1,0:T(8,128)(2,1)} %collective-permute-done.6.refs_5_), channel_id=1, source_target_pairs={{0,8},{8,0},{16,24},{24,16},{32,40},{40,32},{48,56},{56,48},{64,72... | collective-permute-start | bytes 2359304 | tf_op jit(solution)/shard_map/ppermute | solution.py:43
  116.6 25.3 %collective-permute-start.15 = (bf16[32,96,128]{2,1,0:T(8,128)(2,1)}, bf16[32,96,128]{2,1,0:T(8,128)(2,1)S(1)}, u32[]{:S(2)}, u32[]{:S(2)}) collective-permute-start(bf16[32,96,128]{2,1,0:T(8,128)(2,1)} %collective-permute-done.6.refs_5_), channel_id=1, source_target_pairs={{0,1},{1,2},{2,3},{3,4},{4,5},{5,6},{6,7},{7,0},{16,17},{17,18},{1... | collective-permute-start | bytes 2359304 | tf_op jit(solution)/shard_map/ppermute | solution.py:37
  117.3 24.6 %collective-permute-start.18 = (bf16[32,96,128]{2,1,0:T(8,128)(2,1)}, bf16[32,96,128]{2,1,0:T(8,128)(2,1)S(1)}, u32[]{:S(2)}, u32[]{:S(2)}) collective-permute-start(bf16[32,96,128]{2,1,0:T(8,128)(2,1)} %collective-permute-done.9.refs_6_), channel_id=1, source_target_pairs={{0,8},{8,0},{16,24},{24,16},{32,40},{40,32},{48,56},{56,48},{64,72... | collective-permute-start | bytes 2359304 | tf_op jit(solution)/shard_map/ppermute | solution.py:43
  119.1 22.9 %collective-permute-start.16 = (bf16[32,96,128]{2,1,0:T(8,128)(2,1)}, bf16[32,96,128]{2,1,0:T(8,128)(2,1)}, u32[]{:S(2)}, u32[]{:S(2)}) collective-permute-start(bf16[32,96,128]{2,1,0:T(8,128)(2,1)} %collective-permute-done.9.refs_6_), channel_id=1, source_target_pairs={{8,15},{9,8},{10,9},{11,10},{12,11},{13,12},{14,13},{15,14},{24,31... | collective-permute-start | bytes 2359304 | tf_op jit(solution)/shard_map/ppermute | solution.py:37
  141.9 13.4 %copy-start.12 = (bf16[32,96,128]{2,1,0:T(8,128)(2,1)}, bf16[32,96,128]{2,1,0:T(8,128)(2,1)S(1)}, u32[]{:S(2)}) copy-start(bf16[32,96,128]{2,1,0:T(8,128)(2,1)S(1)} %collective-permute-done.15.refs_14_) | copy-start | bytes 2359300
  142.0 13.4 %collective-permute-start.19 = (bf16[32,96,128]{2,1,0:T(8,128)(2,1)S(1)}, bf16[32,96,128]{2,1,0:T(8,128)(2,1)}, u32[]{:S(2)}, u32[]{:S(2)}) collective-permute-start(bf16[32,96,128]{2,1,0:T(8,128)(2,1)S(1)} %collective-permute-done.15.refs_14_), channel_id=1, source_target_pairs={{0,8},{16,24},{32,40},{48,56},{64,72},{80,88},{96,104},{112,120},{... | collective-permute-start | bytes 2359304 | tf_op jit(solution)/shard_map/ppermute | solution.py:43
  143.3 12.1 %collective-permute-start.20 = (bf16[32,96,128]{2,1,0:T(8,128)(2,1)}, bf16[32,96,128]{2,1,0:T(8,128)(2,1)}, u32[]{:S(2)}, u32[]{:S(2)}) collective-permute-start(bf16[32,96,128]{2,1,0:T(8,128)(2,1)} %collective-permute-done.16.refs_15_), channel_id=1, source_target_pairs={{8,0},{24,16},{40,32},{56,48},{72,64},{88,80},{104,96},{120,112},{... | collective-permute-start | bytes 2359304 | tf_op jit(solution)/shard_map/ppermute | solution.py:43
  148.1 38.8 %all-to-all-start.2 = ((bf16[32,128,128]{2,1,0:T(8,128)(2,1)}), bf16[32,128,128]{2,1,0:T(8,128)(2,1)S(1)}, u32[]{:S(2)}, u32[]{:S(2)}) async-start(bf16[32,128,128]{2,1,0:T(8,128)(2,1)} %bitcast.25), calls=%async_computation.2 | async-start | bytes 2097152 | tf_op jit(solution)/shard_map/all_to_all | solution.py:400
  171.6 13.8 %collective-permute-start.21 = (bf16[32,768]{1,0:T(8,128)(2,1)S(1)}, bf16[32,768]{1,0:T(8,128)(2,1)S(1)}, u32[]{:S(2)}, u32[]{:S(2)}) collective-permute-start(bf16[32,768]{1,0:T(8,128)(2,1)S(1)} %get-tuple-element.48), channel_id=1, source_target_pairs={{8,0},{16,8},{24,16},{32,24},{40,32},{48,40},{56,48},{64,56},{72,6... | collective-permute-start | bytes 147464 | tf_op jit(solution)/shard_map/ppermute | solution.py:25
  173.7 11.6 %collective-permute-start.22 = (bf16[32,768]{1,0:T(8,128)(2,1)S(1)}, bf16[32,768]{1,0:T(8,128)(2,1)S(1)}, u32[]{:S(2)}, u32[]{:S(2)}) collective-permute-start(bf16[32,768]{1,0:T(8,128)(2,1)S(1)} %get-tuple-element.49), channel_id=1, source_target_pairs={{0,8},{8,16},{16,24},{24,32},{32,40},{40,48},{48,56},{56,64},{64,7... | collective-permute-start | bytes 147464 | tf_op jit(solution)/shard_map/ppermute | solution.py:25
  177.1 4.6 %collective-permute-start.23 = (bf16[16,768]{1,0:T(8,128)(2,1)S(1)}, bf16[16,768]{1,0:T(8,128)(2,1)S(1)}, u32[]{:S(2)}, u32[]{:S(2)}) collective-permute-start(bf16[16,768]{1,0:T(8,128)(2,1)S(1)} %get-tuple-element.46), channel_id=1, source_target_pairs={{0,16},{8,24},{16,32},{24,40},{32,48},{40,56},{48,64},{56,72},{64,... | collective-permute-start | bytes 73736 | tf_op jit(solution)/shard_map/ppermute | solution.py:25
  180.4 4.9 %collective-permute-start.24 = (bf16[16,768]{1,0:T(8,128)(2,1)S(1)}, bf16[16,768]{1,0:T(8,128)(2,1)S(1)}, u32[]{:S(2)}, u32[]{:S(2)}) collective-permute-start(bf16[16,768]{1,0:T(8,128)(2,1)S(1)} %get-tuple-element.47), channel_id=1, source_target_pairs={{16,0},{24,8},{32,16},{40,24},{48,32},{56,40},{64,48},{72,56},{80,... | collective-permute-start | bytes 73736 | tf_op jit(solution)/shard_map/ppermute | solution.py:25
  (10 other events, 39.6 us)

commit v3 on v0

v3 whole, which is shorter than its diff:
```python
import functools

import jax
import jax.numpy as jnp
from jax import lax
from jax.experimental import pallas as pl
from jax.experimental.pallas import tpu as pltpu
from jax.sharding import PartitionSpec as P

HD = 128
AB = 16
REACH = 3
PAD = 16
SCALING = HD ** (-0.5)
EXP2_SCALING = SCALING * 1.4426950408889634
F32 = jnp.float32
BF16 = jnp.bfloat16
VMEM_BYTES = 48 * 1024 * 1024


def kernel_params():
    return pltpu.CompilerParams(vmem_limit_bytes=VMEM_BYTES)


def handed_over(parts):
    return lax.all_to_all(parts, "seq", split_axis=0, concat_axis=0, tiled=True)


def gathered_by_doubling(block, axis):
    size = lax.axis_size(axis)
    here = lax.axis_index(axis)
    step = 1
    while step < size:
        other = lax.ppermute(block, axis, [(i, i ^ step) for i in range(size)])
        upper = (here & step) != 0
        block = jnp.concatenate(
            [jnp.where(upper, other, block), jnp.where(upper, block, other)], axis=0
        )
        step *= 2
    return block


def from_other_core(block):
    size = lax.axis_size("seq")
    return lax.ppermute(block, "seq", [(i, i ^ 1) for i in range(size)])


def contract(a, b, dim_a, dim_b):
    return lax.dot_general(a, b, (((dim_a,), (dim_b,)), ((), ())), preferred_element_type=F32)


def self_heads_kernel(group, q_ref, k_ref, v_ref, out_ref):
    rows = q_ref.shape[0]
    for head in range(group):
        cols = slice(head * HD, (head + 1) * HD)
        out_ref[head, 0:rows] = q_ref[:, cols]
        out_ref[head, rows : 2 * rows] = k_ref[:, cols]
        out_ref[head, 2 * rows : 3 * rows] = v_ref[:, cols]


def self_heads(q_local, k_local, v_local):
    _, rows, width = q_local.shape
    heads = width // HD
    group = 8
    block = pl.BlockSpec((None, rows, group * HD), lambda i: (0, 0, i))
    return pl.pallas_call(
        functools.partial(self_heads_kernel, group),
        grid=(heads // group,),
        in_specs=[block] * 3,
        out_specs=pl.BlockSpec((group, 3 * rows, HD), lambda i: (i, 0, 0)),
        out_shape=jax.ShapeDtypeStruct((heads, 3 * rows, HD), BF16),
        compiler_params=kernel_params(),
        cost_estimate=pl.CostEstimate(
            flops=0, bytes_accessed=6 * rows * width * 2, transcendentals=0
        ),
        name="self_heads",
    )(q_local, k_local, v_local)


def cross_heads_kernel(group, q_ref, grad_ref, audio_ref, live_ref, out_ref):
    rows = q_ref.shape[0]
    owned, features = audio_ref.shape
    chunks = features // HD // 2
    for head in range(group):
        cols = slice(head * HD, (head + 1) * HD)
        out_ref[head, 0:rows] = q_ref[:, cols]
        out_ref[head, rows : 2 * rows] = grad_ref[:, cols]
        for chunk in range(chunks):
            first = 2 * rows + chunk * owned
            lane = (head % 2 * chunks + chunk) * HD
            out_ref[head, first : first + owned] = audio_ref[:, lane : lane + HD]
        out_ref[head, 2 * rows + chunks * owned :] = live_ref[...]


def cross_heads(queries, grads, audio, live):
    _, rows, width = queries.shape
    _, owned, features = audio.shape
    heads = width // HD
    group = 8
    total = 2 * rows + owned * (features // HD // 2) + PAD
    block = pl.BlockSpec((None, rows, group * HD), lambda i: (0, 0, i))
    return pl.pallas_call(
        functools.partial(cross_heads_kernel, group),
        grid=(heads // group,),
        in_specs=[
            block,
            block,
            pl.BlockSpec((None, owned, features), lambda i: (0, 0, 0)),
            pl.BlockSpec((PAD, HD), lambda i: (0, 0)),
        ],
        out_specs=pl.BlockSpec((group, total, HD), lambda i: (i, 0, 0)),
        out_shape=jax.ShapeDtypeStruct((heads, total, HD), BF16),
        compiler_params=kernel_params(),
        cost_estimate=pl.CostEstimate(
            flops=0, bytes_accessed=5 * rows * width * 2, transcendentals=0
        ),
        name="cross_heads",
    )(queries, grads, audio, live)


def cross_kernel(
    rows,
    place_ref,
    got_ref,
    other_ref,
    proj_ref,
    out_ref,
    sent_ref,
    audio,
    keys,
    values,
    d_keys,
    d_values,
):
    sources = got_ref.shape[0]
    owned = AB * 2
    chunks = other_ref.shape[1] // owned
    length = sources * owned
    edge = REACH * AB
    band = HD
    at_once = 8
    first_audio = 2 * rows

    for chunk in range(chunks):
        own_lanes = pl.ds(pl.multiple_of(place_ref[0] + chunk * HD, HD), HD)
        other_lanes = pl.ds(pl.multiple_of(place_ref[1] + chunk * HD, HD), HD)
        own_rows = slice(first_audio + chunk * owned, first_audio + (chunk + 1) * owned)
        other_rows = slice(chunk * owned, (chunk + 1) * owned)
        audio[:, own_lanes] = got_ref[:, own_rows].reshape(length, HD)
        audio[:, other_lanes] = other_ref[:, other_rows].reshape(length, HD)

    keys[...] = jnp.zeros_like(keys)
    values[...] = jnp.zeros_like(values)
    d_keys[...] = jnp.zeros_like(d_keys)
    d_values[...] = jnp.zeros_like(d_values)
    step = 256
    for i in range(length // step):
        both = jnp.dot(
            audio[i * step : (i + 1) * step], proj_ref[...], preferred_element_type=F32
        ).astype(BF16)
        keys[edge + i * step : edge + (i + 1) * step] = both[:, :HD]
        values[edge + i * step : edge + (i + 1) * step] = both[:, HD:]

    def some(block, carry):
        sources_here = [block * at_once + i for i in range(at_once)]
        bands = [pl.ds(pl.multiple_of(t * owned, owned), band) for t in sources_here]
        k = [keys[b] for b in bands]
        v = [values[b] for b in bands]
        scores = [contract(got_ref[t, 0:rows], k[i], 1, 1) for i, t in enumerate(sources_here)]
        d_probs = [
            contract(got_ref[t, rows : 2 * rows], v[i], 1, 1)
            for i, t in enumerate(sources_here)
        ]
        weights = []
        for i, t in enumerate(sources_here):
            masks = got_ref[t, first_audio + chunks * owned :].astype(F32)
            live = jnp.concatenate(
                [jnp.broadcast_to(masks[f : f + 1], (rows // 2, band)) for f in range(2)], axis=0
            )
            masked = jnp.where(live > 0, scores[i], -1e30)
            top = jnp.max(masked, axis=1, keepdims=True)
            raised = jnp.exp2((masked - top) * EXP2_SCALING)
            weights.append(raised / jnp.sum(raised, axis=1, keepdims=True))
        weights_b = [part.astype(BF16) for part in weights]
        d_scores = []
        for i in range(at_once):
            weighed = weights[i] * d_probs[i]
            inner = jnp.sum(weighed, axis=1, keepdims=True)
            d_scores.append((weighed - weights[i] * inner).astype(BF16))
        for i, t in enumerate(sources_here):
            out_ref[t] = jnp.dot(weights_b[i], v[i], preferred_element_type=F32)
        for i, t in enumerate(sources_here):
            d_values[bands[i]] += contract(weights_b[i], got_ref[t, rows : 2 * rows], 0, 0)
            d_keys[bands[i]] += contract(d_scores[i], got_ref[t, 0:rows], 0, 0)
        return carry

    lax.fori_loop(0, sources // at_once, some, 0)

    for i in range(length // step):
        here = slice(edge + i * step, edge + (i + 1) * step)
        d_both = jnp.concatenate(
            [(d_keys[here] * SCALING).astype(BF16), d_values[here].astype(BF16)], axis=1
        )
        term = contract(d_both, proj_ref[...], 1, 1).astype(BF16)
        per = step // owned
        for chunk in range(2 * chunks):
            sent_ref[i * per : (i + 1) * per, chunk * owned : (chunk + 1) * owned] = term[
                :, chunk * HD : (chunk + 1) * HD
            ].reshape(per, owned, HD)


def cross_attention(place, got, other_audio, proj, rows):
    sources, total, _ = got.shape
    audio_rows = other_audio.shape[1]
    features = proj.shape[0]
    owned = 2 * AB
    length = sources * owned
    padded = length + HD - owned
    return pl.pallas_call(
        functools.partial(cross_kernel, rows),
        grid=(1,),
        in_specs=[
            pl.BlockSpec(memory_space=pltpu.SMEM),
            pl.BlockSpec((sources, total, HD), lambda i: (0, 0, 0)),
            pl.BlockSpec((sources, audio_rows, HD), lambda i: (0, 0, 0)),
            pl.BlockSpec((features, 2 * HD), lambda i: (0, 0)),
        ],
        out_specs=[
            pl.BlockSpec((sources, rows, HD), lambda i: (0, 0, 0)),
            pl.BlockSpec((sources, 2 * audio_rows, HD), lambda i: (0, 0, 0)),
        ],
        out_shape=[
            jax.ShapeDtypeStruct((sources, rows, HD), F32),
            jax.ShapeDtypeStruct((sources, 2 * audio_rows, HD), BF16),
        ],
        scratch_shapes=[
            pltpu.VMEM((length, features), BF16),
            pltpu.VMEM((padded, HD), BF16),
            pltpu.VMEM((padded, HD), BF16),
            pltpu.VMEM((padded, HD), F32),
            pltpu.VMEM((padded, HD), F32),
        ],
        compiler_params=kernel_params(),
        cost_estimate=pl.CostEstimate(
            flops=8 * length * features * HD + 10 * sources * rows * HD * HD,
            bytes_accessed=2 * (got.size + 3 * other_audio.size + proj.size),
            transcendentals=sources * rows * HD,
        ),
        name="cross_attention",
    )(place, got, other_audio, proj)


def self_attention_kernel(
    block_rows,
    block_keys,
    q_ref,
    k_ref,
    v_ref,
    cross_ref,
    out_ref,
    keys_t,
    values_x,
    scores,
    tops,
):
    chunk = q_ref.shape[1]
    length = k_ref.shape[0] * chunk
    key_blocks = length // block_keys
    query_blocks = length // block_rows
    for piece in range(length // chunk):
        keys_t[:, piece * chunk : (piece + 1) * chunk] = k_ref[piece].T
        values_x[piece * chunk : (piece + 1) * chunk, :HD] = v_ref[piece]
    values_x[:, HD:] = jnp.ones((length, HD), BF16)
    per_block = block_rows // chunk

    def queries_of(block):
        rows = q_ref[pl.ds(block * per_block, per_block)]
        return rows.reshape(block_rows, HD)

    def highest(top, part):
        for group in range(part.shape[1] // HD):
            lanes = part[:, group * HD : (group + 1) * HD]
            top = lanes if top is None else jnp.maximum(top, lanes)
        return top

    def row_max(top):
        return jnp.broadcast_to(jnp.max(top, axis=1, keepdims=True), (block_rows, HD))

    first = queries_of(0)
    top = None
    for j in range(key_blocks):
        keys = slice(j * block_keys, (j + 1) * block_keys)
        part = jnp.dot(first, keys_t[:, keys], preferred_element_type=F32)
        scores[0, :, keys] = part
        top = highest(top, part)
    tops[0] = row_max(top)

    def body(i, carry):
        slot = lax.rem(i, 2)
        later = 1 - slot
        queries = queries_of(jnp.minimum(i + 1, query_blocks - 1))
        top_here = tops[slot][:, :1]
        top = None
        total = None
        for j in range(key_blocks):
            keys = slice(j * block_keys, (j + 1) * block_keys)
            part = jnp.dot(queries, keys_t[:, keys], preferred_element_type=F32)
            scores[later, :, keys] = part
            top = highest(top, part)
            raised = jnp.exp2((scores[slot, :, keys] - top_here) * EXP2_SCALING).astype(BF16)
            mixed = jnp.dot(raised, values_x[keys, :], preferred_element_type=F32)
            total = mixed if total is None else total + mixed
        tops[later] = row_max(top)
        own = (total[:, :HD] / total[:, HD:]).astype(BF16).astype(F32)
        rows = pl.ds(i * per_block, per_block)
        own = own.reshape(per_block, chunk, HD)
        out_ref[rows] = (own + cross_ref[rows]).astype(BF16)
        return carry

    lax.fori_loop(0, query_blocks, body, 0)


def attend_self(qkv, cross_out):
    sources, _, rows, _ = qkv.shape
    length = sources * rows
    block_rows, block_keys = 512, 512

    def whole(which):
        return pl.BlockSpec((sources, None, rows, HD), lambda i: (0, which, 0, 0))

    flat = pl.BlockSpec((sources, rows, HD), lambda i: (0, 0, 0))
    return pl.pallas_call(
        functools.partial(self_attention_kernel, block_rows, block_keys),
        grid=(1,),
        in_specs=[whole(0), whole(1), whole(2), flat],
        out_specs=flat,
        out_shape=jax.ShapeDtypeStruct((sources, rows, HD), BF16),
        scratch_shapes=[
            pltpu.VMEM((HD, length), BF16),
            pltpu.VMEM((length, 2 * HD), BF16),
            pltpu.VMEM((2, block_rows, length), F32),
            pltpu.VMEM((2, block_rows, HD), F32),
        ],
        compiler_params=kernel_params(),
        cost_estimate=pl.CostEstimate(
            flops=8 * length * length * HD,
            bytes_accessed=12 * length * HD,
            transcendentals=length * length,
        ),
        name="self_attention",
    )(qkv, qkv, qkv, cross_out)


def tokens_kernel(group, own_ref, out_ref):
    for head in range(group):
        out_ref[:, head * HD : (head + 1) * HD] = own_ref[head]


def heads_beside(own_tokens):
    heads, rows, _ = own_tokens.shape
    group = 8
    return pl.pallas_call(
        functools.partial(tokens_kernel, group),
        grid=(heads // group,),
        in_specs=[pl.BlockSpec((group, rows, HD), lambda i: (i, 0, 0))],
        out_specs=pl.BlockSpec((None, rows, group * HD), lambda i: (0, 0, i)),
        out_shape=jax.ShapeDtypeStruct((1, rows, heads * HD), BF16),
        compiler_params=kernel_params(),
        cost_estimate=pl.CostEstimate(
            flops=0, bytes_accessed=4 * rows * heads * HD, transcendentals=0
        ),
        name="heads_beside",
    )(own_tokens)


def sum_kernel(terms_ref, out_ref):
    owned = out_ref.shape[0]
    total = jnp.sum(terms_ref[...].astype(F32), axis=0)
    for chunk in range(total.shape[0] // owned):
        out_ref[:, chunk * HD : (chunk + 1) * HD] = total[chunk * owned : (chunk + 1) * owned]


def summed(terms, owned):
    heads, total, _ = terms.shape
    features = total // owned * HD
    return pl.pallas_call(
        sum_kernel,
        grid=(1,),
        in_specs=[pl.BlockSpec((heads, total, HD), lambda i: (0, 0, 0))],
        out_specs=pl.BlockSpec((None, owned, features), lambda i: (0, 0, 0)),
        out_shape=jax.ShapeDtypeStruct((1, owned, features), F32),
        compiler_params=kernel_params(),
        cost_estimate=pl.CostEstimate(
            flops=terms.size, bytes_accessed=2 * terms.size, transcendentals=0
        ),
        name="summed",
    )(terms)


def live_band(window_ids, live_counts, band_first, band_blocks):
    slots = jnp.arange(window_ids.shape[1], dtype=jnp.int32)
    blocks = band_first + jnp.arange(band_blocks, dtype=jnp.int32)
    hits = (window_ids[:, :, None] == blocks[None, None, :]) & (
        slots[None, :, None] < live_counts[:, None, None]
    )
    live = jnp.any(hits, axis=1).astype(BF16)
    live = jnp.repeat(live, AB, axis=1)
    return jnp.pad(live, ((0, PAD - live.shape[0]), (0, 0)))


def local(
    self_q,
    self_k,
    self_v,
    cross_q,
    audio,
    key_weight,
    value_weight,
    intersection,
    counts,
    cotangent,
):
    here = lax.axis_index("seq")
    core = lax.rem(here, 2)
    rows = self_q.shape[1]
    owned, features = audio.shape[1:]

    live = live_band(intersection[0], counts[0], here * 2 - REACH, HD // AB)
    cross = cross_heads(cross_q, cotangent, audio, live)
    cross, key_weight, value_weight = lax.optimization_barrier((cross, key_weight, value_weight))
    cross = handed_over(cross)

    both = jnp.concatenate([key_weight, value_weight], axis=1)
    proj = gathered_by_doubling(both[None], "fsdp").reshape(-1, 2 * HD)
    place = jnp.stack([core, 1 - core]).astype(jnp.int32) * (features // 2)
    qkv = self_heads(self_q, self_k, self_v)
    cross, qkv, proj, place = lax.optimization_barrier((cross, qkv, proj, place))

    qkv = handed_over(qkv).reshape(-1, 3, rows, HD)
    other_audio = from_other_core(cross[:, 2 * rows : cross.shape[1] - PAD])
    cross_out, sent = cross_attention(place, cross, other_audio, proj, rows)
    terms = handed_over(sent)
    own_heads = attend_self(qkv, cross_out)
    own_heads, terms = lax.optimization_barrier((own_heads, terms))
    own_tokens = handed_over(own_heads)
    audio_grad = summed(terms, owned)
    return (heads_beside(own_tokens), audio_grad)


def solution(mesh):
    in_specs = (
        P("fsdp", "seq", None),
        P("fsdp", "seq", None),
        P("fsdp", "seq", None),
        P("fsdp", "seq", None),
        P("fsdp", "seq", None),
        P("fsdp", "seq"),
        P("fsdp", "seq"),
        P("fsdp", "seq", None),
        P("fsdp", "seq"),
        P("fsdp", "seq", None),
    )
    out_specs = (P("fsdp", "seq", None), P("fsdp", "seq", None))
    return jax.shard_map(local, mesh=mesh, in_specs=in_specs, out_specs=out_specs, check_vma=False)
```

time: 206 us -> 170 us (0.83); the launches traced: 203 us -> 169 us
  Pallas kernels: 65.2 us -> 48 us
  between operations: 14.3 us -> 0.8 us
  starting transfers between devices: 54.1 us -> 43 us
  local copies, waits for them, and re-layouts: 3.64 us -> 10.2 us
  waiting for transfers between devices: 61.3 us -> 64.9 us
    ppermute x8 -> x1, starting transfers between devices: 20 us -> 0.44 us  [from_other_core(): return lax.ppermute(block, 'seq', [(i, i ^ 1) for i in range(size)])]
    pallas_call x2 -> x5, Pallas kernels: 35 us -> 16.1 us  [the longest x1 8.62 us: cross_attention(): pl.pallas_call(functools.partial(cross_kernel, rows), grid=(1,), in_specs...]
    all_to_all x2 -> x4, starting transfers between devices: 21.3 us -> 29 us  [handed_over(): return lax.all_to_all(parts, 'seq', split_axis=0, concat_axis=0, tiled=True)]
    unnamed x22 -> x24, local copies, waits for them, and re-layouts: 3.45 us -> 8.83 us
    ppermute x3, waiting for transfers between devices: 6.66 us -> 9.34 us  [gathered_by_doubling(): other = lax.ppermute(block, axis, [(i, i ^ step) for i in range(size)])]
    all_to_all x2 -> x4, waiting for transfers between devices: 51.3 us -> 53.6 us  [handed_over(): return lax.all_to_all(parts, 'seq', split_axis=0, concat_axis=0, tiled=True)]
  transfers between devices with their start and end apart: 14 -> 8, of which waited for: 6 -> 7; matrix products, arithmetic and copies ran while one was open for 0% -> 1% of each run, Pallas kernels for 16% -> 26%
where the time goes in v3:
time: 170 us; the launch traced here: 169 us
  waiting for transfers between devices  64.9 us (38%)
  Pallas kernels  48 us (28%)
  starting transfers between devices  43 us (25%)
  local copies, waits for them, and re-layouts  10.2 us (6%)
  other arithmetic  2.66 us (2%)
    all_to_all x4, waiting for transfers between devices, handed_over(): return lax.all_to_all(parts, 'seq', split_axis=0, concat_axis=0, tiled=True)  53.6 us
    pallas_call x1, Pallas kernels, attend_self(): pl.pallas_call(functools.partial(self_attention_kernel, block_rows, block...  31.9 us
    all_to_all x4, starting transfers between devices, handed_over(): return lax.all_to_all(parts, 'seq', split_axis=0, concat_axis=0, tiled=True)  29 us
    ppermute x3, starting transfers between devices, gathered_by_doubling(): other = lax.ppermute(block, axis, [(i, i ^ step) for i in range(size)])  13.5 us
    ppermute x3, waiting for transfers between devices, gathered_by_doubling(): other = lax.ppermute(block, axis, [(i, i ^ step) for i in range(size)])  9.34 us
    unnamed x24, local copies, waits for them, and re-layouts  8.83 us
    pallas_call x1, Pallas kernels, cross_attention(): pl.pallas_call(functools.partial(cross_kernel, rows), grid=(1,), in_specs...  8.62 us
  transfers between devices with their start and end apart: 8, of which 7 were waited for; matrix products, arithmetic and copies ran while one was open for 1% of the time, Pallas kernels for 26%

profile of v3, /device:TPU:1, one launch (start us, length us, event | category | flops | bytes accessed | tf_op | source)
XLA Modules:
  0.0 169.5 jit_solution(13356919039665511344)
XLA Ops:
  0.6 0.7 iota_compare_fusion
  1.4 0.8 and_reduce_fusion
  2.3 1.2 copy-done.1
  3.6 1.2 copy-done.2
  4.8 0.8 copy-done.6
  5.6 2.5 %cross_heads.1 = bf16[32,368,128]{2,1,0:T(8,128)(2,1)} custom-call(bf16[1,128,4096]{2,1,0:T(8,128)(2,1)S(1)} %copy-done.1, bf16[1,128,4096]{2,1,0:T(8,128)(2,1)S(1)} %copy-done.2, bf16[1,32,768]{2,1,0:T(8,128)(2,1)S(1)} %copy-done.6, bf16[16,128]{1,0:T(8,128)(2,1)S(1)} %pad.4.live_ref), custom_call_target="tpu_custom_call" | custom-call | bytes 5242880 | tf_op jit(solution)/shard_map/cross_heads/pallas_call | solution.py:102
  8.1 8.9 %all-to-all-start = ((bf16[32,368,128]{2,1,0:T(8,128)(2,1)}), bf16[32,368,128]{2,1,0:T(8,128)(2,1)}, u32[]{:S(2)}, u32[]{:S(2)}) async-start(bf16[32,368,128]{2,1,0:T(8,128)(2,1)} %cross_heads.1), calls=%async_computation | async-start | bytes 6029312 | tf_op jit(solution)/shard_map/all_to_all | solution.py:26
  17.0 1.7 %collective-permute-start = (bf16[1,96,256]{2,1,0:T(8,128)(2,1)S(1)}, bf16[1,96,256]{2,1,0:T(8,128)(2,1)S(1)}, u32[]{:S(2)}, u32[]{:S(2)}) collective-permute-start(bf16[1,96,256]{2,1,0:T(8,128)(2,1)S(1)} %maximum_bitcast_fusion), channel_id=1, source_target_pairs={{0,1},{1,0},{2,3},{3,2},{4,5},{5,4},{6,7},{7,6},{8,9},{9,8},{10,11... | collective-permute-start | bytes 147464 | tf_op jit(solution)/shard_map/ppermute | solution.py:34
  18.8 1.9 %collective-permute-done = bf16[1,96,256]{2,1,0:T(8,128)(2,1)S(1)} collective-permute-done((bf16[1,96,256]{2,1,0:T(8,128)(2,1)S(1)}, bf16[1,96,256]{2,1,0:T(8,128)(2,1)S(1)}, u32[]{:S(2)}, u32[]{:S(2)}) %collective-permute-start) | collective-permute-done | bytes 49184 | tf_op jit(solution)/shard_map/ppermute | solution.py:34
  20.7 3.1 %collective-permute-start.1 = (bf16[2,96,256]{2,1,0:T(8,128)(2,1)S(1)}, bf16[2,96,256]{2,1,0:T(8,128)(2,1)S(1)}, u32[]{:S(2)}, u32[]{:S(2)}) collective-permute-start(bf16[2,96,256]{2,1,0:T(8,128)(2,1)S(1)} %pad_maximum_fusion.2), channel_id=1, source_target_pairs={{0,2},{1,3},{2,0},{3,1},{4,6},{5,7},{6,4},{7,5},{8,10},{9,11},{10,... | collective-permute-start | bytes 294920 | tf_op jit(solution)/shard_map/ppermute | solution.py:34
  23.8 2.4 %collective-permute-done.1 = bf16[2,96,256]{2,1,0:T(8,128)(2,1)S(1)} collective-permute-done((bf16[2,96,256]{2,1,0:T(8,128)(2,1)S(1)}, bf16[2,96,256]{2,1,0:T(8,128)(2,1)S(1)}, u32[]{:S(2)}, u32[]{:S(2)}) %collective-permute-start.1) | collective-permute-done | bytes 98336 | tf_op jit(solution)/shard_map/ppermute | solution.py:34
  26.2 8.7 %collective-permute-start.2 = (bf16[4,96,256]{2,1,0:T(8,128)(2,1)S(1)}, bf16[4,96,256]{2,1,0:T(8,128)(2,1)}, u32[]{:S(2)}, u32[]{:S(2)}) collective-permute-start(bf16[4,96,256]{2,1,0:T(8,128)(2,1)S(1)} %pad_maximum_fusion.1), channel_id=1, source_target_pairs={{0,4},{1,5},{2,6},{3,7},{4,0},{5,1},{6,2},{7,3},{8,12},{9,13},{10,... | collective-permute-start | bytes 589832 | tf_op jit(solution)/shard_map/ppermute | solution.py:34
  35.0 2.5 %self_heads.1 = bf16[32,384,128]{2,1,0:T(8,128)(2,1)} custom-call(bf16[1,128,4096]{2,1,0:T(8,128)(2,1)S(1)} %copy-done.3, bf16[1,128,4096]{2,1,0:T(8,128)(2,1)S(1)} %copy-done.4, bf16[1,128,4096]{2,1,0:T(8,128)(2,1)S(1)} %copy-done.5), custom_call_target="tpu_custom_call" | custom-call | bytes 6291456 | tf_op jit(solution)/shard_map/self_heads/pallas_call | solution.py:66
  37.5 5.1 %collective-permute-done.2 = bf16[4,96,256]{2,1,0:T(8,128)(2,1)} collective-permute-done((bf16[4,96,256]{2,1,0:T(8,128)(2,1)S(1)}, bf16[4,96,256]{2,1,0:T(8,128)(2,1)}, u32[]{:S(2)}, u32[]{:S(2)}) %collective-permute-start.2) | collective-permute-done | bytes 196640 | tf_op jit(solution)/shard_map/ppermute | solution.py:34
  42.6 1.0 broadcast_select_fusion.1
  43.6 11.6 %all-to-all-done.got_ref = bf16[32,368,128]{2,1,0:T(8,128)(2,1)} async-done(((bf16[32,368,128]{2,1,0:T(8,128)(2,1)}), bf16[32,368,128]{2,1,0:T(8,128)(2,1)}, u32[]{:S(2)}, u32[]{:S(2)}) %all-to-all-start) | async-done | bytes 3014688 | tf_op jit(solution)/shard_map/all_to_all | solution.py:26
  55.2 6.1 %all-to-all-start.1 = ((bf16[32,384,128]{2,1,0:T(8,128)(2,1)}), bf16[32,384,128]{2,1,0:T(8,128)(2,1)S(1)}, u32[]{:S(2)}, u32[]{:S(2)}) async-start(bf16[32,384,128]{2,1,0:T(8,128)(2,1)} %self_heads.1), calls=%async_computation.1 | async-start | bytes 6291456 | tf_op jit(solution)/shard_map/all_to_all | solution.py:26
  61.3 1.2 slice.3
  62.5 0.4 collective-permute-start.3
  62.9 1.9 %collective-permute-done.3.other_ref = bf16[32,96,128]{2,1,0:T(8,128)(2,1)S(1)} collective-permute-done((bf16[32,96,128]{2,1,0:T(8,128)(2,1)S(1)}, bf16[32,96,128]{2,1,0:T(8,128)(2,1)S(1)}, u32[]{:S(2)}, u32[]{:S(2)}) %collective-permute-start.3) | collective-permute-done | bytes 786464 | tf_op jit(solution)/shard_map/ppermute | solution.py:45
  64.9 8.6 %cross_attention.1 = (f32[32,128,128]{2,1,0:T(8,128)S(1)}, bf16[32,192,128]{2,1,0:T(8,128)(2,1)}) custom-call(s32[2]{0:T(128)S(1)} %add_multiply_fusion.place_ref, bf16[32,368,128]{2,1,0:T(8,128)(2,1)} %all-to-all-done.got_ref, bf16[32,96,128]{2,1,0:T(8,128)(2,1)S(1)} %collective-permute-done.3.other_ref, bf16[768,256]{1,0:T(8,128)(2,1)S(1)} %bitcast.12), custom_call_target="tpu_custom_call" | custom-call | flops 1476395008 | bytes 5767168 | tf_op jit(solution)/shard_map/cross_attention/pallas_call | solution.py:219
  73.5 1.4 copy-done.7
  74.9 25.7 %all-to-all-done.1 = bf16[32,384,128]{2,1,0:T(8,128)(2,1)S(1)} async-done(((bf16[32,384,128]{2,1,0:T(8,128)(2,1)}), bf16[32,384,128]{2,1,0:T(8,128)(2,1)S(1)}, u32[]{:S(2)}, u32[]{:S(2)}) %all-to-all-start.1) | async-done | bytes 3145760 | tf_op jit(solution)/shard_map/all_to_all | solution.py:26
  100.6 1.6 copy-done.9
  102.2 6.5 %all-to-all-start.2 = ((bf16[32,192,128]{2,1,0:T(8,128)(2,1)}), bf16[32,192,128]{2,1,0:T(8,128)(2,1)S(1)}, u32[]{:S(2)}, u32[]{:S(2)}) async-start(bf16[32,192,128]{2,1,0:T(8,128)(2,1)} %get-tuple-element.21), calls=%async_computation.2 | async-start | bytes 3145728 | tf_op jit(solution)/shard_map/all_to_all | solution.py:26
  108.7 1.6 copy-done.8
  110.3 31.9 %self_attention.1 = bf16[32,128,128]{2,1,0:T(8,128)(2,1)S(1)} custom-call(bf16[32,3,128,128]{3,2,1,0:T(8,128)(2,1)} %bitcast.13, bf16[32,3,128,128]{3,2,1,0:T(8,128)(2,1)} %bitcast.14, bf16[32,3,128,128]{3,2,1,0:T(8,128)(2,1)} %bitcast.15, f32[32,128,128]{2,1,0:T(8,128)S(1)} %copy-done.8), custom_call_target="tpu_custom_call" | custom-call | flops 17179869184 | bytes 6291456 | tf_op jit(solution)/shard_map/self_attention/pallas_call | solution.py:332
  142.2 1.0 copy-done
  143.2 7.5 %all-to-all-start.3 = ((bf16[32,128,128]{2,1,0:T(8,128)(2,1)}), bf16[32,128,128]{2,1,0:T(8,128)(2,1)S(1)}, u32[]{:S(2)}, u32[]{:S(2)}) async-start(bf16[32,128,128]{2,1,0:T(8,128)(2,1)} %copy-done), calls=%async_computation.3 | async-start | bytes 2097152 | tf_op jit(solution)/shard_map/all_to_all | solution.py:26
  150.7 0.9 summed.1
  151.5 16.3 %all-to-all-done.3.own_ref = bf16[32,128,128]{2,1,0:T(8,128)(2,1)S(1)} async-done(((bf16[32,128,128]{2,1,0:T(8,128)(2,1)}), bf16[32,128,128]{2,1,0:T(8,128)(2,1)S(1)}, u32[]{:S(2)}, u32[]{:S(2)}) %all-to-all-start.3) | async-done | bytes 1048608 | tf_op jit(solution)/shard_map/all_to_all | solution.py:26
  167.9 1.6 heads_beside.1
  (30 shorter events, 0.4 us)
Async XLA Ops:
  2.3 1.2 copy-start.1
  3.6 1.2 copy-start.2
  4.8 0.8 copy-start.6
  8.1 8.9 %copy-start.10 = (bf16[96,128]{1,0:T(8,128)(2,1)S(1)}, bf16[96,128]{1,0:T(8,128)(2,1)}, u32[]{:S(2)}) copy-start(bf16[96,128]{1,0:T(8,128)(2,1)} %param.16) | copy-start | bytes 73732
  8.1 9.0 %copy-start.11 = (bf16[96,128]{1,0:T(8,128)(2,1)S(1)}, bf16[96,128]{1,0:T(8,128)(2,1)}, u32[]{:S(2)}) copy-start(bf16[96,128]{1,0:T(8,128)(2,1)} %param.15) | copy-start | bytes 73732
  8.1 26.9 %copy-start.3 = (bf16[1,128,4096]{2,1,0:T(8,128)(2,1)S(1)}, bf16[1,128,4096]{2,1,0:T(8,128)(2,1)}, u32[]{:S(2)}) copy-start(bf16[1,128,4096]{2,1,0:T(8,128)(2,1)} %q_ref.3) | copy-start | bytes 3145732
  8.1 26.9 %copy-start.4 = (bf16[1,128,4096]{2,1,0:T(8,128)(2,1)S(1)}, bf16[1,128,4096]{2,1,0:T(8,128)(2,1)}, u32[]{:S(2)}) copy-start(bf16[1,128,4096]{2,1,0:T(8,128)(2,1)} %k_ref.1) | copy-start | bytes 3145732
  8.1 26.9 %copy-start.5 = (bf16[1,128,4096]{2,1,0:T(8,128)(2,1)S(1)}, bf16[1,128,4096]{2,1,0:T(8,128)(2,1)}, u32[]{:S(2)}) copy-start(bf16[1,128,4096]{2,1,0:T(8,128)(2,1)} %v_ref.1) | copy-start | bytes 3145732
  8.1 47.1 %all-to-all-start = ((bf16[32,368,128]{2,1,0:T(8,128)(2,1)}), bf16[32,368,128]{2,1,0:T(8,128)(2,1)}, u32[]{:S(2)}, u32[]{:S(2)}) async-start(bf16[32,368,128]{2,1,0:T(8,128)(2,1)} %cross_heads.1), calls=%async_computation | async-start | bytes 6029312 | tf_op jit(solution)/shard_map/all_to_all | solution.py:26
  17.0 3.6 %collective-permute-start = (bf16[1,96,256]{2,1,0:T(8,128)(2,1)S(1)}, bf16[1,96,256]{2,1,0:T(8,128)(2,1)S(1)}, u32[]{:S(2)}, u32[]{:S(2)}) collective-permute-start(bf16[1,96,256]{2,1,0:T(8,128)(2,1)S(1)} %maximum_bitcast_fusion), channel_id=1, source_target_pairs={{0,1},{1,0},{2,3},{3,2},{4,5},{5,4},{6,7},{7,6},{8,9},{9,8},{10,11... | collective-permute-start | bytes 147464 | tf_op jit(solution)/shard_map/ppermute | solution.py:34
  20.7 5.5 %collective-permute-start.1 = (bf16[2,96,256]{2,1,0:T(8,128)(2,1)S(1)}, bf16[2,96,256]{2,1,0:T(8,128)(2,1)S(1)}, u32[]{:S(2)}, u32[]{:S(2)}) collective-permute-start(bf16[2,96,256]{2,1,0:T(8,128)(2,1)S(1)} %pad_maximum_fusion.2), channel_id=1, source_target_pairs={{0,2},{1,3},{2,0},{3,1},{4,6},{5,7},{6,4},{7,5},{8,10},{9,11},{10,... | collective-permute-start | bytes 294920 | tf_op jit(solution)/shard_map/ppermute | solution.py:34
  26.2 16.4 %collective-permute-start.2 = (bf16[4,96,256]{2,1,0:T(8,128)(2,1)S(1)}, bf16[4,96,256]{2,1,0:T(8,128)(2,1)}, u32[]{:S(2)}, u32[]{:S(2)}) collective-permute-start(bf16[4,96,256]{2,1,0:T(8,128)(2,1)S(1)} %pad_maximum_fusion.1), channel_id=1, source_target_pairs={{0,4},{1,5},{2,6},{3,7},{4,0},{5,1},{6,2},{7,3},{8,12},{9,13},{10,... | collective-permute-start | bytes 589832 | tf_op jit(solution)/shard_map/ppermute | solution.py:34
  55.2 45.4 %all-to-all-start.1 = ((bf16[32,384,128]{2,1,0:T(8,128)(2,1)}), bf16[32,384,128]{2,1,0:T(8,128)(2,1)S(1)}, u32[]{:S(2)}, u32[]{:S(2)}) async-start(bf16[32,384,128]{2,1,0:T(8,128)(2,1)} %self_heads.1), calls=%async_computation.1 | async-start | bytes 6291456 | tf_op jit(solution)/shard_map/all_to_all | solution.py:26
  62.5 2.4 %collective-permute-start.3 = (bf16[32,96,128]{2,1,0:T(8,128)(2,1)S(1)}, bf16[32,96,128]{2,1,0:T(8,128)(2,1)S(1)}, u32[]{:S(2)}, u32[]{:S(2)}) collective-permute-start(bf16[32,96,128]{2,1,0:T(8,128)(2,1)S(1)} %slice.3), channel_id=1, source_target_pairs={{0,8},{8,0},{16,24},{24,16},{32,40},{40,32},{48,56},{56,48},{64,72... | collective-permute-start | bytes 2359304 | tf_op jit(solution)/shard_map/ppermute | solution.py:45
  73.5 1.4 copy-start.7
  100.6 1.6 copy-start.9
  102.2 41.0 %all-to-all-start.2 = ((bf16[32,192,128]{2,1,0:T(8,128)(2,1)}), bf16[32,192,128]{2,1,0:T(8,128)(2,1)S(1)}, u32[]{:S(2)}, u32[]{:S(2)}) async-start(bf16[32,192,128]{2,1,0:T(8,128)(2,1)} %get-tuple-element.21), calls=%async_computation.2 | async-start | bytes 3145728 | tf_op jit(solution)/shard_map/all_to_all | solution.py:26
  108.7 1.6 copy-start.8
  142.2 1.0 copy-start
  143.2 24.7 %all-to-all-start.3 = ((bf16[32,128,128]{2,1,0:T(8,128)(2,1)}), bf16[32,128,128]{2,1,0:T(8,128)(2,1)S(1)}, u32[]{:S(2)}, u32[]{:S(2)}) async-start(bf16[32,128,128]{2,1,0:T(8,128)(2,1)} %copy-done), calls=%async_computation.3 | async-start | bytes 2097152 | tf_op jit(solution)/shard_map/all_to_all | solution.py:26

commit v4 on v3

v4 whole, which is shorter than its diff:
```python
import functools

import jax
import jax.numpy as jnp
from jax import lax
from jax.experimental import pallas as pl
from jax.experimental.pallas import tpu as pltpu
from jax.sharding import PartitionSpec as P

HD = 128
AB = 16
REACH = 3
PAD = 16
SCALING = HD ** (-0.5)
EXP2_SCALING = SCALING * 1.4426950408889634
F32 = jnp.float32
BF16 = jnp.bfloat16
MIB = 1024 * 1024


def kernel_params(mib=48):
    return pltpu.CompilerParams(vmem_limit_bytes=mib * MIB)


def handed_over(parts):
    return lax.all_to_all(parts, "seq", split_axis=0, concat_axis=0, tiled=True)


def gathered_by_doubling(block, axis):
    size = lax.axis_size(axis)
    here = lax.axis_index(axis)
    step = 1
    while step < size:
        other = lax.ppermute(block, axis, [(i, i ^ step) for i in range(size)])
        upper = (here & step) != 0
        block = jnp.concatenate(
            [jnp.where(upper, other, block), jnp.where(upper, block, other)], axis=0
        )
        step *= 2
    return block


def from_other_core(block):
    size = lax.axis_size("seq")
    return lax.ppermute(block, "seq", [(i, i ^ 1) for i in range(size)])


def contract(a, b, dim_a, dim_b):
    return lax.dot_general(a, b, (((dim_a,), (dim_b,)), ((), ())), preferred_element_type=F32)


def self_heads_kernel(group, q_ref, k_ref, v_ref, audio_ref, out_ref):
    rows = q_ref.shape[0]
    owned, features = audio_ref.shape
    chunks = features // HD // 2
    for head in range(group):
        cols = slice(head * HD, (head + 1) * HD)
        out_ref[head, 0:rows] = q_ref[:, cols]
        out_ref[head, rows : 2 * rows] = k_ref[:, cols]
        out_ref[head, 2 * rows : 3 * rows] = v_ref[:, cols]
        for chunk in range(chunks):
            first = 3 * rows + chunk * owned
            lane = (head % 2 * chunks + chunk) * HD
            out_ref[head, first : first + owned] = audio_ref[:, lane : lane + HD]


def self_heads(q_local, k_local, v_local, audio):
    _, rows, width = q_local.shape
    _, owned, features = audio.shape
    heads = width // HD
    group = 4
    total = 3 * rows + owned * (features // HD // 2)
    block = pl.BlockSpec((None, rows, group * HD), lambda i: (0, 0, i))
    return pl.pallas_call(
        functools.partial(self_heads_kernel, group),
        grid=(heads // group,),
        in_specs=[block] * 3 + [pl.BlockSpec((None, owned, features), lambda i: (0, 0, 0))],
        out_specs=pl.BlockSpec((group, total, HD), lambda i: (i, 0, 0)),
        out_shape=jax.ShapeDtypeStruct((heads, total, HD), BF16),
        compiler_params=kernel_params(60),
        cost_estimate=pl.CostEstimate(
            flops=0, bytes_accessed=7 * rows * width * 2, transcendentals=0
        ),
        name="self_heads",
    )(q_local, k_local, v_local, audio)


def cross_heads_kernel(group, ids_ref, counts_ref, first_ref, q_ref, grad_ref, out_ref):
    rows = q_ref.shape[0]
    frames, slots = ids_ref.shape
    blocks = first_ref[0] + lax.broadcasted_iota(jnp.int32, (PAD, HD), 1) // AB
    row = lax.broadcasted_iota(jnp.int32, (PAD, HD), 0)
    live = jnp.zeros((PAD, HD), F32)
    for frame in range(frames):
        for slot in range(slots):
            hit = (blocks == ids_ref[frame, slot]) & (row == frame)
            hit = hit & (counts_ref[frame] > slot)
            live = jnp.where(hit, 1.0, live)
    live = live.astype(BF16)
    for head in range(group):
        cols = slice(head * HD, (head + 1) * HD)
        out_ref[head, 0:rows] = q_ref[:, cols]
        out_ref[head, rows : 2 * rows] = grad_ref[:, cols]
        out_ref[head, 2 * rows :] = live


def cross_heads(window_ids, live_counts, band_first, queries, grads):
    _, rows, width = queries.shape
    heads = width // HD
    group = 8
    total = 2 * rows + PAD
    block = pl.BlockSpec((None, rows, group * HD), lambda i: (0, 0, i))
    scalars = pl.BlockSpec(memory_space=pltpu.SMEM)
    return pl.pallas_call(
        functools.partial(cross_heads_kernel, group),
        grid=(heads // group,),
        in_specs=[scalars, scalars, scalars, block, block],
        out_specs=pl.BlockSpec((group, total, HD), lambda i: (i, 0, 0)),
        out_shape=jax.ShapeDtypeStruct((heads, total, HD), BF16),
        compiler_params=kernel_params(60),
        cost_estimate=pl.CostEstimate(
            flops=0, bytes_accessed=4 * rows * width * 2, transcendentals=0
        ),
        name="cross_heads",
    )(window_ids, live_counts, band_first, queries, grads)


def cross_kernel(
    rows,
    place_ref,
    got_ref,
    mine_ref,
    other_ref,
    proj_ref,
    own_ref,
    out_ref,
    audio,
    keys,
    values,
    d_keys,
    d_values,
):
    sources = got_ref.shape[0]
    owned = AB * 2
    chunks = other_ref.shape[1] // owned
    length = sources * owned
    edge = REACH * AB
    band = HD
    at_once = 8

    for chunk in range(chunks):
        own_lanes = pl.ds(pl.multiple_of(place_ref[0] + chunk * HD, HD), HD)
        other_lanes = pl.ds(pl.multiple_of(place_ref[1] + chunk * HD, HD), HD)
        chunk_rows = slice(chunk * owned, (chunk + 1) * owned)
        audio[:, own_lanes] = mine_ref[:, chunk_rows].reshape(length, HD)
        audio[:, other_lanes] = other_ref[:, chunk_rows].reshape(length, HD)

    keys[...] = jnp.zeros_like(keys)
    values[...] = jnp.zeros_like(values)
    d_keys[...] = jnp.zeros_like(d_keys)
    d_values[...] = jnp.zeros_like(d_values)
    step = 256
    for i in range(length // step):
        both = jnp.dot(
            audio[i * step : (i + 1) * step], proj_ref[...], preferred_element_type=F32
        ).astype(BF16)
        keys[edge + i * step : edge + (i + 1) * step] = both[:, :HD]
        values[edge + i * step : edge + (i + 1) * step] = both[:, HD:]

    def some(block, carry):
        sources_here = [block * at_once + i for i in range(at_once)]
        bands = [pl.ds(pl.multiple_of(t * owned, owned), band) for t in sources_here]
        k = [keys[b] for b in bands]
        v = [values[b] for b in bands]
        scores = [contract(got_ref[t, 0:rows], k[i], 1, 1) for i, t in enumerate(sources_here)]
        d_probs = [
            contract(got_ref[t, rows : 2 * rows], v[i], 1, 1)
            for i, t in enumerate(sources_here)
        ]
        weights = []
        for i, t in enumerate(sources_here):
            masks = got_ref[t, 2 * rows :].astype(F32)
            live = jnp.concatenate(
                [jnp.broadcast_to(masks[f : f + 1], (rows // 2, band)) for f in range(2)], axis=0
            )
            masked = jnp.where(live > 0, scores[i], -1e30)
            top = jnp.max(masked, axis=1, keepdims=True)
            raised = jnp.exp2((masked - top) * EXP2_SCALING)
            weights.append(raised / jnp.sum(raised, axis=1, keepdims=True))
        weights_b = [part.astype(BF16) for part in weights]
        d_scores = []
        for i in range(at_once):
            weighed = weights[i] * d_probs[i]
            inner = jnp.sum(weighed, axis=1, keepdims=True)
            d_scores.append((weighed - weights[i] * inner).astype(BF16))
        for i, t in enumerate(sources_here):
            mixed = jnp.dot(weights_b[i], v[i], preferred_element_type=F32)
            out_ref[t, 0:rows] = (own_ref[t].astype(F32) + mixed).astype(BF16)
        for i, t in enumerate(sources_here):
            d_values[bands[i]] += contract(weights_b[i], got_ref[t, rows : 2 * rows], 0, 0)
            d_keys[bands[i]] += contract(d_scores[i], got_ref[t, 0:rows], 0, 0)
        return carry

    lax.fori_loop(0, sources // at_once, some, 0)

    for i in range(length // step):
        here = slice(edge + i * step, edge + (i + 1) * step)
        d_both = jnp.concatenate(
            [(d_keys[here] * SCALING).astype(BF16), d_values[here].astype(BF16)], axis=1
        )
        term = contract(d_both, proj_ref[...], 1, 1).astype(BF16)
        per = step // owned
        for chunk in range(2 * chunks):
            first = rows + chunk * owned
            out_ref[i * per : (i + 1) * per, first : first + owned] = term[
                :, chunk * HD : (chunk + 1) * HD
            ].reshape(per, owned, HD)


def cross_attention(place, got, mine, other, proj, own_heads):
    sources, rows, _ = own_heads.shape
    total = got.shape[1]
    audio_rows = mine.shape[1]
    features = proj.shape[0]
    owned = 2 * AB
    length = sources * owned
    padded = length + HD - owned

    def whole(*shape):
        return pl.BlockSpec(shape, lambda i: (0,) * len(shape))

    return pl.pallas_call(
        functools.partial(cross_kernel, rows),
        grid=(1,),
        in_specs=[
            pl.BlockSpec(memory_space=pltpu.SMEM),
            whole(sources, total, HD),
            whole(sources, audio_rows, HD),
            whole(sources, audio_rows, HD),
            whole(features, 2 * HD),
            whole(sources, rows, HD),
        ],
        out_specs=whole(sources, rows + 2 * audio_rows, HD),
        out_shape=jax.ShapeDtypeStruct((sources, rows + 2 * audio_rows, HD), BF16),
        scratch_shapes=[
            pltpu.VMEM((length, features), BF16),
            pltpu.VMEM((padded, HD), BF16),
            pltpu.VMEM((padded, HD), BF16),
            pltpu.VMEM((padded, HD), F32),
            pltpu.VMEM((padded, HD), F32),
        ],
        compiler_params=kernel_params(),
        cost_estimate=pl.CostEstimate(
            flops=8 * length * features * HD + 10 * sources * rows * HD * HD,
            bytes_accessed=2 * (got.size + 4 * mine.size + proj.size + 2 * own_heads.size),
            transcendentals=sources * rows * HD,
        ),
        name="cross_attention",
    )(place, got, mine, other, proj, own_heads)


def self_attention_kernel(
    block_rows,
    block_keys,
    q_ref,
    k_ref,
    v_ref,
    out_ref,
    keys_t,
    values_x,
    scores,
    tops,
):
    chunk = q_ref.shape[1]
    length = k_ref.shape[0] * chunk
    key_blocks = length // block_keys
    query_blocks = length // block_rows
    for piece in range(length // chunk):
        keys_t[:, piece * chunk : (piece + 1) * chunk] = k_ref[piece].T
        values_x[piece * chunk : (piece + 1) * chunk, :HD] = v_ref[piece]
    values_x[:, HD:] = jnp.ones((length, HD), BF16)
    per_block = block_rows // chunk

    def queries_of(block):
        rows = q_ref[pl.ds(block * per_block, per_block)]
        return rows.reshape(block_rows, HD)

    def highest(top, part):
        for group in range(part.shape[1] // HD):
            lanes = part[:, group * HD : (group + 1) * HD]
            top = lanes if top is None else jnp.maximum(top, lanes)
        return top

    def row_max(top):
        return jnp.broadcast_to(jnp.max(top, axis=1, keepdims=True), (block_rows, HD))

    first = queries_of(0)
    top = None
    for j in range(key_blocks):
        keys = slice(j * block_keys, (j + 1) * block_keys)
        part = jnp.dot(first, keys_t[:, keys], preferred_element_type=F32)
        scores[0, :, keys] = part
        top = highest(top, part)
    tops[0] = row_max(top)

    def body(i, carry):
        slot = lax.rem(i, 2)
        later = 1 - slot
        queries = queries_of(jnp.minimum(i + 1, query_blocks - 1))
        top_here = tops[slot][:, :1]
        top = None
        total = None
        for j in range(key_blocks):
            keys = slice(j * block_keys, (j + 1) * block_keys)
            part = jnp.dot(queries, keys_t[:, keys], preferred_element_type=F32)
            scores[later, :, keys] = part
            top = highest(top, part)
            raised = jnp.exp2((scores[slot, :, keys] - top_here) * EXP2_SCALING).astype(BF16)
            mixed = jnp.dot(raised, values_x[keys, :], preferred_element_type=F32)
            total = mixed if total is None else total + mixed
        tops[later] = row_max(top)
        own = (total[:, :HD] / total[:, HD:]).astype(BF16)
        out_ref[pl.ds(i * per_block, per_block)] = own.reshape(per_block, chunk, HD)
        return carry

    lax.fori_loop(0, query_blocks, body, 0)


def attend_self(qkv, rows):
    sources = qkv.shape[0]
    length = sources * rows
    block_rows, block_keys = 512, 512

    def whole(which):
        return pl.BlockSpec((sources, rows, HD), lambda i: (0, which, 0))

    flat = pl.BlockSpec((sources, rows, HD), lambda i: (0, 0, 0))
    return pl.pallas_call(
        functools.partial(self_attention_kernel, block_rows, block_keys),
        grid=(1,),
        in_specs=[whole(0), whole(1), whole(2)],
        out_specs=flat,
        out_shape=jax.ShapeDtypeStruct((sources, rows, HD), BF16),
        scratch_shapes=[
            pltpu.VMEM((HD, length), BF16),
            pltpu.VMEM((length, 2 * HD), BF16),
            pltpu.VMEM((2, block_rows, length), F32),
            pltpu.VMEM((2, block_rows, HD), F32),
        ],
        compiler_params=kernel_params(),
        cost_estimate=pl.CostEstimate(
            flops=8 * length * length * HD,
            bytes_accessed=8 * length * HD,
            transcendentals=length * length,
        ),
        name="self_attention",
    )(qkv, qkv, qkv)


def arrive_kernel(group, owned, got_ref, out_ref, sum_ref, total):
    rows = out_ref.shape[0]
    for head in range(group):
        out_ref[:, head * HD : (head + 1) * HD] = got_ref[head, 0:rows]

    @pl.when(pl.program_id(0) == 0)
    def _():
        total[...] = jnp.zeros_like(total)

    total[...] += jnp.sum(got_ref[:, rows:].astype(F32), axis=0)
    for chunk in range(total.shape[0] // owned):
        sum_ref[:, chunk * HD : (chunk + 1) * HD] = total[chunk * owned : (chunk + 1) * owned]


def arrived(got, rows, owned):
    heads, total, _ = got.shape
    features = (total - rows) // owned * HD
    group = 8
    return pl.pallas_call(
        functools.partial(arrive_kernel, group, owned),
        grid=(heads // group,),
        in_specs=[pl.BlockSpec((group, total, HD), lambda i: (i, 0, 0))],
        out_specs=[
            pl.BlockSpec((None, rows, group * HD), lambda i: (0, 0, i)),
            pl.BlockSpec((None, owned, features), lambda i: (0, 0, 0)),
        ],
        out_shape=[
            jax.ShapeDtypeStruct((1, rows, heads * HD), BF16),
            jax.ShapeDtypeStruct((1, owned, features), F32),
        ],
        scratch_shapes=[pltpu.VMEM((total - rows, HD), F32)],
        compiler_params=kernel_params(),
        cost_estimate=pl.CostEstimate(
            flops=got.size, bytes_accessed=4 * got.size, transcendentals=0
        ),
        name="arrived",
    )(got)


def local(
    self_q,
    self_k,
    self_v,
    cross_q,
    audio,
    key_weight,
    value_weight,
    intersection,
    counts,
    cotangent,
):
    here = lax.axis_index("seq")
    core = lax.rem(here, 2)
    rows = self_q.shape[1]
    owned, features = audio.shape[1:]

    qkv = self_heads(self_q, self_k, self_v, audio)
    qkv, cross_q, key_weight, value_weight = lax.optimization_barrier(
        (qkv, cross_q, key_weight, value_weight)
    )
    qkv = handed_over(qkv)

    band_first = (here * (owned // AB) - REACH)[None].astype(jnp.int32)
    cross = cross_heads(intersection[0], counts[0], band_first, cross_q, cotangent)
    both = jnp.concatenate([key_weight, value_weight], axis=1)
    proj = gathered_by_doubling(both[None], "fsdp").reshape(-1, 2 * HD)
    place = jnp.stack([core, 1 - core]).astype(jnp.int32) * (features // 2)
    qkv, cross, proj, place = lax.optimization_barrier((qkv, cross, proj, place))

    cross = handed_over(cross)
    mine = qkv[:, 3 * rows :]
    other = from_other_core(mine)
    own_heads = attend_self(qkv, rows)
    sent = cross_attention(place, cross, mine, other, proj, own_heads)
    block_out, audio_grad = arrived(handed_over(sent), rows, owned)
    return (block_out, audio_grad)


def solution(mesh):
    in_specs = (
        P("fsdp", "seq", None),
        P("fsdp", "seq", None),
        P("fsdp", "seq", None),
        P("fsdp", "seq", None),
        P("fsdp", "seq", None),
        P("fsdp", "seq"),
        P("fsdp", "seq"),
        P("fsdp", "seq", None),
        P("fsdp", "seq"),
        P("fsdp", "seq", None),
    )
    out_specs = (P("fsdp", "seq", None), P("fsdp", "seq", None))
    return jax.shard_map(local, mesh=mesh, in_specs=in_specs, out_specs=out_specs, check_vma=False)
```

time: 170 us -> 160 us (0.941)
  blocking collectives: 0 us -> 41.3 us
  waiting for transfers between devices: 64.9 us -> 29.8 us
  starting transfers between devices: 43 us -> 29.8 us
  local copies, waits for them, and re-layouts: 10.2 us -> 5.43 us
  Pallas kernels: 48 us -> 52 us
  other arithmetic: 2.66 us -> 0.23 us
    all_to_all x0 -> x1, blocking collectives: none -> 41.3 us  [handed_over(): return lax.all_to_all(parts, 'seq', split_axis=0, concat_axis=0, tiled=True)]
    all_to_all x4 -> x2, waiting for transfers between devices: 53.6 us -> 22 us  [handed_over(): return lax.all_to_all(parts, 'seq', split_axis=0, concat_axis=0, tiled=True)]
    all_to_all x4 -> x2, starting transfers between devices: 29 us -> 15.8 us  [handed_over(): return lax.all_to_all(parts, 'seq', split_axis=0, concat_axis=0, tiled=True)]
    unnamed x24 -> x12, local copies, waits for them, and re-layouts: 8.83 us -> 4.23 us
    pallas_call x1, Pallas kernels: 2.49 us -> 6.68 us  [self_heads(): pl.pallas_call(functools.partial(self_heads_kernel, group), grid=(heads /...]
    ppermute x1, waiting for transfers between devices: 1.94 us -> 0.01 us  [from_other_core(): return lax.ppermute(block, 'seq', [(i, i ^ 1) for i in range(size)])]
  transfers between devices with their start and end apart: 8 -> 6, of which waited for: 7 -> 4; matrix products, arithmetic and copies ran while one was open for 1% -> 1% of each run, Pallas kernels for 26% -> 23%
where the time goes in v4:
time: 160 us; the launch traced here: 159 us
  Pallas kernels  52 us (32%)
  blocking collectives  41.3 us (26%)
  starting transfers between devices  29.8 us (19%)
  waiting for transfers between devices  29.8 us (19%)
  local copies, waits for them, and re-layouts  5.43 us (3%)
    all_to_all x1, blocking collectives, handed_over(): return lax.all_to_all(parts, 'seq', split_axis=0, concat_axis=0, tiled=True)  41.3 us
    pallas_call x1, Pallas kernels, attend_self(): pl.pallas_call(functools.partial(self_attention_kernel, block_rows, block...  31.9 us
    all_to_all x2, waiting for transfers between devices, handed_over(): return lax.all_to_all(parts, 'seq', split_axis=0, concat_axis=0, tiled=True)  22 us
    all_to_all x2, starting transfers between devices, handed_over(): return lax.all_to_all(parts, 'seq', split_axis=0, concat_axis=0, tiled=True)  15.8 us
    ppermute x3, starting transfers between devices, gathered_by_doubling(): other = lax.ppermute(block, axis, [(i, i ^ step) for i in range(size)])  13.5 us
    ppermute x3, waiting for transfers between devices, gathered_by_doubling(): other = lax.ppermute(block, axis, [(i, i ^ step) for i in range(size)])  7.76 us
    pallas_call x1, Pallas kernels, cross_attention(): pl.pallas_call(functools.partial(cross_kernel, rows), grid=(1,), in_specs...  7.66 us
    pallas_call x1, Pallas kernels, self_heads(): pl.pallas_call(functools.partial(self_heads_kernel, group), grid=(heads /...  6.68 us
  transfers between devices with their start and end apart: 6, of which 4 were waited for; matrix products, arithmetic and copies ran while one was open for 1% of the time, Pallas kernels for 23%

profile of v4, /device:TPU:1, one launch (start us, length us, event | category | flops | bytes accessed | tf_op | source)
XLA Modules:
  0.0 159.2 jit_solution(18343718979942443033)
XLA Ops:
  0.6 6.7 %self_heads.1 = bf16[32,480,128]{2,1,0:T(8,128)(2,1)} custom-call(bf16[1,128,4096]{2,1,0:T(8,128)(2,1)} %q_ref.1, bf16[1,128,4096]{2,1,0:T(8,128)(2,1)} %k_ref.1, bf16[1,128,4096]{2,1,0:T(8,128)(2,1)} %v_ref.1, bf16[1,32,768]{2,1,0:T(8,128)(2,1)} %audio_ref.1), custom_call_target="tpu_custom_call" | custom-call | bytes 7340032 | tf_op jit(solution)/shard_map/self_heads/pallas_call | solution.py:74
  7.3 0.0 copy-start.4
  7.3 0.0 copy-start.5
  7.3 8.8 %all-to-all-start = ((bf16[32,480,128]{2,1,0:T(8,128)(2,1)}), bf16[32,480,128]{2,1,0:T(8,128)(2,1)}, u32[]{:S(2)}, u32[]{:S(2)}) async-start(bf16[32,480,128]{2,1,0:T(8,128)(2,1)} %self_heads.1), calls=%async_computation | async-start | bytes 7864320 | tf_op jit(solution)/shard_map/all_to_all | solution.py:26
  16.1 0.0 copy-done.4
  16.1 0.0 copy-done.5
  16.1 1.7 %collective-permute-start = (bf16[1,96,256]{2,1,0:T(8,128)(2,1)S(1)}, bf16[1,96,256]{2,1,0:T(8,128)(2,1)S(1)}, u32[]{:S(2)}, u32[]{:S(2)}) collective-permute-start(bf16[1,96,256]{2,1,0:T(8,128)(2,1)S(1)} %maximum_bitcast_fusion), channel_id=1, source_target_pairs={{0,1},{1,0},{2,3},{3,2},{4,5},{5,4},{6,7},{7,6},{8,9},{9,8},{10,11... | collective-permute-start | bytes 147464 | tf_op jit(solution)/shard_map/ppermute | solution.py:34
  17.8 1.9 %collective-permute-done = bf16[1,96,256]{2,1,0:T(8,128)(2,1)S(1)} collective-permute-done((bf16[1,96,256]{2,1,0:T(8,128)(2,1)S(1)}, bf16[1,96,256]{2,1,0:T(8,128)(2,1)S(1)}, u32[]{:S(2)}, u32[]{:S(2)}) %collective-permute-start) | collective-permute-done | bytes 49184 | tf_op jit(solution)/shard_map/ppermute | solution.py:34
  19.8 3.1 %collective-permute-start.1 = (bf16[2,96,256]{2,1,0:T(8,128)(2,1)S(1)}, bf16[2,96,256]{2,1,0:T(8,128)(2,1)S(1)}, u32[]{:S(2)}, u32[]{:S(2)}) collective-permute-start(bf16[2,96,256]{2,1,0:T(8,128)(2,1)S(1)} %pad_maximum_fusion.2), channel_id=1, source_target_pairs={{0,2},{1,3},{2,0},{3,1},{4,6},{5,7},{6,4},{7,5},{8,10},{9,11},{10,... | collective-permute-start | bytes 294920 | tf_op jit(solution)/shard_map/ppermute | solution.py:34
  22.9 2.4 %collective-permute-done.1 = bf16[2,96,256]{2,1,0:T(8,128)(2,1)S(1)} collective-permute-done((bf16[2,96,256]{2,1,0:T(8,128)(2,1)S(1)}, bf16[2,96,256]{2,1,0:T(8,128)(2,1)S(1)}, u32[]{:S(2)}, u32[]{:S(2)}) %collective-permute-start.1) | collective-permute-done | bytes 98336 | tf_op jit(solution)/shard_map/ppermute | solution.py:34
  25.3 8.7 %collective-permute-start.2 = (bf16[4,96,256]{2,1,0:T(8,128)(2,1)S(1)}, bf16[4,96,256]{2,1,0:T(8,128)(2,1)S(1)}, u32[]{:S(2)}, u32[]{:S(2)}) collective-permute-start(bf16[4,96,256]{2,1,0:T(8,128)(2,1)S(1)} %pad_maximum_fusion.1), channel_id=1, source_target_pairs={{0,4},{1,5},{2,6},{3,7},{4,0},{5,1},{6,2},{7,3},{8,12},{9,13},{10,... | collective-permute-start | bytes 589832 | tf_op jit(solution)/shard_map/ppermute | solution.py:34
  34.0 4.0 %cross_heads.1 = bf16[32,272,128]{2,1,0:T(8,128)(2,1)} custom-call(s32[2,4]{1,0:T(2,128)} %bitcast.13, s32[2]{0:T(128)} %bitcast.14, s32[1]{0:T(128)} %bitcast.2.first_ref, bf16[1,128,4096]{2,1,0:T(8,128)(2,1)} %q_ref.2, bf16[1,128,4096]{2,1,0:T(8,128)(2,1)} %grad_ref.1), custom_call_target="tpu_custom_call" | custom-call | bytes 4194304 | tf_op jit(solution)/shard_map/cross_heads/pallas_call | solution.py:114
  38.0 0.1 add_multiply_fusion.place_ref
  38.1 3.5 %collective-permute-done.2 = bf16[4,96,256]{2,1,0:T(8,128)(2,1)S(1)} collective-permute-done((bf16[4,96,256]{2,1,0:T(8,128)(2,1)S(1)}, bf16[4,96,256]{2,1,0:T(8,128)(2,1)S(1)}, u32[]{:S(2)}, u32[]{:S(2)}) %collective-permute-start.2) | collective-permute-done | bytes 196640 | tf_op jit(solution)/shard_map/ppermute | solution.py:34
  41.6 22.0 %all-to-all-done.q_ref.k_ref.v_ref = bf16[32,480,128]{2,1,0:T(8,128)(2,1)} async-done(((bf16[32,480,128]{2,1,0:T(8,128)(2,1)}), bf16[32,480,128]{2,1,0:T(8,128)(2,1)}, u32[]{:S(2)}, u32[]{:S(2)}) %all-to-all-start) | async-done | bytes 3932192 | tf_op jit(solution)/shard_map/all_to_all | solution.py:26
  63.7 7.0 %all-to-all-start.1 = ((bf16[32,272,128]{2,1,0:T(8,128)(2,1)}), bf16[32,272,128]{2,1,0:T(8,128)(2,1)S(1)}, u32[]{:S(2)}, u32[]{:S(2)}) async-start(bf16[32,272,128]{2,1,0:T(8,128)(2,1)} %cross_heads.1), calls=%async_computation.1 | async-start | bytes 4456448 | tf_op jit(solution)/shard_map/all_to_all | solution.py:26
  70.7 1.2 slice.3.mine_ref
  71.9 0.4 collective-permute-start.3
  72.3 31.9 %self_attention.1.own_ref = bf16[32,128,128]{2,1,0:T(8,128)(2,1)S(1)} custom-call(bf16[32,480,128]{2,1,0:T(8,128)(2,1)} %all-to-all-done.q_ref.k_ref.v_ref, bf16[32,480,128]{2,1,0:T(8,128)(2,1)} %all-to-all-done.q_ref.k_ref.v_ref, bf16[32,480,128]{2,1,0:T(8,128)(2,1)} %all-to-all-done.q_ref.k_ref.v_ref), custom_call_target="tpu_custom_call" | custom-call | flops 17179869184 | bytes 4194304 | tf_op jit(solution)/shard_map/self_attention/pallas_call | solution.py:338
  104.3 0.0 copy-start
  104.3 1.0 copy-done
  105.2 0.0 collective-permute-done.3.other_ref
  105.2 0.0 copy-start.2
  105.2 0.9 copy-done.2
  106.1 0.0 all-to-all-done.1.got_ref
  106.1 0.0 copy-start.1
  106.1 1.2 copy-done.1
  107.4 0.0 copy-start.3
  107.4 1.1 copy-done.3
  108.5 7.7 %cross_attention.1 = bf16[32,320,128]{2,1,0:T(8,128)(2,1)} custom-call(s32[2]{0:T(128)S(1)} %add_multiply_fusion.place_ref, bf16[32,272,128]{2,1,0:T(8,128)(2,1)S(1)} %all-to-all-done.1.got_ref, bf16[32,96,128]{2,1,0:T(8,128)(2,1)S(1)} %slice.3.mine_ref, bf16[32,96,128]{2,1,0:T(8,128)(2,1)S(1)} %copy-done.3, bf16[768,256]{1,0:T(8,128)(2,1)S(1)} %bitcast.12, ...), custom_call_target="tpu_custom_call" | custom-call | flops 1476395008 | bytes 7864320 | tf_op jit(solution)/shard_map/cross_attention/pallas_call | solution.py:232
  116.2 41.3 %all_to_all.15.got_ref = bf16[32,320,128]{2,1,0:T(8,128)(2,1)S(1)} all-to-all(bf16[32,320,128]{2,1,0:T(8,128)(2,1)} %cross_attention.1), channel_id=1, replica_groups=mesh['seq'=32,'fsdp'=8] {'seq'}, dimensions={0} | all-to-all | bytes 5242880 | tf_op jit(solution)/shard_map/all_to_all | solution.py:26
  157.5 1.7 %arrived.1 = (bf16[1,128,4096]{2,1,0:T(8,128)(2,1)}, f32[1,32,768]{2,1,0:T(8,128)}) custom-call(bf16[32,320,128]{2,1,0:T(8,128)(2,1)S(1)} %all_to_all.15.got_ref), custom_call_target="tpu_custom_call" | custom-call | flops 1310720 | bytes 5242880 | tf_op jit(solution)/shard_map/arrived/pallas_call | solution.py:378
  (7 shorter events, 0.1 us)
Async XLA Ops:
  7.3 8.8 %copy-start.4 = (bf16[96,128]{1,0:T(8,128)(2,1)S(1)}, bf16[96,128]{1,0:T(8,128)(2,1)}, u32[]{:S(2)}) copy-start(bf16[96,128]{1,0:T(8,128)(2,1)} %param.16) | copy-start | bytes 73732
  7.3 8.8 %copy-start.5 = (bf16[96,128]{1,0:T(8,128)(2,1)S(1)}, bf16[96,128]{1,0:T(8,128)(2,1)}, u32[]{:S(2)}) copy-start(bf16[96,128]{1,0:T(8,128)(2,1)} %param.15) | copy-start | bytes 73732
  7.3 56.3 %all-to-all-start = ((bf16[32,480,128]{2,1,0:T(8,128)(2,1)}), bf16[32,480,128]{2,1,0:T(8,128)(2,1)}, u32[]{:S(2)}, u32[]{:S(2)}) async-start(bf16[32,480,128]{2,1,0:T(8,128)(2,1)} %self_heads.1), calls=%async_computation | async-start | bytes 7864320 | tf_op jit(solution)/shard_map/all_to_all | solution.py:26
  16.1 3.6 %collective-permute-start = (bf16[1,96,256]{2,1,0:T(8,128)(2,1)S(1)}, bf16[1,96,256]{2,1,0:T(8,128)(2,1)S(1)}, u32[]{:S(2)}, u32[]{:S(2)}) collective-permute-start(bf16[1,96,256]{2,1,0:T(8,128)(2,1)S(1)} %maximum_bitcast_fusion), channel_id=1, source_target_pairs={{0,1},{1,0},{2,3},{3,2},{4,5},{5,4},{6,7},{7,6},{8,9},{9,8},{10,11... | collective-permute-start | bytes 147464 | tf_op jit(solution)/shard_map/ppermute | solution.py:34
  19.8 5.5 %collective-permute-start.1 = (bf16[2,96,256]{2,1,0:T(8,128)(2,1)S(1)}, bf16[2,96,256]{2,1,0:T(8,128)(2,1)S(1)}, u32[]{:S(2)}, u32[]{:S(2)}) collective-permute-start(bf16[2,96,256]{2,1,0:T(8,128)(2,1)S(1)} %pad_maximum_fusion.2), channel_id=1, source_target_pairs={{0,2},{1,3},{2,0},{3,1},{4,6},{5,7},{6,4},{7,5},{8,10},{9,11},{10,... | collective-permute-start | bytes 294920 | tf_op jit(solution)/shard_map/ppermute | solution.py:34
  25.3 16.3 %collective-permute-start.2 = (bf16[4,96,256]{2,1,0:T(8,128)(2,1)S(1)}, bf16[4,96,256]{2,1,0:T(8,128)(2,1)S(1)}, u32[]{:S(2)}, u32[]{:S(2)}) collective-permute-start(bf16[4,96,256]{2,1,0:T(8,128)(2,1)S(1)} %pad_maximum_fusion.1), channel_id=1, source_target_pairs={{0,4},{1,5},{2,6},{3,7},{4,0},{5,1},{6,2},{7,3},{8,12},{9,13},{10,... | collective-permute-start | bytes 589832 | tf_op jit(solution)/shard_map/ppermute | solution.py:34
  63.7 42.5 %all-to-all-start.1 = ((bf16[32,272,128]{2,1,0:T(8,128)(2,1)}), bf16[32,272,128]{2,1,0:T(8,128)(2,1)S(1)}, u32[]{:S(2)}, u32[]{:S(2)}) async-start(bf16[32,272,128]{2,1,0:T(8,128)(2,1)} %cross_heads.1), calls=%async_computation.1 | async-start | bytes 4456448 | tf_op jit(solution)/shard_map/all_to_all | solution.py:26
  71.9 33.3 %collective-permute-start.3 = (bf16[32,96,128]{2,1,0:T(8,128)(2,1)S(1)}, bf16[32,96,128]{2,1,0:T(8,128)(2,1)S(1)}, u32[]{:S(2)}, u32[]{:S(2)}) collective-permute-start(bf16[32,96,128]{2,1,0:T(8,128)(2,1)S(1)} %slice.3.mine_ref), channel_id=1, source_target_pairs={{0,8},{8,0},{16,24},{24,16},{32,40},{40,32},{48,56},{56,48},{64,72... | collective-permute-start | bytes 2359304 | tf_op jit(solution)/shard_map/ppermute | solution.py:45
  104.3 1.0 copy-start
  105.2 0.9 copy-start.2
  106.1 1.2 copy-start.1
  107.4 1.1 copy-start.3

commit v5 on v4

--- a/solution.py
+++ b/solution.py
@@ -68,7 +68,7 @@
     _, rows, width = q_local.shape
     _, owned, features = audio.shape
     heads = width // HD
-    group = 4
+    group = 8
     total = 3 * rows + owned * (features // HD // 2)
     block = pl.BlockSpec((None, rows, group * HD), lambda i: (0, 0, i))
     return pl.pallas_call(
@@ -125,61 +125,132 @@
     )(window_ids, live_counts, band_first, queries, grads)
 
 
+def project_kernel(
+    audio_first, place_ref, qkv_ref, other_ref, proj_ref, keys_ref, values_ref, audio, sem
+):
+    sources, owned, features = audio.shape
+    chunks = features // HD // 2
+    length = sources * owned
+    edge = REACH * AB
+    copies = []
+    for chunk in range(chunks):
+        for kind, (ref, first) in enumerate(((qkv_ref, audio_first), (other_ref, 0))):
+            lanes = pl.ds(pl.multiple_of(place_ref[kind] + chunk * HD, HD), HD)
+            copies.append(
+                pltpu.make_async_copy(
+                    ref.at[:, pl.ds(first + chunk * owned, owned), :],
+                    audio.at[:, :, lanes],
+                    sem.at[kind, chunk],
+                )
+            )
+            copies[-1].start()
+    tail = keys_ref.shape[0] - edge - length
+    for ref in (keys_ref, values_ref):
+        ref[0:edge] = jnp.zeros((edge, HD), BF16)
+        ref[edge + length :] = jnp.zeros((tail, HD), BF16)
+    for copy in copies:
+        copy.wait()
+    step = 256
+    per = step // owned
+    for i in range(length // step):
+        rows = audio[i * per : (i + 1) * per].reshape(step, features)
+        both = jnp.dot(rows, proj_ref[...], preferred_element_type=F32).astype(BF16)
+        keys_ref[edge + i * step : edge + (i + 1) * step] = both[:, :HD]
+        values_ref[edge + i * step : edge + (i + 1) * step] = both[:, HD:]
+
+
+def projected(place, qkv, audio_first, other, proj):
+    sources, audio_rows, _ = other.shape
+    features = proj.shape[0]
+    owned = 2 * AB
+    length = sources * owned
+    padded = length + HD - owned
+    anywhere = pl.BlockSpec(memory_space=pl.ANY)
+    flat = pl.BlockSpec((padded, HD), lambda i: (0, 0))
+    return pl.pallas_call(
+        functools.partial(project_kernel, audio_first),
+        grid=(1,),
+        in_specs=[
+            pl.BlockSpec(memory_space=pltpu.SMEM),
+            anywhere,
+            anywhere,
+            pl.BlockSpec((features, 2 * HD), lambda i: (0, 0)),
+        ],
+        out_specs=[flat, flat],
+        out_shape=[jax.ShapeDtypeStruct((padded, HD), BF16)] * 2,
+        scratch_shapes=[
+            pltpu.VMEM((sources, owned, features), BF16),
+            pltpu.SemaphoreType.DMA((2, features // HD // 2)),
+        ],
+        compiler_params=kernel_params(16),
+        cost_estimate=pl.CostEstimate(
+            flops=4 * length * features * HD,
+            bytes_accessed=2 * (length * features + proj.size + 2 * padded * HD),
+            transcendentals=0,
+        ),
+        name="projected",
+    )(place, qkv, other, proj)
+
+
 def cross_kernel(
     rows,
     place_ref,
-    got_ref,
-    mine_ref,
-    other_ref,
+    got_hbm,
+    own_hbm,
+    keys_ref,
+    values_ref,
     proj_ref,
-    own_ref,
-    out_ref,
-    audio,
-    keys,
-    values,
+    sent_hbm,
+    away_hbm,
+    got,
+    own,
+    out,
+    terms,
+    away,
     d_keys,
     d_values,
+    in_sem,
+    out_sem,
 ):
-    sources = got_ref.shape[0]
+    sources = got.shape[0]
     owned = AB * 2
-    chunks = other_ref.shape[1] // owned
+    features = proj_ref.shape[0]
+    half = features // 2
+    chunks = half // HD
     length = sources * owned
     edge = REACH * AB
     band = HD
     at_once = 8
-
-    for chunk in range(chunks):
-        own_lanes = pl.ds(pl.multiple_of(place_ref[0] + chunk * HD, HD), HD)
-        other_lanes = pl.ds(pl.multiple_of(place_ref[1] + chunk * HD, HD), HD)
-        chunk_rows = slice(chunk * owned, (chunk + 1) * owned)
-        audio[:, own_lanes] = mine_ref[:, chunk_rows].reshape(length, HD)
-        audio[:, other_lanes] = other_ref[:, chunk_rows].reshape(length, HD)
-
-    keys[...] = jnp.zeros_like(keys)
-    values[...] = jnp.zeros_like(values)
+    blocks = sources // at_once
+
+    fetched = []
+    for block in range(blocks):
+        here = pl.ds(block * at_once, at_once)
+        pair = (
+            pltpu.make_async_copy(got_hbm.at[here], got.at[here], in_sem.at[0, block]),
+            pltpu.make_async_copy(own_hbm.at[here], own.at[here], in_sem.at[1, block]),
+        )
+        for copy in pair:
+            copy.start()
+        fetched.append(pair)
     d_keys[...] = jnp.zeros_like(d_keys)
     d_values[...] = jnp.zeros_like(d_values)
-    step = 256
-    for i in range(length // step):
-        both = jnp.dot(
-            audio[i * step : (i + 1) * step], proj_ref[...], preferred_element_type=F32
-        ).astype(BF16)
-        keys[edge + i * step : edge + (i + 1) * step] = both[:, :HD]
-        values[edge + i * step : edge + (i + 1) * step] = both[:, HD:]
-
-    def some(block, carry):
+
+    stored = []
+    for block in range(blocks):
+        for copy in fetched[block]:
+            copy.wait()
         sources_here = [block * at_once + i for i in range(at_once)]
-        bands = [pl.ds(pl.multiple_of(t * owned, owned), band) for t in sources_here]
-        k = [keys[b] for b in bands]
-        v = [values[b] for b in bands]
-        scores = [contract(got_ref[t, 0:rows], k[i], 1, 1) for i, t in enumerate(sources_here)]
+        bands = [slice(t * owned, t * owned + band) for t in sources_here]
+        k = [keys_ref[b] for b in bands]
+        v = [values_ref[b] for b in bands]
+        scores = [contract(got[t, 0:rows], k[i], 1, 1) for i, t in enumerate(sources_here)]
         d_probs = [
-            contract(got_ref[t, rows : 2 * rows], v[i], 1, 1)
-            for i, t in enumerate(sources_here)
+            contract(got[t, rows : 2 * rows], v[i], 1, 1) for i, t in enumerate(sources_here)
         ]
         weights = []
         for i, t in enumerate(sources_here):
-            masks = got_ref[t, 2 * rows :].astype(F32)
+            masks = got[t, 2 * rows :].astype(F32)
             live = jnp.concatenate(
                 [jnp.broadcast_to(masks[f : f + 1], (rows // 2, band)) for f in range(2)], axis=0
             )
@@ -195,73 +266,123 @@
             d_scores.append((weighed - weights[i] * inner).astype(BF16))
         for i, t in enumerate(sources_here):
             mixed = jnp.dot(weights_b[i], v[i], preferred_element_type=F32)
-            out_ref[t, 0:rows] = (own_ref[t].astype(F32) + mixed).astype(BF16)
+            out[t] = (own[t].astype(F32) + mixed).astype(BF16)
         for i, t in enumerate(sources_here):
-            d_values[bands[i]] += contract(weights_b[i], got_ref[t, rows : 2 * rows], 0, 0)
-            d_keys[bands[i]] += contract(d_scores[i], got_ref[t, 0:rows], 0, 0)
-        return carry
-
-    lax.fori_loop(0, sources // at_once, some, 0)
-
-    for i in range(length // step):
-        here = slice(edge + i * step, edge + (i + 1) * step)
+            d_values[bands[i]] += contract(weights_b[i], got[t, rows : 2 * rows], 0, 0)
+            d_keys[bands[i]] += contract(d_scores[i], got[t, 0:rows], 0, 0)
+        here = pl.ds(block * at_once, at_once)
+        stored.append(
+            pltpu.make_async_copy(
+                out.at[here], sent_hbm.at[here, pl.ds(0, rows), :], out_sem.at[0, block]
+            )
+        )
+        stored[-1].start()
+
+    own_proj = proj_ref[pl.ds(pl.multiple_of(place_ref[0], HD), half)]
+    other_proj = proj_ref[pl.ds(pl.multiple_of(place_ref[1], HD), half)]
+    step = length // blocks
+    per = step // owned
+    for block in range(blocks):
+        rows_here = slice(edge + block * step, edge + (block + 1) * step)
         d_both = jnp.concatenate(
-            [(d_keys[here] * SCALING).astype(BF16), d_values[here].astype(BF16)], axis=1
+            [(d_keys[rows_here] * SCALING).astype(BF16), d_values[rows_here].astype(BF16)], axis=1
         )
-        term = contract(d_both, proj_ref[...], 1, 1).astype(BF16)
-        per = step // owned
-        for chunk in range(2 * chunks):
-            first = rows + chunk * owned
-            out_ref[i * per : (i + 1) * per, first : first + owned] = term[
-                :, chunk * HD : (chunk + 1) * HD
-            ].reshape(per, owned, HD)
-
-
-def cross_attention(place, got, mine, other, proj, own_heads):
+        for buffer, part in ((away, other_proj), (terms, own_proj)):
+            term = contract(d_both, part, 1, 1).astype(BF16)
+            for chunk in range(chunks):
+                buffer[
+                    block * per : (block + 1) * per, chunk * owned : (chunk + 1) * owned
+                ] = term[:, chunk * HD : (chunk + 1) * HD].reshape(per, owned, HD)
+        here = pl.ds(block * per, per)
+        stored += [
+            pltpu.make_async_copy(away.at[here], away_hbm.at[here], out_sem.at[1, block]),
+            pltpu.make_async_copy(
+                terms.at[here],
+                sent_hbm.at[here, pl.ds(rows, chunks * owned), :],
+                out_sem.at[2, block],
+            ),
+        ]
+        for copy in stored[-2:]:
+            copy.start()
+    for copy in stored:
+        copy.wait()
+
+
+def cross_attention(place, got, own_heads, keys, values, proj):
     sources, rows, _ = own_heads.shape
     total = got.shape[1]
-    audio_rows = mine.shape[1]
     features = proj.shape[0]
     owned = 2 * AB
-    length = sources * owned
-    padded = length + HD - owned
-
-    def whole(*shape):
-        return pl.BlockSpec(shape, lambda i: (0,) * len(shape))
-
+    padded = keys.shape[0]
+    term_rows = features // 2 // HD * owned
+    anywhere = pl.BlockSpec(memory_space=pl.ANY)
+    flat = pl.BlockSpec((padded, HD), lambda i: (0, 0))
     return pl.pallas_call(
         functools.partial(cross_kernel, rows),
         grid=(1,),
         in_specs=[
             pl.BlockSpec(memory_space=pltpu.SMEM),
-            whole(sources, total, HD),
-            whole(sources, audio_rows, HD),
-            whole(sources, audio_rows, HD),
-            whole(features, 2 * HD),
-            whole(sources, rows, HD),
-        ],
-        out_specs=whole(sources, rows + 2 * audio_rows, HD),
-        out_shape=jax.ShapeDtypeStruct((sources, rows + 2 * audio_rows, HD), BF16),
+            anywhere,
+            anywhere,
+            flat,
+            flat,
+            pl.BlockSpec((features, 2 * HD), lambda i: (0, 0)),
+        ],
+        out_specs=[anywhere, anywhere],
+        out_shape=[
+            jax.ShapeDtypeStruct((sources, rows + term_rows, HD), BF16),
+            jax.ShapeDtypeStruct((sources, term_rows, HD), BF16),
+        ],
         scratch_shapes=[
-            pltpu.VMEM((length, features), BF16),
-            pltpu.VMEM((padded, HD), BF16),
-            pltpu.VMEM((padded, HD), BF16),
+            pltpu.VMEM((sources, total, HD), BF16),
+            pltpu.VMEM((sources, rows, HD), BF16),
+            pltpu.VMEM((sources, rows, HD), BF16),
+            pltpu.VMEM((sources, term_rows, HD), BF16),
+            pltpu.VMEM((sources, term_rows, HD), BF16),
             pltpu.VMEM((padded, HD), F32),
             pltpu.VMEM((padded, HD), F32),
-        ],
-        compiler_params=kernel_params(),
-        cost_estimate=pl.CostEstimate(
-            flops=8 * length * features * HD + 10 * sources * rows * HD * HD,
-            bytes_accessed=2 * (got.size + 4 * mine.size + proj.size + 2 * own_heads.size),
+            pltpu.SemaphoreType.DMA((2, sources // 8)),
+            pltpu.SemaphoreType.DMA((3, sources // 8)),
+        ],
+        compiler_params=kernel_params(60),
+        cost_estimate=pl.CostEstimate(
+            flops=4 * sources * owned * features * HD + 10 * sources * rows * HD * HD,
+            bytes_accessed=2 * (got.size + proj.size + 4 * own_heads.size),
             transcendentals=sources * rows * HD,
         ),
         name="cross_attention",
-    )(place, got, mine, other, proj, own_heads)
+    )(place, got, own_heads, keys, values, proj)
+
+
+def pair_kernel(sent_ref, came_ref, out_ref):
+    out_ref[...] = (sent_ref[...].astype(F32) + came_ref[...].astype(F32)).astype(BF16)
+
+
+def pair_added(sent, came):
+    sources, term_rows, _ = came.shape
+    total = sent.shape[1]
+    width = 32
+    ahead = (total - term_rows) // width
+    block = pl.BlockSpec((sources, width, HD), lambda i: (0, ahead + i, 0))
+    return pl.pallas_call(
+        pair_kernel,
+        grid=(term_rows // width,),
+        in_specs=[block, pl.BlockSpec((sources, width, HD), lambda i: (0, i, 0))],
+        out_specs=block,
+        out_shape=jax.ShapeDtypeStruct(sent.shape, BF16),
+        input_output_aliases={0: 0},
+        compiler_params=kernel_params(8),
+        cost_estimate=pl.CostEstimate(
+            flops=came.size, bytes_accessed=6 * came.size, transcendentals=0
+        ),
+        name="pair_added",
+    )(sent, came)
 
 
 def self_attention_kernel(
     block_rows,
     block_keys,
+    unrolled,
     q_ref,
     k_ref,
     v_ref,
@@ -303,10 +424,8 @@
         top = highest(top, part)
     tops[0] = row_max(top)
 
-    def body(i, carry):
-        slot = lax.rem(i, 2)
-        later = 1 - slot
-        queries = queries_of(jnp.minimum(i + 1, query_blocks - 1))
+    def one(block, slot, later):
+        queries = queries_of(jnp.minimum(block + 1, query_blocks - 1))
         top_here = tops[slot][:, :1]
         top = None
         total = None
@@ -320,23 +439,27 @@
             total = mixed if total is None else total + mixed
         tops[later] = row_max(top)
         own = (total[:, :HD] / total[:, HD:]).astype(BF16)
-        out_ref[pl.ds(i * per_block, per_block)] = own.reshape(per_block, chunk, HD)
+        out_ref[pl.ds(block * per_block, per_block)] = own.reshape(per_block, chunk, HD)
+
+    def body(i, carry):
+        for u in range(unrolled):
+            one(i * unrolled + u, u % 2, 1 - u % 2)
         return carry
 
-    lax.fori_loop(0, query_blocks, body, 0)
+    lax.fori_loop(0, query_blocks // unrolled, body, 0)
 
 
 def attend_self(qkv, rows):
     sources = qkv.shape[0]
     length = sources * rows
-    block_rows, block_keys = 512, 512
+    block_rows, block_keys, unrolled = 512, 512, 4
 
     def whole(which):
         return pl.BlockSpec((sources, rows, HD), lambda i: (0, which, 0))
 
     flat = pl.BlockSpec((sources, rows, HD), lambda i: (0, 0, 0))
     return pl.pallas_call(
-        functools.partial(self_attention_kernel, block_rows, block_keys),
+        functools.partial(self_attention_kernel, block_rows, block_keys, unrolled),
         grid=(1,),
         in_specs=[whole(0), whole(1), whole(2)],
         out_specs=flat,
@@ -347,7 +470,7 @@
             pltpu.VMEM((2, block_rows, length), F32),
             pltpu.VMEM((2, block_rows, HD), F32),
         ],
-        compiler_params=kernel_params(),
+        compiler_params=kernel_params(60),
         cost_estimate=pl.CostEstimate(
             flops=8 * length * length * HD,
             bytes_accessed=8 * length * HD,
@@ -366,14 +489,24 @@
     def _():
         total[...] = jnp.zeros_like(total)
 
-    total[...] += jnp.sum(got_ref[:, rows:].astype(F32), axis=0)
-    for chunk in range(total.shape[0] // owned):
-        sum_ref[:, chunk * HD : (chunk + 1) * HD] = total[chunk * owned : (chunk + 1) * owned]
+    chunks = total.shape[1] // owned
+    for core in range(2):
+        part = total[core]
+        for head in range(core, group, 2):
+            part = part + got_ref[head, rows:].astype(F32)
+        total[core] = part
+
+    @pl.when(pl.program_id(0) == pl.num_programs(0) - 1)
+    def _():
+        for core in range(2):
+            for chunk in range(chunks):
+                lane = (core * chunks + chunk) * HD
+                sum_ref[:, lane : lane + HD] = total[core, chunk * owned : (chunk + 1) * owned]
 
 
 def arrived(got, rows, owned):
     heads, total, _ = got.shape
-    features = (total - rows) // owned * HD
+    features = 2 * (total - rows) // owned * HD
     group = 8
     return pl.pallas_call(
         functools.partial(arrive_kernel, group, owned),
@@ -387,8 +520,8 @@
             jax.ShapeDtypeStruct((1, rows, heads * HD), BF16),
             jax.ShapeDtypeStruct((1, owned, features), F32),
         ],
-        scratch_shapes=[pltpu.VMEM((total - rows, HD), F32)],
-        compiler_params=kernel_params(),
+        scratch_shapes=[pltpu.VMEM((2, total - rows, HD), F32)],
+        compiler_params=kernel_params(16),
         cost_estimate=pl.CostEstimate(
             flops=got.size, bytes_accessed=4 * got.size, transcendentals=0
         ),
@@ -427,10 +560,11 @@
     qkv, cross, proj, place = lax.optimization_barrier((qkv, cross, proj, place))
 
     cross = handed_over(cross)
-    mine = qkv[:, 3 * rows :]
-    other = from_other_core(mine)
+    other = from_other_core(qkv[:, 3 * rows :])
     own_heads = attend_self(qkv, rows)
-    sent = cross_attention(place, cross, mine, other, proj, own_heads)
+    keys, values = projected(place, qkv, 3 * rows, other, proj)
+    sent, away = cross_attention(place, cross, own_heads, keys, values, proj)
+    sent = pair_added(sent, from_other_core(away))
     block_out, audio_grad = arrived(handed_over(sent), rows, owned)
     return (block_out, audio_grad)
 

time: 160 us -> 147 us (0.919)
  blocking collectives: 41.3 us -> 30.8 us
  Pallas kernels: 52 us -> 44.5 us
  starting transfers between devices: 29.8 us -> 32 us
  waiting for transfers between devices: 29.8 us -> 31.9 us
    all_to_all x1, blocking collectives: 41.3 us -> 30.8 us  [handed_over(): return lax.all_to_all(parts, 'seq', split_axis=0, concat_axis=0, tiled=True)]
    pallas_call x1, Pallas kernels: 31.9 us -> 23.5 us  [attend_self(): pl.pallas_call(functools.partial(self_attention_kernel, block_rows, block...]
    pallas_call x0 -> x2, Pallas kernels: none -> 2.72 us  [the longest x1 2.31 us: projected(): pl.pallas_call(functools.partial(project_kernel, audio_first), grid=(1,),...]
    ppermute x1 -> x2, starting transfers between devices: 0.44 us -> 2.61 us  [from_other_core(): return lax.ppermute(block, 'seq', [(i, i ^ 1) for i in range(size)])]
    ppermute x1 -> x2, waiting for transfers between devices: 0.01 us -> 2.13 us  [from_other_core(): return lax.ppermute(block, 'seq', [(i, i ^ 1) for i in range(size)])]
    pallas_call x1, Pallas kernels: 6.68 us -> 4.58 us  [self_heads(): pl.pallas_call(functools.partial(self_heads_kernel, group), grid=(heads /...]
    unnamed x12 -> x16, local copies, waits for them, and re-layouts: 4.23 us -> 4.32 us
  transfers between devices with their start and end apart: 6 -> 7, of which waited for: 4 -> 5; matrix products, arithmetic and copies ran while one was open for 1% -> 2% of each run, Pallas kernels for 23% -> 20%
where the time goes in v5:
time: 147 us
  Pallas kernels  44.5 us (30%)
  starting transfers between devices  32 us (22%)
  waiting for transfers between devices  31.9 us (22%)
  blocking collectives  30.8 us (21%)
  local copies, waits for them, and re-layouts  6.4 us (4%)
    all_to_all x1, blocking collectives, handed_over(): return lax.all_to_all(parts, 'seq', split_axis=0, concat_axis=0, tiled=True)  30.8 us
    pallas_call x1, Pallas kernels, attend_self(): pl.pallas_call(functools.partial(self_attention_kernel, block_rows, block...  23.5 us
    all_to_all x2, waiting for transfers between devices, handed_over(): return lax.all_to_all(parts, 'seq', split_axis=0, concat_axis=0, tiled=True)  22 us
    all_to_all x2, starting transfers between devices, handed_over(): return lax.all_to_all(parts, 'seq', split_axis=0, concat_axis=0, tiled=True)  15.8 us
    ppermute x3, starting transfers between devices, gathered_by_doubling(): other = lax.ppermute(block, axis, [(i, i ^ step) for i in range(size)])  13.5 us
    pallas_call x1, Pallas kernels, cross_attention(): pl.pallas_call(functools.partial(cross_kernel, rows), grid=(1,), in_specs...  7.96 us
    ppermute x3, waiting for transfers between devices, gathered_by_doubling(): other = lax.ppermute(block, axis, [(i, i ^ step) for i in range(size)])  7.76 us
    pallas_call x1, Pallas kernels, self_heads(): pl.pallas_call(functools.partial(self_heads_kernel, group), grid=(heads /...  4.58 us
  transfers between devices with their start and end apart: 7, of which 5 were waited for; matrix products, arithmetic and copies ran while one was open for 2% of the time, Pallas kernels for 20%

profile of v5, /device:TPU:1, one launch (start us, length us, event | category | flops | bytes accessed | tf_op | source)
XLA Modules:
  0.0 146.5 jit_solution(2648451426777428924)
XLA Ops:
  0.6 4.6 %self_heads.1 = bf16[32,480,128]{2,1,0:T(8,128)(2,1)} custom-call(bf16[1,128,4096]{2,1,0:T(8,128)(2,1)} %q_ref.1, bf16[1,128,4096]{2,1,0:T(8,128)(2,1)} %k_ref.1, bf16[1,128,4096]{2,1,0:T(8,128)(2,1)} %v_ref.1, bf16[1,32,768]{2,1,0:T(8,128)(2,1)} %audio_ref.1), custom_call_target="tpu_custom_call" | custom-call | bytes 7340032 | tf_op jit(solution)/shard_map/self_heads/pallas_call | solution.py:74
  5.2 8.8 %all-to-all-start = ((bf16[32,480,128]{2,1,0:T(8,128)(2,1)}), bf16[32,480,128]{2,1,0:T(8,128)(2,1)}, u32[]{:S(2)}, u32[]{:S(2)}) async-start(bf16[32,480,128]{2,1,0:T(8,128)(2,1)} %self_heads.1), calls=%async_computation | async-start | bytes 7864320 | tf_op jit(solution)/shard_map/all_to_all | solution.py:26
  14.0 0.0 copy-done.6
  14.0 0.0 copy-done.7
  14.0 1.7 %collective-permute-start = (bf16[1,96,256]{2,1,0:T(8,128)(2,1)S(1)}, bf16[1,96,256]{2,1,0:T(8,128)(2,1)S(1)}, u32[]{:S(2)}, u32[]{:S(2)}) collective-permute-start(bf16[1,96,256]{2,1,0:T(8,128)(2,1)S(1)} %maximum_bitcast_fusion), channel_id=1, source_target_pairs={{0,1},{1,0},{2,3},{3,2},{4,5},{5,4},{6,7},{7,6},{8,9},{9,8},{10,11... | collective-permute-start | bytes 147464 | tf_op jit(solution)/shard_map/ppermute | solution.py:34
  15.8 1.9 %collective-permute-done = bf16[1,96,256]{2,1,0:T(8,128)(2,1)S(1)} collective-permute-done((bf16[1,96,256]{2,1,0:T(8,128)(2,1)S(1)}, bf16[1,96,256]{2,1,0:T(8,128)(2,1)S(1)}, u32[]{:S(2)}, u32[]{:S(2)}) %collective-permute-start) | collective-permute-done | bytes 49184 | tf_op jit(solution)/shard_map/ppermute | solution.py:34
  17.7 3.1 %collective-permute-start.1 = (bf16[2,96,256]{2,1,0:T(8,128)(2,1)S(1)}, bf16[2,96,256]{2,1,0:T(8,128)(2,1)S(1)}, u32[]{:S(2)}, u32[]{:S(2)}) collective-permute-start(bf16[2,96,256]{2,1,0:T(8,128)(2,1)S(1)} %pad_maximum_fusion.2), channel_id=1, source_target_pairs={{0,2},{1,3},{2,0},{3,1},{4,6},{5,7},{6,4},{7,5},{8,10},{9,11},{10,... | collective-permute-start | bytes 294920 | tf_op jit(solution)/shard_map/ppermute | solution.py:34
  20.8 2.4 %collective-permute-done.1 = bf16[2,96,256]{2,1,0:T(8,128)(2,1)S(1)} collective-permute-done((bf16[2,96,256]{2,1,0:T(8,128)(2,1)S(1)}, bf16[2,96,256]{2,1,0:T(8,128)(2,1)S(1)}, u32[]{:S(2)}, u32[]{:S(2)}) %collective-permute-start.1) | collective-permute-done | bytes 98336 | tf_op jit(solution)/shard_map/ppermute | solution.py:34
  23.2 8.7 %collective-permute-start.2 = (bf16[4,96,256]{2,1,0:T(8,128)(2,1)S(1)}, bf16[4,96,256]{2,1,0:T(8,128)(2,1)S(1)}, u32[]{:S(2)}, u32[]{:S(2)}) collective-permute-start(bf16[4,96,256]{2,1,0:T(8,128)(2,1)S(1)} %pad_maximum_fusion.1), channel_id=1, source_target_pairs={{0,4},{1,5},{2,6},{3,7},{4,0},{5,1},{6,2},{7,3},{8,12},{9,13},{10,... | collective-permute-start | bytes 589832 | tf_op jit(solution)/shard_map/ppermute | solution.py:34
  31.9 4.0 %cross_heads.1 = bf16[32,272,128]{2,1,0:T(8,128)(2,1)} custom-call(s32[2,4]{1,0:T(2,128)} %bitcast.14, s32[2]{0:T(128)} %bitcast.15, s32[1]{0:T(128)} %bitcast.2.first_ref, bf16[1,128,4096]{2,1,0:T(8,128)(2,1)} %q_ref.2, bf16[1,128,4096]{2,1,0:T(8,128)(2,1)} %grad_ref.1), custom_call_target="tpu_custom_call" | custom-call | bytes 4194304 | tf_op jit(solution)/shard_map/cross_heads/pallas_call | solution.py:114
  35.9 0.1 add_multiply_fusion.place_ref
  36.0 3.5 %collective-permute-done.2 = bf16[4,96,256]{2,1,0:T(8,128)(2,1)S(1)} collective-permute-done((bf16[4,96,256]{2,1,0:T(8,128)(2,1)S(1)}, bf16[4,96,256]{2,1,0:T(8,128)(2,1)S(1)}, u32[]{:S(2)}, u32[]{:S(2)}) %collective-permute-start.2) | collective-permute-done | bytes 196640 | tf_op jit(solution)/shard_map/ppermute | solution.py:34
  39.5 0.0 copy-start.1
  39.6 22.0 %all-to-all-done.q_ref.k_ref.v_ref.qkv_ref = bf16[32,480,128]{2,1,0:T(8,128)(2,1)} async-done(((bf16[32,480,128]{2,1,0:T(8,128)(2,1)}), bf16[32,480,128]{2,1,0:T(8,128)(2,1)}, u32[]{:S(2)}, u32[]{:S(2)}) %all-to-all-start) | async-done | bytes 3932192 | tf_op jit(solution)/shard_map/all_to_all | solution.py:26
  61.6 7.0 %all-to-all-start.1 = ((bf16[32,272,128]{2,1,0:T(8,128)(2,1)}), bf16[32,272,128]{2,1,0:T(8,128)(2,1)S(1)}, u32[]{:S(2)}, u32[]{:S(2)}) async-start(bf16[32,272,128]{2,1,0:T(8,128)(2,1)} %cross_heads.1), calls=%async_computation.1 | async-start | bytes 4456448 | tf_op jit(solution)/shard_map/all_to_all | solution.py:26
  68.6 2.1 %slice.3 = bf16[32,96,128]{2,1,0:T(8,128)(2,1)} slice(bf16[32,480,128]{2,1,0:T(8,128)(2,1)} %all-to-all-done.q_ref.k_ref.v_ref.qkv_ref), slice={[0:32], [384:480], [0:128]} | slice | bytes 1572864 | tf_op jit(solution)/shard_map/slice | solution.py:563
  70.7 0.3 collective-permute-start.3
  71.0 23.5 %self_attention.1.own_hbm = bf16[32,128,128]{2,1,0:T(8,128)(2,1)} custom-call(bf16[32,480,128]{2,1,0:T(8,128)(2,1)} %all-to-all-done.q_ref.k_ref.v_ref.qkv_ref, bf16[32,480,128]{2,1,0:T(8,128)(2,1)} %all-to-all-done.q_ref.k_ref.v_ref.qkv_ref, bf16[32,480,128]{2,1,0:T(8,128)(2,1)} %all-to-all-done.q_ref.k_ref.v_ref.qkv_ref), custom_call_target="tpu_custom_call" | custom-call | flops 17179869184 | bytes 4194304 | tf_op jit(solution)/shard_map/self_attention/pallas_call | solution.py:461
  94.6 0.0 collective-permute-done.3.other_ref
  94.6 2.3 %projected.1 = (bf16[1120,128]{1,0:T(8,128)(2,1)S(1)}, bf16[1120,128]{1,0:T(8,128)(2,1)S(1)}) custom-call(s32[2]{0:T(128)S(1)} %add_multiply_fusion.place_ref, bf16[32,480,128]{2,1,0:T(8,128)(2,1)} %all-to-all-done.q_ref.k_ref.v_ref.qkv_ref, bf16[32,96,128]{2,1,0:T(8,128)(2,1)S(1)} %collective-permute-done.3.other_ref, bf16[768,256]{1,0:T(8,128)(2,1)S(1)} %bitcast.12), custom_call_target="tpu_custom_call" | custom-call | flops 402653184 | bytes 2539520 | tf_op jit(solution)/shard_map/projected/pallas_call | solution.py:170
  96.9 0.0 copy-start.2
  96.9 0.7 copy-done.2
  97.6 0.7 copy-done.3
  98.3 0.0 all-to-all-done.1.got_hbm
  98.3 1.4 copy-done.5
  99.7 8.0 %cross_attention.1 = (bf16[32,224,128]{2,1,0:T(8,128)(2,1)}, bf16[32,96,128]{2,1,0:T(8,128)(2,1)}) custom-call(s32[2]{0:T(128)} %copy-done.4, bf16[32,272,128]{2,1,0:T(8,128)(2,1)} %copy-done.5, bf16[32,128,128]{2,1,0:T(8,128)(2,1)} %self_attention.1.own_hbm, bf16[1120,128]{1,0:T(8,128)(2,1)} %copy-done.2, bf16[1120,128]{1,0:T(8,128)(2,1)} %copy-done.3, ...), custom_call_target="tpu_custom_call" | custom-call | flops 1073741824 | bytes 6815744 | tf_op jit(solution)/shard_map/cross_attention/pallas_call | solution.py:320
  107.7 2.3 %collective-permute-start.4 = (bf16[32,96,128]{2,1,0:T(8,128)(2,1)}, bf16[32,96,128]{2,1,0:T(8,128)(2,1)S(1)}, u32[]{:S(2)}, u32[]{:S(2)}) collective-permute-start(bf16[32,96,128]{2,1,0:T(8,128)(2,1)} %get-tuple-element.25), channel_id=1, source_target_pairs={{0,8},{8,0},{16,24},{24,16},{32,40},{40,32},{48,56},{56,48},{64,72... | collective-permute-start | bytes 2359304 | tf_op jit(solution)/shard_map/ppermute | solution.py:45
  109.9 2.1 %collective-permute-done.4.came_ref = bf16[32,96,128]{2,1,0:T(8,128)(2,1)S(1)} collective-permute-done((bf16[32,96,128]{2,1,0:T(8,128)(2,1)}, bf16[32,96,128]{2,1,0:T(8,128)(2,1)S(1)}, u32[]{:S(2)}, u32[]{:S(2)}) %collective-permute-start.4) | collective-permute-done | bytes 786464 | tf_op jit(solution)/shard_map/ppermute | solution.py:45
  112.1 1.5 %copy-done = bf16[32,224,128]{2,1,0:T(8,128)(2,1)S(1)} copy-done((bf16[32,224,128]{2,1,0:T(8,128)(2,1)S(1)}, bf16[32,224,128]{2,1,0:T(8,128)(2,1)}, u32[]{:S(2)}) %copy-start) | copy-done | bytes 1835032
  113.6 0.4 pair_added.1
  114.0 30.8 %all_to_all.15.got_ref = bf16[32,224,128]{2,1,0:T(8,128)(2,1)S(1)} all-to-all(bf16[32,224,128]{2,1,0:T(8,128)(2,1)S(1)} %pair_added.1), channel_id=1, replica_groups=mesh['seq'=32,'fsdp'=8] {'seq'}, dimensions={0} | all-to-all | bytes 3670016 | tf_op jit(solution)/shard_map/all_to_all | solution.py:26
  144.8 1.8 %arrived.1 = (bf16[1,128,4096]{2,1,0:T(8,128)(2,1)}, f32[1,32,768]{2,1,0:T(8,128)}) custom-call(bf16[32,224,128]{2,1,0:T(8,128)(2,1)S(1)} %all_to_all.15.got_ref), custom_call_target="tpu_custom_call" | custom-call | flops 917504 | bytes 3670016 | tf_op jit(solution)/shard_map/arrived/pallas_call | solution.py:511
  (15 shorter events, 0.2 us)
Async XLA Ops:
  5.2 8.8 %copy-start.6 = (bf16[96,128]{1,0:T(8,128)(2,1)S(1)}, bf16[96,128]{1,0:T(8,128)(2,1)}, u32[]{:S(2)}) copy-start(bf16[96,128]{1,0:T(8,128)(2,1)} %param.16) | copy-start | bytes 73732
  5.2 8.8 %copy-start.7 = (bf16[96,128]{1,0:T(8,128)(2,1)S(1)}, bf16[96,128]{1,0:T(8,128)(2,1)}, u32[]{:S(2)}) copy-start(bf16[96,128]{1,0:T(8,128)(2,1)} %param.15) | copy-start | bytes 73732
  5.2 56.3 %all-to-all-start = ((bf16[32,480,128]{2,1,0:T(8,128)(2,1)}), bf16[32,480,128]{2,1,0:T(8,128)(2,1)}, u32[]{:S(2)}, u32[]{:S(2)}) async-start(bf16[32,480,128]{2,1,0:T(8,128)(2,1)} %self_heads.1), calls=%async_computation | async-start | bytes 7864320 | tf_op jit(solution)/shard_map/all_to_all | solution.py:26
  14.0 3.6 %collective-permute-start = (bf16[1,96,256]{2,1,0:T(8,128)(2,1)S(1)}, bf16[1,96,256]{2,1,0:T(8,128)(2,1)S(1)}, u32[]{:S(2)}, u32[]{:S(2)}) collective-permute-start(bf16[1,96,256]{2,1,0:T(8,128)(2,1)S(1)} %maximum_bitcast_fusion), channel_id=1, source_target_pairs={{0,1},{1,0},{2,3},{3,2},{4,5},{5,4},{6,7},{7,6},{8,9},{9,8},{10,11... | collective-permute-start | bytes 147464 | tf_op jit(solution)/shard_map/ppermute | solution.py:34
  17.7 5.5 %collective-permute-start.1 = (bf16[2,96,256]{2,1,0:T(8,128)(2,1)S(1)}, bf16[2,96,256]{2,1,0:T(8,128)(2,1)S(1)}, u32[]{:S(2)}, u32[]{:S(2)}) collective-permute-start(bf16[2,96,256]{2,1,0:T(8,128)(2,1)S(1)} %pad_maximum_fusion.2), channel_id=1, source_target_pairs={{0,2},{1,3},{2,0},{3,1},{4,6},{5,7},{6,4},{7,5},{8,10},{9,11},{10,... | collective-permute-start | bytes 294920 | tf_op jit(solution)/shard_map/ppermute | solution.py:34
  23.2 16.3 %collective-permute-start.2 = (bf16[4,96,256]{2,1,0:T(8,128)(2,1)S(1)}, bf16[4,96,256]{2,1,0:T(8,128)(2,1)S(1)}, u32[]{:S(2)}, u32[]{:S(2)}) collective-permute-start(bf16[4,96,256]{2,1,0:T(8,128)(2,1)S(1)} %pad_maximum_fusion.1), channel_id=1, source_target_pairs={{0,4},{1,5},{2,6},{3,7},{4,0},{5,1},{6,2},{7,3},{8,12},{9,13},{10,... | collective-permute-start | bytes 589832 | tf_op jit(solution)/shard_map/ppermute | solution.py:34
  36.0 58.6 %copy-start.4 = (s32[2]{0:T(128)}, s32[2]{0:T(128)S(1)}, u32[]{:S(2)}) copy-start(s32[2]{0:T(128)S(1)} %add_multiply_fusion.place_ref) | copy-start | bytes 28
  39.5 55.0 %copy-start.1 = (bf16[8,96,256]{2,1,0:T(8,128)(2,1)}, bf16[8,96,256]{2,1,0:T(8,128)(2,1)S(1)}, u32[]{:S(2)}) copy-start(bf16[8,96,256]{2,1,0:T(8,128)(2,1)S(1)} %pad_maximum_fusion) | copy-start | bytes 1179652
  61.6 36.8 %all-to-all-start.1 = ((bf16[32,272,128]{2,1,0:T(8,128)(2,1)}), bf16[32,272,128]{2,1,0:T(8,128)(2,1)S(1)}, u32[]{:S(2)}, u32[]{:S(2)}) async-start(bf16[32,272,128]{2,1,0:T(8,128)(2,1)} %cross_heads.1), calls=%async_computation.1 | async-start | bytes 4456448 | tf_op jit(solution)/shard_map/all_to_all | solution.py:26
  70.7 23.9 %collective-permute-start.3 = (bf16[32,96,128]{2,1,0:T(8,128)(2,1)}, bf16[32,96,128]{2,1,0:T(8,128)(2,1)S(1)}, u32[]{:S(2)}, u32[]{:S(2)}) collective-permute-start(bf16[32,96,128]{2,1,0:T(8,128)(2,1)} %slice.3), channel_id=1, source_target_pairs={{0,8},{8,0},{16,24},{24,16},{32,40},{40,32},{48,56},{56,48},{64,72... | collective-permute-start | bytes 2359304 | tf_op jit(solution)/shard_map/ppermute | solution.py:45
  96.9 0.7 copy-start.2
  97.6 0.7 copy-start.3
  98.3 1.4 copy-start.5
  107.7 4.4 %collective-permute-start.4 = (bf16[32,96,128]{2,1,0:T(8,128)(2,1)}, bf16[32,96,128]{2,1,0:T(8,128)(2,1)S(1)}, u32[]{:S(2)}, u32[]{:S(2)}) collective-permute-start(bf16[32,96,128]{2,1,0:T(8,128)(2,1)} %get-tuple-element.25), channel_id=1, source_target_pairs={{0,8},{8,0},{16,24},{24,16},{32,40},{40,32},{48,56},{56,48},{64,72... | collective-permute-start | bytes 2359304 | tf_op jit(solution)/shard_map/ppermute | solution.py:45
  112.1 1.5 %copy-start = (bf16[32,224,128]{2,1,0:T(8,128)(2,1)S(1)}, bf16[32,224,128]{2,1,0:T(8,128)(2,1)}, u32[]{:S(2)}) copy-start(bf16[32,224,128]{2,1,0:T(8,128)(2,1)} %get-tuple-element.24.sent_ref) | copy-start | bytes 5505028

commit v6 on v5

--- a/solution.py
+++ b/solution.py
@@ -16,6 +16,9 @@
 F32 = jnp.float32
 BF16 = jnp.bfloat16
 MIB = 1024 * 1024
+
+
+IN_HBM = pl.BlockSpec(memory_space=pltpu.HBM)
 
 
 def kernel_params(mib=48):
@@ -49,34 +52,67 @@
     return lax.dot_general(a, b, (((dim_a,), (dim_b,)), ((), ())), preferred_element_type=F32)
 
 
-def self_heads_kernel(group, q_ref, k_ref, v_ref, audio_ref, out_ref):
-    rows = q_ref.shape[0]
-    owned, features = audio_ref.shape
+def self_heads_kernel(
+    group, q_hbm, k_hbm, v_hbm, audio_hbm, out_hbm, loaded, audio, out, in_sem, audio_sem, out_sem
+):
+    heads = out.shape[0]
+    rows = loaded.shape[1]
+    owned, features = audio.shape
     chunks = features // HD // 2
-    for head in range(group):
-        cols = slice(head * HD, (head + 1) * HD)
-        out_ref[head, 0:rows] = q_ref[:, cols]
-        out_ref[head, rows : 2 * rows] = k_ref[:, cols]
-        out_ref[head, 2 * rows : 3 * rows] = v_ref[:, cols]
-        for chunk in range(chunks):
-            first = 3 * rows + chunk * owned
-            lane = (head % 2 * chunks + chunk) * HD
-            out_ref[head, first : first + owned] = audio_ref[:, lane : lane + HD]
+    loads = []
+    for first in range(0, heads, group):
+        cols = pl.ds(first * HD, group * HD)
+        part = [
+            pltpu.make_async_copy(
+                source.at[0, :, cols], loaded.at[which, :, cols], in_sem.at[which, first // group]
+            )
+            for which, source in enumerate((q_hbm, k_hbm, v_hbm))
+        ]
+        for copy in part:
+            copy.start()
+        loads.append(part)
+    audio_load = pltpu.make_async_copy(audio_hbm.at[0], audio, audio_sem)
+    audio_load.start()
+    audio_load.wait()
+    stores = []
+    for part in range(len(loads)):
+        for copy in loads[part]:
+            copy.wait()
+        for head in range(part * group, (part + 1) * group):
+            for which in range(3):
+                out[head, which * rows : (which + 1) * rows] = loaded[
+                    which, :, head * HD : (head + 1) * HD
+                ]
+            for chunk in range(chunks):
+                first = 3 * rows + chunk * owned
+                lane = (head % 2 * chunks + chunk) * HD
+                out[head, first : first + owned] = audio[:, lane : lane + HD]
+        here = pl.ds(part * group, group)
+        stores.append(pltpu.make_async_copy(out.at[here], out_hbm.at[here], out_sem.at[part]))
+        stores[-1].start()
+    for copy in stores:
+        copy.wait()
 
 
 def self_heads(q_local, k_local, v_local, audio):
     _, rows, width = q_local.shape
     _, owned, features = audio.shape
     heads = width // HD
-    group = 8
+    group = 4
     total = 3 * rows + owned * (features // HD // 2)
-    block = pl.BlockSpec((None, rows, group * HD), lambda i: (0, 0, i))
     return pl.pallas_call(
         functools.partial(self_heads_kernel, group),
-        grid=(heads // group,),
-        in_specs=[block] * 3 + [pl.BlockSpec((None, owned, features), lambda i: (0, 0, 0))],
-        out_specs=pl.BlockSpec((group, total, HD), lambda i: (i, 0, 0)),
+        in_specs=[IN_HBM] * 4,
+        out_specs=IN_HBM,
         out_shape=jax.ShapeDtypeStruct((heads, total, HD), BF16),
+        scratch_shapes=[
+            pltpu.VMEM((3, rows, width), BF16),
+            pltpu.VMEM((owned, features), BF16),
+            pltpu.VMEM((heads, total, HD), BF16),
+            pltpu.SemaphoreType.DMA((3, heads // group)),
+            pltpu.SemaphoreType.DMA,
+            pltpu.SemaphoreType.DMA((heads // group,)),
+        ],
         compiler_params=kernel_params(60),
         cost_estimate=pl.CostEstimate(
             flops=0, bytes_accessed=7 * rows * width * 2, transcendentals=0
@@ -201,6 +237,7 @@
     values_ref,
     proj_ref,
     sent_hbm,
+    terms_hbm,
     away_hbm,
     got,
     own,
@@ -296,11 +333,7 @@
         here = pl.ds(block * per, per)
         stored += [
             pltpu.make_async_copy(away.at[here], away_hbm.at[here], out_sem.at[1, block]),
-            pltpu.make_async_copy(
-                terms.at[here],
-                sent_hbm.at[here, pl.ds(rows, chunks * owned), :],
-                out_sem.at[2, block],
-            ),
+            pltpu.make_async_copy(terms.at[here], terms_hbm.at[here], out_sem.at[2, block]),
         ]
         for copy in stored[-2:]:
             copy.start()
@@ -317,6 +350,7 @@
     term_rows = features // 2 // HD * owned
     anywhere = pl.BlockSpec(memory_space=pl.ANY)
     flat = pl.BlockSpec((padded, HD), lambda i: (0, 0))
+    term_shape = jax.ShapeDtypeStruct((sources, term_rows, HD), BF16)
     return pl.pallas_call(
         functools.partial(cross_kernel, rows),
         grid=(1,),
@@ -328,10 +362,11 @@
             flat,
             pl.BlockSpec((features, 2 * HD), lambda i: (0, 0)),
         ],
-        out_specs=[anywhere, anywhere],
+        out_specs=[anywhere, anywhere, anywhere],
         out_shape=[
             jax.ShapeDtypeStruct((sources, rows + term_rows, HD), BF16),
-            jax.ShapeDtypeStruct((sources, term_rows, HD), BF16),
+            term_shape,
+            term_shape,
         ],
         scratch_shapes=[
             pltpu.VMEM((sources, total, HD), BF16),
@@ -344,7 +379,7 @@
             pltpu.SemaphoreType.DMA((2, sources // 8)),
             pltpu.SemaphoreType.DMA((3, sources // 8)),
         ],
-        compiler_params=kernel_params(60),
+        compiler_params=kernel_params(24),
         cost_estimate=pl.CostEstimate(
             flops=4 * sources * owned * features * HD + 10 * sources * rows * HD * HD,
             bytes_accessed=2 * (got.size + proj.size + 4 * own_heads.size),
@@ -352,31 +387,6 @@
         ),
         name="cross_attention",
     )(place, got, own_heads, keys, values, proj)
-
-
-def pair_kernel(sent_ref, came_ref, out_ref):
-    out_ref[...] = (sent_ref[...].astype(F32) + came_ref[...].astype(F32)).astype(BF16)
-
-
-def pair_added(sent, came):
-    sources, term_rows, _ = came.shape
-    total = sent.shape[1]
-    width = 32
-    ahead = (total - term_rows) // width
-    block = pl.BlockSpec((sources, width, HD), lambda i: (0, ahead + i, 0))
-    return pl.pallas_call(
-        pair_kernel,
-        grid=(term_rows // width,),
-        in_specs=[block, pl.BlockSpec((sources, width, HD), lambda i: (0, i, 0))],
-        out_specs=block,
-        out_shape=jax.ShapeDtypeStruct(sent.shape, BF16),
-        input_output_aliases={0: 0},
-        compiler_params=kernel_params(8),
-        cost_estimate=pl.CostEstimate(
-            flops=came.size, bytes_accessed=6 * came.size, transcendentals=0
-        ),
-        name="pair_added",
-    )(sent, came)
 
 
 def self_attention_kernel(
@@ -563,8 +573,9 @@
     other = from_other_core(qkv[:, 3 * rows :])
     own_heads = attend_self(qkv, rows)
     keys, values = projected(place, qkv, 3 * rows, other, proj)
-    sent, away = cross_attention(place, cross, own_heads, keys, values, proj)
-    sent = pair_added(sent, from_other_core(away))
+    sent, terms, away = cross_attention(place, cross, own_heads, keys, values, proj)
+    both_terms = terms.astype(F32) + from_other_core(away).astype(F32)
+    sent = lax.dynamic_update_slice(sent, both_terms.astype(BF16), (0, rows, 0))
     block_out, audio_grad = arrived(handed_over(sent), rows, owned)
     return (block_out, audio_grad)
 

time: 147 us -> 147 us (level)
    pallas_call x2 -> x1, Pallas kernels: 4.99 us -> 4.1 us  [self_heads(): pl.pallas_call(functools.partial(self_heads_kernel, group), in_specs=[IN_...]
    unnamed x16 -> x14, local copies, waits for them, and re-layouts: 4.32 us -> 4.55 us
where the time goes in v6:
time: 147 us
  Pallas kernels  44.4 us (30%)
  starting transfers between devices  31.9 us (22%)
  waiting for transfers between devices  31.7 us (22%)
  blocking collectives  30.7 us (21%)
  local copies, waits for them, and re-layouts  6.64 us (5%)
    all_to_all x1, blocking collectives, handed_over(): return lax.all_to_all(parts, 'seq', split_axis=0, concat_axis=0, tiled=True)  30.7 us
    pallas_call x1, Pallas kernels, attend_self(): pl.pallas_call(functools.partial(self_attention_kernel, block_rows, block...  23.5 us
    all_to_all x2, waiting for transfers between devices, handed_over(): return lax.all_to_all(parts, 'seq', split_axis=0, concat_axis=0, tiled=True)  22 us
    all_to_all x2, starting transfers between devices, handed_over(): return lax.all_to_all(parts, 'seq', split_axis=0, concat_axis=0, tiled=True)  15.7 us
    ppermute x3, starting transfers between devices, gathered_by_doubling(): other = lax.ppermute(block, axis, [(i, i ^ step) for i in range(size)])  13.5 us
    pallas_call x1, Pallas kernels, cross_attention(): pl.pallas_call(functools.partial(cross_kernel, rows), grid=(1,), in_specs...  8.82 us
    ppermute x3, waiting for transfers between devices, gathered_by_doubling(): other = lax.ppermute(block, axis, [(i, i ^ step) for i in range(size)])  7.77 us
    unnamed x14, local copies, waits for them, and re-layouts  4.55 us
  transfers between devices with their start and end apart: 7, of which 5 were waited for; matrix products, arithmetic and copies ran while one was open for 2% of the time, Pallas kernels for 20%

profile of v6, /device:TPU:1, one launch (start us, length us, event | category | flops | bytes accessed | tf_op | source)
XLA Modules:
  0.0 146.6 jit_solution(2532289078445120077)
XLA Ops:
  0.6 4.1 %self_heads.1 = bf16[32,480,128]{2,1,0:T(8,128)(2,1)} custom-call(bf16[1,128,4096]{2,1,0:T(8,128)(2,1)} %q_hbm.1, bf16[1,128,4096]{2,1,0:T(8,128)(2,1)} %k_hbm.1, bf16[1,128,4096]{2,1,0:T(8,128)(2,1)} %v_hbm.1, bf16[1,32,768]{2,1,0:T(8,128)(2,1)} %audio_hbm.1), custom_call_target="tpu_custom_call" | custom-call | bytes 7340032 | tf_op jit(solution)/shard_map/self_heads/pallas_call | solution.py:103
  4.7 0.0 copy-start.5
  4.7 0.0 copy-start.6
  4.8 8.7 %all-to-all-start = ((bf16[32,480,128]{2,1,0:T(8,128)(2,1)}), bf16[32,480,128]{2,1,0:T(8,128)(2,1)}, u32[]{:S(2)}, u32[]{:S(2)}) async-start(bf16[32,480,128]{2,1,0:T(8,128)(2,1)} %self_heads.1), calls=%async_computation | async-start | bytes 7864320 | tf_op jit(solution)/shard_map/all_to_all | solution.py:29
  13.5 1.7 %collective-permute-start = (bf16[1,96,256]{2,1,0:T(8,128)(2,1)S(1)}, bf16[1,96,256]{2,1,0:T(8,128)(2,1)S(1)}, u32[]{:S(2)}, u32[]{:S(2)}) collective-permute-start(bf16[1,96,256]{2,1,0:T(8,128)(2,1)S(1)} %maximum_bitcast_fusion), channel_id=1, source_target_pairs={{0,1},{1,0},{2,3},{3,2},{4,5},{5,4},{6,7},{7,6},{8,9},{9,8},{10,11... | collective-permute-start | bytes 147464 | tf_op jit(solution)/shard_map/ppermute | solution.py:37
  15.2 1.9 %collective-permute-done = bf16[1,96,256]{2,1,0:T(8,128)(2,1)S(1)} collective-permute-done((bf16[1,96,256]{2,1,0:T(8,128)(2,1)S(1)}, bf16[1,96,256]{2,1,0:T(8,128)(2,1)S(1)}, u32[]{:S(2)}, u32[]{:S(2)}) %collective-permute-start) | collective-permute-done | bytes 49184 | tf_op jit(solution)/shard_map/ppermute | solution.py:37
  17.1 3.1 %collective-permute-start.1 = (bf16[2,96,256]{2,1,0:T(8,128)(2,1)S(1)}, bf16[2,96,256]{2,1,0:T(8,128)(2,1)S(1)}, u32[]{:S(2)}, u32[]{:S(2)}) collective-permute-start(bf16[2,96,256]{2,1,0:T(8,128)(2,1)S(1)} %pad_maximum_fusion.2), channel_id=1, source_target_pairs={{0,2},{1,3},{2,0},{3,1},{4,6},{5,7},{6,4},{7,5},{8,10},{9,11},{10,... | collective-permute-start | bytes 294920 | tf_op jit(solution)/shard_map/ppermute | solution.py:37
  20.2 2.4 %collective-permute-done.1 = bf16[2,96,256]{2,1,0:T(8,128)(2,1)S(1)} collective-permute-done((bf16[2,96,256]{2,1,0:T(8,128)(2,1)S(1)}, bf16[2,96,256]{2,1,0:T(8,128)(2,1)S(1)}, u32[]{:S(2)}, u32[]{:S(2)}) %collective-permute-start.1) | collective-permute-done | bytes 98336 | tf_op jit(solution)/shard_map/ppermute | solution.py:37
  22.6 8.7 %collective-permute-start.2 = (bf16[4,96,256]{2,1,0:T(8,128)(2,1)S(1)}, bf16[4,96,256]{2,1,0:T(8,128)(2,1)S(1)}, u32[]{:S(2)}, u32[]{:S(2)}) collective-permute-start(bf16[4,96,256]{2,1,0:T(8,128)(2,1)S(1)} %pad_maximum_fusion.1), channel_id=1, source_target_pairs={{0,4},{1,5},{2,6},{3,7},{4,0},{5,1},{6,2},{7,3},{8,12},{9,13},{10,... | collective-permute-start | bytes 589832 | tf_op jit(solution)/shard_map/ppermute | solution.py:37
  31.4 4.0 %cross_heads.1 = bf16[32,272,128]{2,1,0:T(8,128)(2,1)} custom-call(s32[2,4]{1,0:T(2,128)} %bitcast.14, s32[2]{0:T(128)} %bitcast.15, s32[1]{0:T(128)} %bitcast.2.first_ref, bf16[1,128,4096]{2,1,0:T(8,128)(2,1)} %q_ref, bf16[1,128,4096]{2,1,0:T(8,128)(2,1)} %grad_ref.1), custom_call_target="tpu_custom_call" | custom-call | bytes 4194304 | tf_op jit(solution)/shard_map/cross_heads/pallas_call | solution.py:150
  35.3 0.1 add_multiply_fusion.place_ref
  35.4 3.5 %collective-permute-done.2 = bf16[4,96,256]{2,1,0:T(8,128)(2,1)S(1)} collective-permute-done((bf16[4,96,256]{2,1,0:T(8,128)(2,1)S(1)}, bf16[4,96,256]{2,1,0:T(8,128)(2,1)S(1)}, u32[]{:S(2)}, u32[]{:S(2)}) %collective-permute-start.2) | collective-permute-done | bytes 196640 | tf_op jit(solution)/shard_map/ppermute | solution.py:37
  39.0 22.0 %all-to-all-done.q_ref.k_ref.v_ref.qkv_ref = bf16[32,480,128]{2,1,0:T(8,128)(2,1)} async-done(((bf16[32,480,128]{2,1,0:T(8,128)(2,1)}), bf16[32,480,128]{2,1,0:T(8,128)(2,1)}, u32[]{:S(2)}, u32[]{:S(2)}) %all-to-all-start) | async-done | bytes 3932192 | tf_op jit(solution)/shard_map/all_to_all | solution.py:29
  61.0 7.0 %all-to-all-start.1 = ((bf16[32,272,128]{2,1,0:T(8,128)(2,1)}), bf16[32,272,128]{2,1,0:T(8,128)(2,1)S(1)}, u32[]{:S(2)}, u32[]{:S(2)}) async-start(bf16[32,272,128]{2,1,0:T(8,128)(2,1)} %cross_heads.1), calls=%async_computation.1 | async-start | bytes 4456448 | tf_op jit(solution)/shard_map/all_to_all | solution.py:29
  68.0 2.1 %slice.3 = bf16[32,96,128]{2,1,0:T(8,128)(2,1)} slice(bf16[32,480,128]{2,1,0:T(8,128)(2,1)} %all-to-all-done.q_ref.k_ref.v_ref.qkv_ref), slice={[0:32], [384:480], [0:128]} | slice | bytes 1572864 | tf_op jit(solution)/shard_map/slice | solution.py:573
  70.1 0.3 collective-permute-start.3
  70.5 23.5 %self_attention.1.own_hbm = bf16[32,128,128]{2,1,0:T(8,128)(2,1)} custom-call(bf16[32,480,128]{2,1,0:T(8,128)(2,1)} %all-to-all-done.q_ref.k_ref.v_ref.qkv_ref, bf16[32,480,128]{2,1,0:T(8,128)(2,1)} %all-to-all-done.q_ref.k_ref.v_ref.qkv_ref, bf16[32,480,128]{2,1,0:T(8,128)(2,1)} %all-to-all-done.q_ref.k_ref.v_ref.qkv_ref), custom_call_target="tpu_custom_call" | custom-call | flops 17179869184 | bytes 4194304 | tf_op jit(solution)/shard_map/self_attention/pallas_call | solution.py:471
  94.0 0.0 collective-permute-done.3.other_ref
  94.0 2.3 %projected.1 = (bf16[1120,128]{1,0:T(8,128)(2,1)S(1)}, bf16[1120,128]{1,0:T(8,128)(2,1)S(1)}) custom-call(s32[2]{0:T(128)S(1)} %add_multiply_fusion.place_ref, bf16[32,480,128]{2,1,0:T(8,128)(2,1)} %all-to-all-done.q_ref.k_ref.v_ref.qkv_ref, bf16[32,96,128]{2,1,0:T(8,128)(2,1)S(1)} %collective-permute-done.3.other_ref, bf16[768,256]{1,0:T(8,128)(2,1)S(1)} %bitcast.12), custom_call_target="tpu_custom_call" | custom-call | flops 402653184 | bytes 2539520 | tf_op jit(solution)/shard_map/projected/pallas_call | solution.py:206
  96.3 0.0 copy-start.1
  96.3 0.7 copy-done.1
  97.0 0.7 copy-done.3
  97.7 0.0 all-to-all-done.1.got_hbm
  97.7 1.2 copy-done
  98.9 1.0 copy-done.2
  99.9 1.0 copy-done.4
  100.8 8.8 %cross_attention.1 = (bf16[32,224,128]{2,1,0:T(8,128)(2,1)S(1)}, bf16[32,96,128]{2,1,0:T(8,128)(2,1)S(1)}, bf16[32,96,128]{2,1,0:T(8,128)(2,1)S(1)}) custom-call(s32[2]{0:T(128)S(1)} %add_multiply_fusion.place_ref, bf16[32,272,128]{2,1,0:T(8,128)(2,1)S(1)} %all-to-all-done.1.got_hbm, bf16[32,128,128]{2,1,0:T(8,128)(2,1)S(1)} %copy-done, ...), custom_call_target="tpu_custom_call" | custom-call | flops 1073741824 | bytes 6815744 | tf_op jit(solution)/shard_map/cross_attention/pallas_call | solution.py:354
  109.7 2.3 %collective-permute-start.4 = (bf16[32,96,128]{2,1,0:T(8,128)(2,1)S(1)}, bf16[32,96,128]{2,1,0:T(8,128)(2,1)S(1)}, u32[]{:S(2)}, u32[]{:S(2)}) collective-permute-start(bf16[32,96,128]{2,1,0:T(8,128)(2,1)S(1)} %get-tuple-element.27), channel_id=1, source_target_pairs={{0,8},{8,0},{16,24},{24,16},{32,40},{40,32},{48,56},{56,48},{64,72... | collective-permute-start | bytes 2359304 | tf_op jit(solution)/shard_map/ppermute | solution.py:48
  112.0 1.9 %collective-permute-done.4 = bf16[32,96,128]{2,1,0:T(8,128)(2,1)S(1)} collective-permute-done((bf16[32,96,128]{2,1,0:T(8,128)(2,1)S(1)}, bf16[32,96,128]{2,1,0:T(8,128)(2,1)S(1)}, u32[]{:S(2)}, u32[]{:S(2)}) %collective-permute-start.4) | collective-permute-done | bytes 786464 | tf_op jit(solution)/shard_map/ppermute | solution.py:48
  113.9 0.3 fusion
  114.2 30.7 %all_to_all.15.got_ref = bf16[32,224,128]{2,1,0:T(8,128)(2,1)S(1)} all-to-all(bf16[32,224,128]{2,1,0:T(8,128)(2,1)S(1)} %fusion), channel_id=1, replica_groups=mesh['seq'=32,'fsdp'=8] {'seq'}, dimensions={0} | all-to-all | bytes 3670016 | tf_op jit(solution)/shard_map/all_to_all | solution.py:29
  144.8 1.8 %arrived.1 = (bf16[1,128,4096]{2,1,0:T(8,128)(2,1)}, f32[1,32,768]{2,1,0:T(8,128)}) custom-call(bf16[32,224,128]{2,1,0:T(8,128)(2,1)S(1)} %all_to_all.15.got_ref), custom_call_target="tpu_custom_call" | custom-call | flops 917504 | bytes 3670016 | tf_op jit(solution)/shard_map/arrived/pallas_call | solution.py:521
  (13 shorter events, 0.2 us)
Async XLA Ops:
  4.7 8.7 %copy-start.5 = (bf16[96,128]{1,0:T(8,128)(2,1)S(1)}, bf16[96,128]{1,0:T(8,128)(2,1)}, u32[]{:S(2)}) copy-start(bf16[96,128]{1,0:T(8,128)(2,1)} %param.16) | copy-start | bytes 73732
  4.7 8.7 %copy-start.6 = (bf16[96,128]{1,0:T(8,128)(2,1)S(1)}, bf16[96,128]{1,0:T(8,128)(2,1)}, u32[]{:S(2)}) copy-start(bf16[96,128]{1,0:T(8,128)(2,1)} %param.15) | copy-start | bytes 73732
  4.8 56.2 %all-to-all-start = ((bf16[32,480,128]{2,1,0:T(8,128)(2,1)}), bf16[32,480,128]{2,1,0:T(8,128)(2,1)}, u32[]{:S(2)}, u32[]{:S(2)}) async-start(bf16[32,480,128]{2,1,0:T(8,128)(2,1)} %self_heads.1), calls=%async_computation | async-start | bytes 7864320 | tf_op jit(solution)/shard_map/all_to_all | solution.py:29
  13.5 3.6 %collective-permute-start = (bf16[1,96,256]{2,1,0:T(8,128)(2,1)S(1)}, bf16[1,96,256]{2,1,0:T(8,128)(2,1)S(1)}, u32[]{:S(2)}, u32[]{:S(2)}) collective-permute-start(bf16[1,96,256]{2,1,0:T(8,128)(2,1)S(1)} %maximum_bitcast_fusion), channel_id=1, source_target_pairs={{0,1},{1,0},{2,3},{3,2},{4,5},{5,4},{6,7},{7,6},{8,9},{9,8},{10,11... | collective-permute-start | bytes 147464 | tf_op jit(solution)/shard_map/ppermute | solution.py:37
  17.1 5.5 %collective-permute-start.1 = (bf16[2,96,256]{2,1,0:T(8,128)(2,1)S(1)}, bf16[2,96,256]{2,1,0:T(8,128)(2,1)S(1)}, u32[]{:S(2)}, u32[]{:S(2)}) collective-permute-start(bf16[2,96,256]{2,1,0:T(8,128)(2,1)S(1)} %pad_maximum_fusion.2), channel_id=1, source_target_pairs={{0,2},{1,3},{2,0},{3,1},{4,6},{5,7},{6,4},{7,5},{8,10},{9,11},{10,... | collective-permute-start | bytes 294920 | tf_op jit(solution)/shard_map/ppermute | solution.py:37
  22.6 16.3 %collective-permute-start.2 = (bf16[4,96,256]{2,1,0:T(8,128)(2,1)S(1)}, bf16[4,96,256]{2,1,0:T(8,128)(2,1)S(1)}, u32[]{:S(2)}, u32[]{:S(2)}) collective-permute-start(bf16[4,96,256]{2,1,0:T(8,128)(2,1)S(1)} %pad_maximum_fusion.1), channel_id=1, source_target_pairs={{0,4},{1,5},{2,6},{3,7},{4,0},{5,1},{6,2},{7,3},{8,12},{9,13},{10,... | collective-permute-start | bytes 589832 | tf_op jit(solution)/shard_map/ppermute | solution.py:37
  61.0 36.7 %all-to-all-start.1 = ((bf16[32,272,128]{2,1,0:T(8,128)(2,1)}), bf16[32,272,128]{2,1,0:T(8,128)(2,1)S(1)}, u32[]{:S(2)}, u32[]{:S(2)}) async-start(bf16[32,272,128]{2,1,0:T(8,128)(2,1)} %cross_heads.1), calls=%async_computation.1 | async-start | bytes 4456448 | tf_op jit(solution)/shard_map/all_to_all | solution.py:29
  70.1 23.8 %collective-permute-start.3 = (bf16[32,96,128]{2,1,0:T(8,128)(2,1)}, bf16[32,96,128]{2,1,0:T(8,128)(2,1)S(1)}, u32[]{:S(2)}, u32[]{:S(2)}) collective-permute-start(bf16[32,96,128]{2,1,0:T(8,128)(2,1)} %slice.3), channel_id=1, source_target_pairs={{0,8},{8,0},{16,24},{24,16},{32,40},{40,32},{48,56},{56,48},{64,72... | collective-permute-start | bytes 2359304 | tf_op jit(solution)/shard_map/ppermute | solution.py:48
  96.3 0.7 copy-start.1
  97.0 0.7 copy-start.3
  97.7 1.2 copy-start
  98.9 1.0 copy-start.2
  99.9 1.0 copy-start.4
  109.7 4.3 %collective-permute-start.4 = (bf16[32,96,128]{2,1,0:T(8,128)(2,1)S(1)}, bf16[32,96,128]{2,1,0:T(8,128)(2,1)S(1)}, u32[]{:S(2)}, u32[]{:S(2)}) collective-permute-start(bf16[32,96,128]{2,1,0:T(8,128)(2,1)S(1)} %get-tuple-element.27), channel_id=1, source_target_pairs={{0,8},{8,0},{16,24},{24,16},{32,40},{40,32},{48,56},{56,48},{64,72... | collective-permute-start | bytes 2359304 | tf_op jit(solution)/shard_map/ppermute | solution.py:48

commit v7 on v6

--- a/solution.py
+++ b/solution.py
@@ -231,23 +231,16 @@
 def cross_kernel(
     rows,
     place_ref,
-    got_hbm,
-    own_hbm,
+    got,
+    own,
     keys_ref,
     values_ref,
     proj_ref,
-    sent_hbm,
-    terms_hbm,
-    away_hbm,
-    got,
-    own,
     out,
     terms,
     away,
     d_keys,
     d_values,
-    in_sem,
-    out_sem,
 ):
     sources = got.shape[0]
     owned = AB * 2
@@ -257,26 +250,13 @@
     length = sources * owned
     edge = REACH * AB
     band = HD
-    at_once = 8
+    at_once = 16
     blocks = sources // at_once
 
-    fetched = []
-    for block in range(blocks):
-        here = pl.ds(block * at_once, at_once)
-        pair = (
-            pltpu.make_async_copy(got_hbm.at[here], got.at[here], in_sem.at[0, block]),
-            pltpu.make_async_copy(own_hbm.at[here], own.at[here], in_sem.at[1, block]),
-        )
-        for copy in pair:
-            copy.start()
-        fetched.append(pair)
     d_keys[...] = jnp.zeros_like(d_keys)
     d_values[...] = jnp.zeros_like(d_values)
 
-    stored = []
     for block in range(blocks):
-        for copy in fetched[block]:
-            copy.wait()
         sources_here = [block * at_once + i for i in range(at_once)]
         bands = [slice(t * owned, t * owned + band) for t in sources_here]
         k = [keys_ref[b] for b in bands]
@@ -303,17 +283,10 @@
             d_scores.append((weighed - weights[i] * inner).astype(BF16))
         for i, t in enumerate(sources_here):
             mixed = jnp.dot(weights_b[i], v[i], preferred_element_type=F32)
-            out[t] = (own[t].astype(F32) + mixed).astype(BF16)
+            out[t, 0:rows] = (own[t].astype(F32) + mixed).astype(BF16)
         for i, t in enumerate(sources_here):
             d_values[bands[i]] += contract(weights_b[i], got[t, rows : 2 * rows], 0, 0)
             d_keys[bands[i]] += contract(d_scores[i], got[t, 0:rows], 0, 0)
-        here = pl.ds(block * at_once, at_once)
-        stored.append(
-            pltpu.make_async_copy(
-                out.at[here], sent_hbm.at[here, pl.ds(0, rows), :], out_sem.at[0, block]
-            )
-        )
-        stored[-1].start()
 
     own_proj = proj_ref[pl.ds(pl.multiple_of(place_ref[0], HD), half)]
     other_proj = proj_ref[pl.ds(pl.multiple_of(place_ref[1], HD), half)]
@@ -330,63 +303,36 @@
                 buffer[
                     block * per : (block + 1) * per, chunk * owned : (chunk + 1) * owned
                 ] = term[:, chunk * HD : (chunk + 1) * HD].reshape(per, owned, HD)
-        here = pl.ds(block * per, per)
-        stored += [
-            pltpu.make_async_copy(away.at[here], away_hbm.at[here], out_sem.at[1, block]),
-            pltpu.make_async_copy(terms.at[here], terms_hbm.at[here], out_sem.at[2, block]),
-        ]
-        for copy in stored[-2:]:
-            copy.start()
-    for copy in stored:
-        copy.wait()
 
 
 def cross_attention(place, got, own_heads, keys, values, proj):
     sources, rows, _ = own_heads.shape
-    total = got.shape[1]
     features = proj.shape[0]
     owned = 2 * AB
     padded = keys.shape[0]
     term_rows = features // 2 // HD * owned
-    anywhere = pl.BlockSpec(memory_space=pl.ANY)
-    flat = pl.BlockSpec((padded, HD), lambda i: (0, 0))
-    term_shape = jax.ShapeDtypeStruct((sources, term_rows, HD), BF16)
+    terms = jax.ShapeDtypeStruct((sources, term_rows, HD), BF16)
+
+    def whole(array):
+        return pl.BlockSpec(array.shape, lambda i: (0,) * len(array.shape))
+
+    operands = (got, own_heads, keys, values, proj)
+    results = [jax.ShapeDtypeStruct((sources, rows + term_rows, HD), BF16), terms, terms]
     return pl.pallas_call(
         functools.partial(cross_kernel, rows),
         grid=(1,),
-        in_specs=[
-            pl.BlockSpec(memory_space=pltpu.SMEM),
-            anywhere,
-            anywhere,
-            flat,
-            flat,
-            pl.BlockSpec((features, 2 * HD), lambda i: (0, 0)),
-        ],
-        out_specs=[anywhere, anywhere, anywhere],
-        out_shape=[
-            jax.ShapeDtypeStruct((sources, rows + term_rows, HD), BF16),
-            term_shape,
-            term_shape,
-        ],
-        scratch_shapes=[
-            pltpu.VMEM((sources, total, HD), BF16),
-            pltpu.VMEM((sources, rows, HD), BF16),
-            pltpu.VMEM((sources, rows, HD), BF16),
-            pltpu.VMEM((sources, term_rows, HD), BF16),
-            pltpu.VMEM((sources, term_rows, HD), BF16),
-            pltpu.VMEM((padded, HD), F32),
-            pltpu.VMEM((padded, HD), F32),
-            pltpu.SemaphoreType.DMA((2, sources // 8)),
-            pltpu.SemaphoreType.DMA((3, sources // 8)),
-        ],
-        compiler_params=kernel_params(24),
+        in_specs=[pl.BlockSpec(memory_space=pltpu.SMEM)] + [whole(x) for x in operands],
+        out_specs=[whole(x) for x in results],
+        out_shape=results,
+        scratch_shapes=[pltpu.VMEM((padded, HD), F32), pltpu.VMEM((padded, HD), F32)],
+        compiler_params=kernel_params(48),
         cost_estimate=pl.CostEstimate(
             flops=4 * sources * owned * features * HD + 10 * sources * rows * HD * HD,
             bytes_accessed=2 * (got.size + proj.size + 4 * own_heads.size),
             transcendentals=sources * rows * HD,
         ),
         name="cross_attention",
-    )(place, got, own_heads, keys, values, proj)
+    )(place, *operands)
 
 
 def self_attention_kernel(
@@ -480,7 +426,7 @@
             pltpu.VMEM((2, block_rows, length), F32),
             pltpu.VMEM((2, block_rows, HD), F32),
         ],
-        compiler_params=kernel_params(60),
+        compiler_params=kernel_params(48),
         cost_estimate=pl.CostEstimate(
             flops=8 * length * length * HD,
             bytes_accessed=8 * length * HD,
@@ -517,7 +463,7 @@
 def arrived(got, rows, owned):
     heads, total, _ = got.shape
     features = 2 * (total - rows) // owned * HD
-    group = 8
+    group = 16
     return pl.pallas_call(
         functools.partial(arrive_kernel, group, owned),
         grid=(heads // group,),

time: 147 us -> 139 us (0.946)
  local copies, waits for them, and re-layouts: 6.64 us -> 1.21 us
  Pallas kernels: 44.4 us -> 39.9 us
  waiting for transfers between devices: 31.7 us -> 34.3 us
  blocking collectives: 30.7 us -> 28.6 us
    unnamed x14 -> x4, local copies, waits for them, and re-layouts: 4.55 us -> 0.01 us
    pallas_call x1, Pallas kernels: 8.82 us -> 5.66 us  [cross_attention(): pl.pallas_call(functools.partial(cross_kernel, rows), grid=(1,), in_specs...]
    all_to_all x2, waiting for transfers between devices: 22 us -> 24.7 us  [handed_over(): return lax.all_to_all(parts, 'seq', split_axis=0, concat_axis=0, tiled=True)]
    all_to_all x1, blocking collectives: 30.7 us -> 28.6 us  [handed_over(): return lax.all_to_all(parts, 'seq', split_axis=0, concat_axis=0, tiled=True)]
  transfers between devices with their start and end apart: 7 -> 7, of which waited for: 5 -> 6; matrix products, arithmetic and copies ran while one was open for 2% -> 1% of each run, Pallas kernels for 20% -> 21%
where the time goes in v7:
time: 139 us; the launch traced here: 138 us
  Pallas kernels  39.9 us (29%)
  waiting for transfers between devices  34.3 us (25%)
  starting transfers between devices  33.2 us (24%)
  blocking collectives  28.6 us (21%)
    all_to_all x1, blocking collectives, handed_over(): return lax.all_to_all(parts, 'seq', split_axis=0, concat_axis=0, tiled=True)  28.6 us
    all_to_all x2, waiting for transfers between devices, handed_over(): return lax.all_to_all(parts, 'seq', split_axis=0, concat_axis=0, tiled=True)  24.7 us
    pallas_call x1, Pallas kernels, attend_self(): pl.pallas_call(functools.partial(self_attention_kernel, block_rows, block...  22.6 us
    all_to_all x2, starting transfers between devices, handed_over(): return lax.all_to_all(parts, 'seq', split_axis=0, concat_axis=0, tiled=True)  16.4 us
    ppermute x3, starting transfers between devices, gathered_by_doubling(): other = lax.ppermute(block, axis, [(i, i ^ step) for i in range(size)])  13.5 us
    ppermute x3, waiting for transfers between devices, gathered_by_doubling(): other = lax.ppermute(block, axis, [(i, i ^ step) for i in range(size)])  7.75 us
    pallas_call x1, Pallas kernels, cross_attention(): pl.pallas_call(functools.partial(cross_kernel, rows), grid=(1,), in_specs...  5.66 us
    pallas_call x1, Pallas kernels, self_heads(): pl.pallas_call(functools.partial(self_heads_kernel, group), in_specs=[IN_...  4.1 us
  transfers between devices with their start and end apart: 7, of which 6 were waited for; matrix products, arithmetic and copies ran while one was open for 1% of the time, Pallas kernels for 21%

profile of v7, /device:TPU:1, one launch (start us, length us, event | category | flops | bytes accessed | tf_op | source)
XLA Modules:
  0.0 138.5 jit_solution(6435254042965622699)
XLA Ops:
  0.6 4.1 %self_heads.1 = bf16[32,480,128]{2,1,0:T(8,128)(2,1)} custom-call(bf16[1,128,4096]{2,1,0:T(8,128)(2,1)} %q_hbm.1, bf16[1,128,4096]{2,1,0:T(8,128)(2,1)} %k_hbm.1, bf16[1,128,4096]{2,1,0:T(8,128)(2,1)} %v_hbm.1, bf16[1,32,768]{2,1,0:T(8,128)(2,1)} %audio_hbm.1), custom_call_target="tpu_custom_call" | custom-call | bytes 7340032 | tf_op jit(solution)/shard_map/self_heads/pallas_call | solution.py:103
  4.7 0.0 copy-start
  4.8 0.0 copy-start.1
  4.8 8.7 %all-to-all-start = ((bf16[32,480,128]{2,1,0:T(8,128)(2,1)}), bf16[32,480,128]{2,1,0:T(8,128)(2,1)}, u32[]{:S(2)}, u32[]{:S(2)}) async-start(bf16[32,480,128]{2,1,0:T(8,128)(2,1)} %self_heads.1), calls=%async_computation | async-start | bytes 7864320 | tf_op jit(solution)/shard_map/all_to_all | solution.py:29
  13.4 0.0 copy-done
  13.4 0.0 copy-done.1
  13.5 1.7 %collective-permute-start = (bf16[1,96,256]{2,1,0:T(8,128)(2,1)S(1)}, bf16[1,96,256]{2,1,0:T(8,128)(2,1)S(1)}, u32[]{:S(2)}, u32[]{:S(2)}) collective-permute-start(bf16[1,96,256]{2,1,0:T(8,128)(2,1)S(1)} %maximum_bitcast_fusion), channel_id=1, source_target_pairs={{0,1},{1,0},{2,3},{3,2},{4,5},{5,4},{6,7},{7,6},{8,9},{9,8},{10,11... | collective-permute-start | bytes 147464 | tf_op jit(solution)/shard_map/ppermute | solution.py:37
  15.2 1.9 %collective-permute-done = bf16[1,96,256]{2,1,0:T(8,128)(2,1)S(1)} collective-permute-done((bf16[1,96,256]{2,1,0:T(8,128)(2,1)S(1)}, bf16[1,96,256]{2,1,0:T(8,128)(2,1)S(1)}, u32[]{:S(2)}, u32[]{:S(2)}) %collective-permute-start) | collective-permute-done | bytes 49184 | tf_op jit(solution)/shard_map/ppermute | solution.py:37
  17.1 3.1 %collective-permute-start.1 = (bf16[2,96,256]{2,1,0:T(8,128)(2,1)S(1)}, bf16[2,96,256]{2,1,0:T(8,128)(2,1)S(1)}, u32[]{:S(2)}, u32[]{:S(2)}) collective-permute-start(bf16[2,96,256]{2,1,0:T(8,128)(2,1)S(1)} %pad_maximum_fusion.2), channel_id=1, source_target_pairs={{0,2},{1,3},{2,0},{3,1},{4,6},{5,7},{6,4},{7,5},{8,10},{9,11},{10,... | collective-permute-start | bytes 294920 | tf_op jit(solution)/shard_map/ppermute | solution.py:37
  20.2 2.4 %collective-permute-done.1 = bf16[2,96,256]{2,1,0:T(8,128)(2,1)S(1)} collective-permute-done((bf16[2,96,256]{2,1,0:T(8,128)(2,1)S(1)}, bf16[2,96,256]{2,1,0:T(8,128)(2,1)S(1)}, u32[]{:S(2)}, u32[]{:S(2)}) %collective-permute-start.1) | collective-permute-done | bytes 98336 | tf_op jit(solution)/shard_map/ppermute | solution.py:37
  22.6 8.7 %collective-permute-start.2 = (bf16[4,96,256]{2,1,0:T(8,128)(2,1)S(1)}, bf16[4,96,256]{2,1,0:T(8,128)(2,1)S(1)}, u32[]{:S(2)}, u32[]{:S(2)}) collective-permute-start(bf16[4,96,256]{2,1,0:T(8,128)(2,1)S(1)} %pad_maximum_fusion.1), channel_id=1, source_target_pairs={{0,4},{1,5},{2,6},{3,7},{4,0},{5,1},{6,2},{7,3},{8,12},{9,13},{10,... | collective-permute-start | bytes 589832 | tf_op jit(solution)/shard_map/ppermute | solution.py:37
  31.4 4.0 %cross_heads.1 = bf16[32,272,128]{2,1,0:T(8,128)(2,1)} custom-call(s32[2,4]{1,0:T(2,128)} %bitcast.14, s32[2]{0:T(128)} %bitcast.15, s32[1]{0:T(128)} %bitcast.2.first_ref, bf16[1,128,4096]{2,1,0:T(8,128)(2,1)} %q_ref, bf16[1,128,4096]{2,1,0:T(8,128)(2,1)} %grad_ref.1), custom_call_target="tpu_custom_call" | custom-call | bytes 4194304 | tf_op jit(solution)/shard_map/cross_heads/pallas_call | solution.py:150
  35.4 0.1 add_multiply_fusion.place_ref
  35.4 3.5 %collective-permute-done.2 = bf16[4,96,256]{2,1,0:T(8,128)(2,1)S(1)} collective-permute-done((bf16[4,96,256]{2,1,0:T(8,128)(2,1)S(1)}, bf16[4,96,256]{2,1,0:T(8,128)(2,1)S(1)}, u32[]{:S(2)}, u32[]{:S(2)}) %collective-permute-start.2) | collective-permute-done | bytes 196640 | tf_op jit(solution)/shard_map/ppermute | solution.py:37
  39.0 22.0 %all-to-all-done.q_ref.k_ref.v_ref.qkv_ref = bf16[32,480,128]{2,1,0:T(8,128)(2,1)} async-done(((bf16[32,480,128]{2,1,0:T(8,128)(2,1)}), bf16[32,480,128]{2,1,0:T(8,128)(2,1)}, u32[]{:S(2)}, u32[]{:S(2)}) %all-to-all-start) | async-done | bytes 3932192 | tf_op jit(solution)/shard_map/all_to_all | solution.py:29
  61.0 7.7 %all-to-all-start.1 = ((bf16[32,272,128]{2,1,0:T(8,128)(2,1)}), bf16[32,272,128]{2,1,0:T(8,128)(2,1)}, u32[]{:S(2)}, u32[]{:S(2)}) async-start(bf16[32,272,128]{2,1,0:T(8,128)(2,1)} %cross_heads.1), calls=%async_computation.1 | async-start | bytes 4456448 | tf_op jit(solution)/shard_map/all_to_all | solution.py:29
  68.7 1.2 slice.3
  69.9 0.7 collective-permute-start.3
  70.6 22.6 %self_attention.1.own = bf16[32,128,128]{2,1,0:T(8,128)(2,1)S(1)} custom-call(bf16[32,480,128]{2,1,0:T(8,128)(2,1)} %all-to-all-done.q_ref.k_ref.v_ref.qkv_ref, bf16[32,480,128]{2,1,0:T(8,128)(2,1)} %all-to-all-done.q_ref.k_ref.v_ref.qkv_ref, bf16[32,480,128]{2,1,0:T(8,128)(2,1)} %all-to-all-done.q_ref.k_ref.v_ref.qkv_ref), custom_call_target="tpu_custom_call" | custom-call | flops 17179869184 | bytes 4194304 | tf_op jit(solution)/shard_map/self_attention/pallas_call | solution.py:417
  93.2 0.0 collective-permute-done.3.other_ref
  93.2 2.3 %projected.1 = (bf16[1120,128]{1,0:T(8,128)(2,1)S(1)}, bf16[1120,128]{1,0:T(8,128)(2,1)S(1)}) custom-call(s32[2]{0:T(128)S(1)} %add_multiply_fusion.place_ref, bf16[32,480,128]{2,1,0:T(8,128)(2,1)} %all-to-all-done.q_ref.k_ref.v_ref.qkv_ref, bf16[32,96,128]{2,1,0:T(8,128)(2,1)S(1)} %collective-permute-done.3.other_ref, bf16[768,256]{1,0:T(8,128)(2,1)S(1)} %bitcast.12), custom_call_target="tpu_custom_call" | custom-call | flops 402653184 | bytes 2539520 | tf_op jit(solution)/shard_map/projected/pallas_call | solution.py:206
  95.5 2.7 %all-to-all-done.1.got = bf16[32,272,128]{2,1,0:T(8,128)(2,1)} async-done(((bf16[32,272,128]{2,1,0:T(8,128)(2,1)}), bf16[32,272,128]{2,1,0:T(8,128)(2,1)}, u32[]{:S(2)}, u32[]{:S(2)}) %all-to-all-start.1) | async-done | bytes 2228256 | tf_op jit(solution)/shard_map/all_to_all | solution.py:29
  98.2 5.7 %cross_attention.1 = (bf16[32,224,128]{2,1,0:T(8,128)(2,1)S(1)}, bf16[32,96,128]{2,1,0:T(8,128)(2,1)S(1)}, bf16[32,96,128]{2,1,0:T(8,128)(2,1)S(1)}) custom-call(s32[2]{0:T(128)S(1)} %add_multiply_fusion.place_ref, bf16[32,272,128]{2,1,0:T(8,128)(2,1)} %all-to-all-done.1.got, bf16[32,128,128]{2,1,0:T(8,128)(2,1)S(1)} %self_attention.1.own, ...), custom_call_target="tpu_custom_call" | custom-call | flops 1073741824 | bytes 6815744 | tf_op jit(solution)/shard_map/cross_attention/pallas_call | solution.py:321
  103.8 2.6 %collective-permute-start.4 = (bf16[32,96,128]{2,1,0:T(8,128)(2,1)S(1)}, bf16[32,96,128]{2,1,0:T(8,128)(2,1)S(1)}, u32[]{:S(2)}, u32[]{:S(2)}) collective-permute-start(bf16[32,96,128]{2,1,0:T(8,128)(2,1)S(1)} %get-tuple-element.27), channel_id=1, source_target_pairs={{0,8},{8,0},{16,24},{24,16},{32,40},{40,32},{48,56},{56,48},{64,72... | collective-permute-start | bytes 2359304 | tf_op jit(solution)/shard_map/ppermute | solution.py:48
  106.5 1.9 %collective-permute-done.4 = bf16[32,96,128]{2,1,0:T(8,128)(2,1)S(1)} collective-permute-done((bf16[32,96,128]{2,1,0:T(8,128)(2,1)S(1)}, bf16[32,96,128]{2,1,0:T(8,128)(2,1)S(1)}, u32[]{:S(2)}, u32[]{:S(2)}) %collective-permute-start.4) | collective-permute-done | bytes 786464 | tf_op jit(solution)/shard_map/ppermute | solution.py:48
  108.4 0.3 fusion
  108.6 28.6 %all_to_all.15.got_ref = bf16[32,224,128]{2,1,0:T(8,128)(2,1)S(1)} all-to-all(bf16[32,224,128]{2,1,0:T(8,128)(2,1)S(1)} %fusion), channel_id=1, replica_groups=mesh['seq'=32,'fsdp'=8] {'seq'}, dimensions={0} | all-to-all | bytes 3670016 | tf_op jit(solution)/shard_map/all_to_all | solution.py:29
  137.2 1.2 arrived.1
  (7 shorter events, 0.1 us)
Async XLA Ops:
  4.7 8.7 %copy-start = (bf16[96,128]{1,0:T(8,128)(2,1)S(1)}, bf16[96,128]{1,0:T(8,128)(2,1)}, u32[]{:S(2)}) copy-start(bf16[96,128]{1,0:T(8,128)(2,1)} %param.16) | copy-start | bytes 73732
  4.8 8.7 %copy-start.1 = (bf16[96,128]{1,0:T(8,128)(2,1)S(1)}, bf16[96,128]{1,0:T(8,128)(2,1)}, u32[]{:S(2)}) copy-start(bf16[96,128]{1,0:T(8,128)(2,1)} %param.15) | copy-start | bytes 73732
  4.8 56.2 %all-to-all-start = ((bf16[32,480,128]{2,1,0:T(8,128)(2,1)}), bf16[32,480,128]{2,1,0:T(8,128)(2,1)}, u32[]{:S(2)}, u32[]{:S(2)}) async-start(bf16[32,480,128]{2,1,0:T(8,128)(2,1)} %self_heads.1), calls=%async_computation | async-start | bytes 7864320 | tf_op jit(solution)/shard_map/all_to_all | solution.py:29
  13.5 3.6 %collective-permute-start = (bf16[1,96,256]{2,1,0:T(8,128)(2,1)S(1)}, bf16[1,96,256]{2,1,0:T(8,128)(2,1)S(1)}, u32[]{:S(2)}, u32[]{:S(2)}) collective-permute-start(bf16[1,96,256]{2,1,0:T(8,128)(2,1)S(1)} %maximum_bitcast_fusion), channel_id=1, source_target_pairs={{0,1},{1,0},{2,3},{3,2},{4,5},{5,4},{6,7},{7,6},{8,9},{9,8},{10,11... | collective-permute-start | bytes 147464 | tf_op jit(solution)/shard_map/ppermute | solution.py:37
  17.1 5.5 %collective-permute-start.1 = (bf16[2,96,256]{2,1,0:T(8,128)(2,1)S(1)}, bf16[2,96,256]{2,1,0:T(8,128)(2,1)S(1)}, u32[]{:S(2)}, u32[]{:S(2)}) collective-permute-start(bf16[2,96,256]{2,1,0:T(8,128)(2,1)S(1)} %pad_maximum_fusion.2), channel_id=1, source_target_pairs={{0,2},{1,3},{2,0},{3,1},{4,6},{5,7},{6,4},{7,5},{8,10},{9,11},{10,... | collective-permute-start | bytes 294920 | tf_op jit(solution)/shard_map/ppermute | solution.py:37
  22.6 16.3 %collective-permute-start.2 = (bf16[4,96,256]{2,1,0:T(8,128)(2,1)S(1)}, bf16[4,96,256]{2,1,0:T(8,128)(2,1)S(1)}, u32[]{:S(2)}, u32[]{:S(2)}) collective-permute-start(bf16[4,96,256]{2,1,0:T(8,128)(2,1)S(1)} %pad_maximum_fusion.1), channel_id=1, source_target_pairs={{0,4},{1,5},{2,6},{3,7},{4,0},{5,1},{6,2},{7,3},{8,12},{9,13},{10,... | collective-permute-start | bytes 589832 | tf_op jit(solution)/shard_map/ppermute | solution.py:37
  61.0 37.2 %all-to-all-start.1 = ((bf16[32,272,128]{2,1,0:T(8,128)(2,1)}), bf16[32,272,128]{2,1,0:T(8,128)(2,1)}, u32[]{:S(2)}, u32[]{:S(2)}) async-start(bf16[32,272,128]{2,1,0:T(8,128)(2,1)} %cross_heads.1), calls=%async_computation.1 | async-start | bytes 4456448 | tf_op jit(solution)/shard_map/all_to_all | solution.py:29
  69.9 23.2 %collective-permute-start.3 = (bf16[32,96,128]{2,1,0:T(8,128)(2,1)S(1)}, bf16[32,96,128]{2,1,0:T(8,128)(2,1)S(1)}, u32[]{:S(2)}, u32[]{:S(2)}) collective-permute-start(bf16[32,96,128]{2,1,0:T(8,128)(2,1)S(1)} %slice.3), channel_id=1, source_target_pairs={{0,8},{8,0},{16,24},{24,16},{32,40},{40,32},{48,56},{56,48},{64,72... | collective-permute-start | bytes 2359304 | tf_op jit(solution)/shard_map/ppermute | solution.py:48
  103.8 4.5 %collective-permute-start.4 = (bf16[32,96,128]{2,1,0:T(8,128)(2,1)S(1)}, bf16[32,96,128]{2,1,0:T(8,128)(2,1)S(1)}, u32[]{:S(2)}, u32[]{:S(2)}) collective-permute-start(bf16[32,96,128]{2,1,0:T(8,128)(2,1)S(1)} %get-tuple-element.27), channel_id=1, source_target_pairs={{0,8},{8,0},{16,24},{24,16},{32,40},{40,32},{48,56},{56,48},{64,72... | collective-permute-start | bytes 2359304 | tf_op jit(solution)/shard_map/ppermute | solution.py:48

commit v8 on v7

--- a/solution.py
+++ b/solution.py
@@ -98,7 +98,7 @@
     _, rows, width = q_local.shape
     _, owned, features = audio.shape
     heads = width // HD
-    group = 4
+    group = 8
     total = 3 * rows + owned * (features // HD // 2)
     return pl.pallas_call(
         functools.partial(self_heads_kernel, group),
@@ -325,7 +325,7 @@
         out_specs=[whole(x) for x in results],
         out_shape=results,
         scratch_shapes=[pltpu.VMEM((padded, HD), F32), pltpu.VMEM((padded, HD), F32)],
-        compiler_params=kernel_params(48),
+        compiler_params=kernel_params(40),
         cost_estimate=pl.CostEstimate(
             flops=4 * sources * owned * features * HD + 10 * sources * rows * HD * HD,
             bytes_accessed=2 * (got.size + proj.size + 4 * own_heads.size),

time: 139 us -> 138 us (level)
  local copies, waits for them, and re-layouts: 1.21 us -> 3.4 us
    unnamed x4 -> x8, local copies, waits for them, and re-layouts: 0.01 us -> 2.2 us
where the time goes in v8:
time: 138 us
  Pallas kernels  38.6 us (28%)
  waiting for transfers between devices  33.4 us (24%)
  starting transfers between devices  32.4 us (23%)
  blocking collectives  28.7 us (21%)
  local copies, waits for them, and re-layouts  3.4 us (2%)
    all_to_all x1, blocking collectives, handed_over(): return lax.all_to_all(parts, 'seq', split_axis=0, concat_axis=0, tiled=True)  28.7 us
    all_to_all x2, waiting for transfers between devices, handed_over(): return lax.all_to_all(parts, 'seq', split_axis=0, concat_axis=0, tiled=True)  23.7 us
    pallas_call x1, Pallas kernels, attend_self(): pl.pallas_call(functools.partial(self_attention_kernel, block_rows, block...  22.6 us
    all_to_all x2, starting transfers between devices, handed_over(): return lax.all_to_all(parts, 'seq', split_axis=0, concat_axis=0, tiled=True)  15.7 us
    ppermute x3, starting transfers between devices, gathered_by_doubling(): other = lax.ppermute(block, axis, [(i, i ^ step) for i in range(size)])  13.5 us
    ppermute x3, waiting for transfers between devices, gathered_by_doubling(): other = lax.ppermute(block, axis, [(i, i ^ step) for i in range(size)])  7.76 us
    pallas_call x1, Pallas kernels, cross_attention(): pl.pallas_call(functools.partial(cross_kernel, rows), grid=(1,), in_specs...  4.56 us
    pallas_call x1, Pallas kernels, cross_heads(): pl.pallas_call(functools.partial(cross_heads_kernel, group), grid=(heads...  3.97 us
  transfers between devices with their start and end apart: 7, of which 6 were waited for; matrix products, arithmetic and copies ran while one was open for 1% of the time, Pallas kernels for 21%

profile of v8, /device:TPU:1, one launch (start us, length us, event | category | flops | bytes accessed | tf_op | source)
XLA Modules:
  0.0 137.8 jit_solution(17987692109626421698)
XLA Ops:
  0.6 3.9 %self_heads.1 = bf16[32,480,128]{2,1,0:T(8,128)(2,1)} custom-call(bf16[1,128,4096]{2,1,0:T(8,128)(2,1)} %q_hbm.1, bf16[1,128,4096]{2,1,0:T(8,128)(2,1)} %k_hbm.1, bf16[1,128,4096]{2,1,0:T(8,128)(2,1)} %v_hbm.1, bf16[1,32,768]{2,1,0:T(8,128)(2,1)} %audio_hbm.1), custom_call_target="tpu_custom_call" | custom-call | bytes 7340032 | tf_op jit(solution)/shard_map/self_heads/pallas_call | solution.py:103
  4.6 0.0 copy-start.2
  4.6 0.0 copy-start.3
  4.6 8.7 %all-to-all-start = ((bf16[32,480,128]{2,1,0:T(8,128)(2,1)}), bf16[32,480,128]{2,1,0:T(8,128)(2,1)}, u32[]{:S(2)}, u32[]{:S(2)}) async-start(bf16[32,480,128]{2,1,0:T(8,128)(2,1)} %self_heads.1), calls=%async_computation | async-start | bytes 7864320 | tf_op jit(solution)/shard_map/all_to_all | solution.py:29
  13.3 0.0 copy-done.2
  13.3 0.0 copy-done.3
  13.3 1.7 %collective-permute-start = (bf16[1,96,256]{2,1,0:T(8,128)(2,1)S(1)}, bf16[1,96,256]{2,1,0:T(8,128)(2,1)S(1)}, u32[]{:S(2)}, u32[]{:S(2)}) collective-permute-start(bf16[1,96,256]{2,1,0:T(8,128)(2,1)S(1)} %maximum_bitcast_fusion), channel_id=1, source_target_pairs={{0,1},{1,0},{2,3},{3,2},{4,5},{5,4},{6,7},{7,6},{8,9},{9,8},{10,11... | collective-permute-start | bytes 147464 | tf_op jit(solution)/shard_map/ppermute | solution.py:37
  15.0 1.9 %collective-permute-done = bf16[1,96,256]{2,1,0:T(8,128)(2,1)S(1)} collective-permute-done((bf16[1,96,256]{2,1,0:T(8,128)(2,1)S(1)}, bf16[1,96,256]{2,1,0:T(8,128)(2,1)S(1)}, u32[]{:S(2)}, u32[]{:S(2)}) %collective-permute-start) | collective-permute-done | bytes 49184 | tf_op jit(solution)/shard_map/ppermute | solution.py:37
  16.9 3.1 %collective-permute-start.1 = (bf16[2,96,256]{2,1,0:T(8,128)(2,1)S(1)}, bf16[2,96,256]{2,1,0:T(8,128)(2,1)S(1)}, u32[]{:S(2)}, u32[]{:S(2)}) collective-permute-start(bf16[2,96,256]{2,1,0:T(8,128)(2,1)S(1)} %pad_maximum_fusion.2), channel_id=1, source_target_pairs={{0,2},{1,3},{2,0},{3,1},{4,6},{5,7},{6,4},{7,5},{8,10},{9,11},{10,... | collective-permute-start | bytes 294920 | tf_op jit(solution)/shard_map/ppermute | solution.py:37
  20.0 2.4 %collective-permute-done.1 = bf16[2,96,256]{2,1,0:T(8,128)(2,1)S(1)} collective-permute-done((bf16[2,96,256]{2,1,0:T(8,128)(2,1)S(1)}, bf16[2,96,256]{2,1,0:T(8,128)(2,1)S(1)}, u32[]{:S(2)}, u32[]{:S(2)}) %collective-permute-start.1) | collective-permute-done | bytes 98336 | tf_op jit(solution)/shard_map/ppermute | solution.py:37
  22.5 8.7 %collective-permute-start.2 = (bf16[4,96,256]{2,1,0:T(8,128)(2,1)S(1)}, bf16[4,96,256]{2,1,0:T(8,128)(2,1)S(1)}, u32[]{:S(2)}, u32[]{:S(2)}) collective-permute-start(bf16[4,96,256]{2,1,0:T(8,128)(2,1)S(1)} %pad_maximum_fusion.1), channel_id=1, source_target_pairs={{0,4},{1,5},{2,6},{3,7},{4,0},{5,1},{6,2},{7,3},{8,12},{9,13},{10,... | collective-permute-start | bytes 589832 | tf_op jit(solution)/shard_map/ppermute | solution.py:37
  31.2 4.0 %cross_heads.1 = bf16[32,272,128]{2,1,0:T(8,128)(2,1)} custom-call(s32[2,4]{1,0:T(2,128)} %bitcast.14, s32[2]{0:T(128)} %bitcast.15, s32[1]{0:T(128)} %bitcast.2.first_ref, bf16[1,128,4096]{2,1,0:T(8,128)(2,1)} %q_ref, bf16[1,128,4096]{2,1,0:T(8,128)(2,1)} %grad_ref.1), custom_call_target="tpu_custom_call" | custom-call | bytes 4194304 | tf_op jit(solution)/shard_map/cross_heads/pallas_call | solution.py:150
  35.2 0.1 add_multiply_fusion.place_ref
  35.3 3.5 %collective-permute-done.2 = bf16[4,96,256]{2,1,0:T(8,128)(2,1)S(1)} collective-permute-done((bf16[4,96,256]{2,1,0:T(8,128)(2,1)S(1)}, bf16[4,96,256]{2,1,0:T(8,128)(2,1)S(1)}, u32[]{:S(2)}, u32[]{:S(2)}) %collective-permute-start.2) | collective-permute-done | bytes 196640 | tf_op jit(solution)/shard_map/ppermute | solution.py:37
  38.8 22.0 %all-to-all-done.q_ref.k_ref.v_ref.qkv_ref = bf16[32,480,128]{2,1,0:T(8,128)(2,1)} async-done(((bf16[32,480,128]{2,1,0:T(8,128)(2,1)}), bf16[32,480,128]{2,1,0:T(8,128)(2,1)}, u32[]{:S(2)}, u32[]{:S(2)}) %all-to-all-start) | async-done | bytes 3932192 | tf_op jit(solution)/shard_map/all_to_all | solution.py:29
  60.8 7.0 %all-to-all-start.1 = ((bf16[32,272,128]{2,1,0:T(8,128)(2,1)}), bf16[32,272,128]{2,1,0:T(8,128)(2,1)S(1)}, u32[]{:S(2)}, u32[]{:S(2)}) async-start(bf16[32,272,128]{2,1,0:T(8,128)(2,1)} %cross_heads.1), calls=%async_computation.1 | async-start | bytes 4456448 | tf_op jit(solution)/shard_map/all_to_all | solution.py:29
  67.9 1.2 slice.3
  69.1 0.6 collective-permute-start.3
  69.7 22.6 %self_attention.1.own = bf16[32,128,128]{2,1,0:T(8,128)(2,1)S(1)} custom-call(bf16[32,480,128]{2,1,0:T(8,128)(2,1)} %all-to-all-done.q_ref.k_ref.v_ref.qkv_ref, bf16[32,480,128]{2,1,0:T(8,128)(2,1)} %all-to-all-done.q_ref.k_ref.v_ref.qkv_ref, bf16[32,480,128]{2,1,0:T(8,128)(2,1)} %all-to-all-done.q_ref.k_ref.v_ref.qkv_ref), custom_call_target="tpu_custom_call" | custom-call | flops 17179869184 | bytes 4194304 | tf_op jit(solution)/shard_map/self_attention/pallas_call | solution.py:417
  92.3 0.0 copy-start
  92.3 1.0 copy-done
  93.2 0.0 collective-permute-done.3.other_ref
  93.2 2.3 %projected.1 = (bf16[1120,128]{1,0:T(8,128)(2,1)S(1)}, bf16[1120,128]{1,0:T(8,128)(2,1)S(1)}) custom-call(s32[2]{0:T(128)S(1)} %add_multiply_fusion.place_ref, bf16[32,480,128]{2,1,0:T(8,128)(2,1)} %all-to-all-done.q_ref.k_ref.v_ref.qkv_ref, bf16[32,96,128]{2,1,0:T(8,128)(2,1)S(1)} %collective-permute-done.3.other_ref, bf16[768,256]{1,0:T(8,128)(2,1)S(1)} %bitcast.12), custom_call_target="tpu_custom_call" | custom-call | flops 402653184 | bytes 2539520 | tf_op jit(solution)/shard_map/projected/pallas_call | solution.py:206
  95.6 1.7 %all-to-all-done.1.got = bf16[32,272,128]{2,1,0:T(8,128)(2,1)S(1)} async-done(((bf16[32,272,128]{2,1,0:T(8,128)(2,1)}), bf16[32,272,128]{2,1,0:T(8,128)(2,1)S(1)}, u32[]{:S(2)}, u32[]{:S(2)}) %all-to-all-start.1) | async-done | bytes 2228256 | tf_op jit(solution)/shard_map/all_to_all | solution.py:29
  97.3 0.0 copy-start.1
  97.3 1.2 copy-done.1
  98.5 4.6 %cross_attention.1 = (bf16[32,224,128]{2,1,0:T(8,128)(2,1)S(1)}, bf16[32,96,128]{2,1,0:T(8,128)(2,1)S(1)}, bf16[32,96,128]{2,1,0:T(8,128)(2,1)S(1)}) custom-call(s32[2]{0:T(128)S(1)} %add_multiply_fusion.place_ref, bf16[32,272,128]{2,1,0:T(8,128)(2,1)S(1)} %all-to-all-done.1.got, bf16[32,128,128]{2,1,0:T(8,128)(2,1)S(1)} %copy-done.1, ...), custom_call_target="tpu_custom_call" | custom-call | flops 1073741824 | bytes 6815744 | tf_op jit(solution)/shard_map/cross_attention/pallas_call | solution.py:321
  103.1 2.6 %collective-permute-start.4 = (bf16[32,96,128]{2,1,0:T(8,128)(2,1)S(1)}, bf16[32,96,128]{2,1,0:T(8,128)(2,1)S(1)}, u32[]{:S(2)}, u32[]{:S(2)}) collective-permute-start(bf16[32,96,128]{2,1,0:T(8,128)(2,1)S(1)} %get-tuple-element.27), channel_id=1, source_target_pairs={{0,8},{8,0},{16,24},{24,16},{32,40},{40,32},{48,56},{56,48},{64,72... | collective-permute-start | bytes 2359304 | tf_op jit(solution)/shard_map/ppermute | solution.py:48
  105.7 1.9 %collective-permute-done.4 = bf16[32,96,128]{2,1,0:T(8,128)(2,1)S(1)} collective-permute-done((bf16[32,96,128]{2,1,0:T(8,128)(2,1)S(1)}, bf16[32,96,128]{2,1,0:T(8,128)(2,1)S(1)}, u32[]{:S(2)}, u32[]{:S(2)}) %collective-permute-start.4) | collective-permute-done | bytes 786464 | tf_op jit(solution)/shard_map/ppermute | solution.py:48
  107.6 0.3 fusion
  107.8 28.7 %all_to_all.15.got_ref = bf16[32,224,128]{2,1,0:T(8,128)(2,1)S(1)} all-to-all(bf16[32,224,128]{2,1,0:T(8,128)(2,1)S(1)} %fusion), channel_id=1, replica_groups=mesh['seq'=32,'fsdp'=8] {'seq'}, dimensions={0} | all-to-all | bytes 3670016 | tf_op jit(solution)/shard_map/all_to_all | solution.py:29
  136.5 1.2 arrived.1
  (7 shorter events, 0.1 us)
Async XLA Ops:
  4.6 8.7 %copy-start.2 = (bf16[96,128]{1,0:T(8,128)(2,1)S(1)}, bf16[96,128]{1,0:T(8,128)(2,1)}, u32[]{:S(2)}) copy-start(bf16[96,128]{1,0:T(8,128)(2,1)} %param.16) | copy-start | bytes 73732
  4.6 8.7 %copy-start.3 = (bf16[96,128]{1,0:T(8,128)(2,1)S(1)}, bf16[96,128]{1,0:T(8,128)(2,1)}, u32[]{:S(2)}) copy-start(bf16[96,128]{1,0:T(8,128)(2,1)} %param.15) | copy-start | bytes 73732
  4.6 56.2 %all-to-all-start = ((bf16[32,480,128]{2,1,0:T(8,128)(2,1)}), bf16[32,480,128]{2,1,0:T(8,128)(2,1)}, u32[]{:S(2)}, u32[]{:S(2)}) async-start(bf16[32,480,128]{2,1,0:T(8,128)(2,1)} %self_heads.1), calls=%async_computation | async-start | bytes 7864320 | tf_op jit(solution)/shard_map/all_to_all | solution.py:29
  13.3 3.6 %collective-permute-start = (bf16[1,96,256]{2,1,0:T(8,128)(2,1)S(1)}, bf16[1,96,256]{2,1,0:T(8,128)(2,1)S(1)}, u32[]{:S(2)}, u32[]{:S(2)}) collective-permute-start(bf16[1,96,256]{2,1,0:T(8,128)(2,1)S(1)} %maximum_bitcast_fusion), channel_id=1, source_target_pairs={{0,1},{1,0},{2,3},{3,2},{4,5},{5,4},{6,7},{7,6},{8,9},{9,8},{10,11... | collective-permute-start | bytes 147464 | tf_op jit(solution)/shard_map/ppermute | solution.py:37
  16.9 5.5 %collective-permute-start.1 = (bf16[2,96,256]{2,1,0:T(8,128)(2,1)S(1)}, bf16[2,96,256]{2,1,0:T(8,128)(2,1)S(1)}, u32[]{:S(2)}, u32[]{:S(2)}) collective-permute-start(bf16[2,96,256]{2,1,0:T(8,128)(2,1)S(1)} %pad_maximum_fusion.2), channel_id=1, source_target_pairs={{0,2},{1,3},{2,0},{3,1},{4,6},{5,7},{6,4},{7,5},{8,10},{9,11},{10,... | collective-permute-start | bytes 294920 | tf_op jit(solution)/shard_map/ppermute | solution.py:37
  22.5 16.3 %collective-permute-start.2 = (bf16[4,96,256]{2,1,0:T(8,128)(2,1)S(1)}, bf16[4,96,256]{2,1,0:T(8,128)(2,1)S(1)}, u32[]{:S(2)}, u32[]{:S(2)}) collective-permute-start(bf16[4,96,256]{2,1,0:T(8,128)(2,1)S(1)} %pad_maximum_fusion.1), channel_id=1, source_target_pairs={{0,4},{1,5},{2,6},{3,7},{4,0},{5,1},{6,2},{7,3},{8,12},{9,13},{10,... | collective-permute-start | bytes 589832 | tf_op jit(solution)/shard_map/ppermute | solution.py:37
  60.8 36.4 %all-to-all-start.1 = ((bf16[32,272,128]{2,1,0:T(8,128)(2,1)}), bf16[32,272,128]{2,1,0:T(8,128)(2,1)S(1)}, u32[]{:S(2)}, u32[]{:S(2)}) async-start(bf16[32,272,128]{2,1,0:T(8,128)(2,1)} %cross_heads.1), calls=%async_computation.1 | async-start | bytes 4456448 | tf_op jit(solution)/shard_map/all_to_all | solution.py:29
  69.1 24.2 %collective-permute-start.3 = (bf16[32,96,128]{2,1,0:T(8,128)(2,1)S(1)}, bf16[32,96,128]{2,1,0:T(8,128)(2,1)S(1)}, u32[]{:S(2)}, u32[]{:S(2)}) collective-permute-start(bf16[32,96,128]{2,1,0:T(8,128)(2,1)S(1)} %slice.3), channel_id=1, source_target_pairs={{0,8},{8,0},{16,24},{24,16},{32,40},{40,32},{48,56},{56,48},{64,72... | collective-permute-start | bytes 2359304 | tf_op jit(solution)/shard_map/ppermute | solution.py:48
  92.3 1.0 copy-start
  97.3 1.2 copy-start.1
  103.1 4.5 %collective-permute-start.4 = (bf16[32,96,128]{2,1,0:T(8,128)(2,1)S(1)}, bf16[32,96,128]{2,1,0:T(8,128)(2,1)S(1)}, u32[]{:S(2)}, u32[]{:S(2)}) collective-permute-start(bf16[32,96,128]{2,1,0:T(8,128)(2,1)S(1)} %get-tuple-element.27), channel_id=1, source_target_pairs={{0,8},{8,0},{16,24},{24,16},{32,40},{40,32},{48,56},{56,48},{64,72... | collective-permute-start | bytes 2359304 | tf_op jit(solution)/shard_map/ppermute | solution.py:48

commit v9 on v8

--- a/solution.py
+++ b/solution.py
@@ -59,6 +59,8 @@
     rows = loaded.shape[1]
     owned, features = audio.shape
     chunks = features // HD // 2
+    audio_load = pltpu.make_async_copy(audio_hbm.at[0], audio, audio_sem)
+    audio_load.start()
     loads = []
     for first in range(0, heads, group):
         cols = pl.ds(first * HD, group * HD)
@@ -71,8 +73,6 @@
         for copy in part:
             copy.start()
         loads.append(part)
-    audio_load = pltpu.make_async_copy(audio_hbm.at[0], audio, audio_sem)
-    audio_load.start()
     audio_load.wait()
     stores = []
     for part in range(len(loads)):

time: 138 us -> 138 us (level)
  no operation moved by 1% of the time
where the time goes in v9:
time: 138 us
  Pallas kernels  38.5 us (28%)
  waiting for transfers between devices  33.4 us (24%)
  starting transfers between devices  32.5 us (24%)
  blocking collectives  28.7 us (21%)
  local copies, waits for them, and re-layouts  3.4 us (2%)
    all_to_all x1, blocking collectives, handed_over(): return lax.all_to_all(parts, 'seq', split_axis=0, concat_axis=0, tiled=True)  28.7 us
    all_to_all x2, waiting for transfers between devices, handed_over(): return lax.all_to_all(parts, 'seq', split_axis=0, concat_axis=0, tiled=True)  23.7 us
    pallas_call x1, Pallas kernels, attend_self(): pl.pallas_call(functools.partial(self_attention_kernel, block_rows, block...  22.6 us
    all_to_all x2, starting transfers between devices, handed_over(): return lax.all_to_all(parts, 'seq', split_axis=0, concat_axis=0, tiled=True)  15.7 us
    ppermute x3, starting transfers between devices, gathered_by_doubling(): other = lax.ppermute(block, axis, [(i, i ^ step) for i in range(size)])  13.5 us
    ppermute x3, waiting for transfers between devices, gathered_by_doubling(): other = lax.ppermute(block, axis, [(i, i ^ step) for i in range(size)])  7.76 us
    pallas_call x1, Pallas kernels, cross_attention(): pl.pallas_call(functools.partial(cross_kernel, rows), grid=(1,), in_specs...  4.55 us
    pallas_call x1, Pallas kernels, cross_heads(): pl.pallas_call(functools.partial(cross_heads_kernel, group), grid=(heads...  3.97 us
  transfers between devices with their start and end apart: 7, of which 6 were waited for; matrix products, arithmetic and copies ran while one was open for 1% of the time, Pallas kernels for 21%

profile of v9, /device:TPU:1, one launch (start us, length us, event | category | flops | bytes accessed | tf_op | source)
XLA Modules:
  0.0 137.7 jit_solution(15519805030651964850)
XLA Ops:
  0.6 3.9 %self_heads.1 = bf16[32,480,128]{2,1,0:T(8,128)(2,1)} custom-call(bf16[1,128,4096]{2,1,0:T(8,128)(2,1)} %q_hbm.1, bf16[1,128,4096]{2,1,0:T(8,128)(2,1)} %k_hbm.1, bf16[1,128,4096]{2,1,0:T(8,128)(2,1)} %v_hbm.1, bf16[1,32,768]{2,1,0:T(8,128)(2,1)} %audio_hbm.1), custom_call_target="tpu_custom_call" | custom-call | bytes 7340032 | tf_op jit(solution)/shard_map/self_heads/pallas_call | solution.py:103
  4.5 0.0 copy-start.2
  4.5 0.0 copy-start.3
  4.5 8.7 %all-to-all-start = ((bf16[32,480,128]{2,1,0:T(8,128)(2,1)}), bf16[32,480,128]{2,1,0:T(8,128)(2,1)}, u32[]{:S(2)}, u32[]{:S(2)}) async-start(bf16[32,480,128]{2,1,0:T(8,128)(2,1)} %self_heads.1), calls=%async_computation | async-start | bytes 7864320 | tf_op jit(solution)/shard_map/all_to_all | solution.py:29
  13.2 0.0 copy-done.2
  13.2 0.0 copy-done.3
  13.2 1.7 %collective-permute-start = (bf16[1,96,256]{2,1,0:T(8,128)(2,1)S(1)}, bf16[1,96,256]{2,1,0:T(8,128)(2,1)S(1)}, u32[]{:S(2)}, u32[]{:S(2)}) collective-permute-start(bf16[1,96,256]{2,1,0:T(8,128)(2,1)S(1)} %maximum_bitcast_fusion), channel_id=1, source_target_pairs={{0,1},{1,0},{2,3},{3,2},{4,5},{5,4},{6,7},{7,6},{8,9},{9,8},{10,11... | collective-permute-start | bytes 147464 | tf_op jit(solution)/shard_map/ppermute | solution.py:37
  14.9 1.9 %collective-permute-done = bf16[1,96,256]{2,1,0:T(8,128)(2,1)S(1)} collective-permute-done((bf16[1,96,256]{2,1,0:T(8,128)(2,1)S(1)}, bf16[1,96,256]{2,1,0:T(8,128)(2,1)S(1)}, u32[]{:S(2)}, u32[]{:S(2)}) %collective-permute-start) | collective-permute-done | bytes 49184 | tf_op jit(solution)/shard_map/ppermute | solution.py:37
  16.9 3.1 %collective-permute-start.1 = (bf16[2,96,256]{2,1,0:T(8,128)(2,1)S(1)}, bf16[2,96,256]{2,1,0:T(8,128)(2,1)S(1)}, u32[]{:S(2)}, u32[]{:S(2)}) collective-permute-start(bf16[2,96,256]{2,1,0:T(8,128)(2,1)S(1)} %pad_maximum_fusion.2), channel_id=1, source_target_pairs={{0,2},{1,3},{2,0},{3,1},{4,6},{5,7},{6,4},{7,5},{8,10},{9,11},{10,... | collective-permute-start | bytes 294920 | tf_op jit(solution)/shard_map/ppermute | solution.py:37
  19.9 2.4 %collective-permute-done.1 = bf16[2,96,256]{2,1,0:T(8,128)(2,1)S(1)} collective-permute-done((bf16[2,96,256]{2,1,0:T(8,128)(2,1)S(1)}, bf16[2,96,256]{2,1,0:T(8,128)(2,1)S(1)}, u32[]{:S(2)}, u32[]{:S(2)}) %collective-permute-start.1) | collective-permute-done | bytes 98336 | tf_op jit(solution)/shard_map/ppermute | solution.py:37
  22.4 8.7 %collective-permute-start.2 = (bf16[4,96,256]{2,1,0:T(8,128)(2,1)S(1)}, bf16[4,96,256]{2,1,0:T(8,128)(2,1)S(1)}, u32[]{:S(2)}, u32[]{:S(2)}) collective-permute-start(bf16[4,96,256]{2,1,0:T(8,128)(2,1)S(1)} %pad_maximum_fusion.1), channel_id=1, source_target_pairs={{0,4},{1,5},{2,6},{3,7},{4,0},{5,1},{6,2},{7,3},{8,12},{9,13},{10,... | collective-permute-start | bytes 589832 | tf_op jit(solution)/shard_map/ppermute | solution.py:37
  31.1 4.0 %cross_heads.1 = bf16[32,272,128]{2,1,0:T(8,128)(2,1)} custom-call(s32[2,4]{1,0:T(2,128)} %bitcast.14, s32[2]{0:T(128)} %bitcast.15, s32[1]{0:T(128)} %bitcast.2.first_ref, bf16[1,128,4096]{2,1,0:T(8,128)(2,1)} %q_ref, bf16[1,128,4096]{2,1,0:T(8,128)(2,1)} %grad_ref.1), custom_call_target="tpu_custom_call" | custom-call | bytes 4194304 | tf_op jit(solution)/shard_map/cross_heads/pallas_call | solution.py:150
  35.1 0.1 add_multiply_fusion.place_ref
  35.2 3.5 %collective-permute-done.2 = bf16[4,96,256]{2,1,0:T(8,128)(2,1)S(1)} collective-permute-done((bf16[4,96,256]{2,1,0:T(8,128)(2,1)S(1)}, bf16[4,96,256]{2,1,0:T(8,128)(2,1)S(1)}, u32[]{:S(2)}, u32[]{:S(2)}) %collective-permute-start.2) | collective-permute-done | bytes 196640 | tf_op jit(solution)/shard_map/ppermute | solution.py:37
  38.7 22.0 %all-to-all-done.q_ref.k_ref.v_ref.qkv_ref = bf16[32,480,128]{2,1,0:T(8,128)(2,1)} async-done(((bf16[32,480,128]{2,1,0:T(8,128)(2,1)}), bf16[32,480,128]{2,1,0:T(8,128)(2,1)}, u32[]{:S(2)}, u32[]{:S(2)}) %all-to-all-start) | async-done | bytes 3932192 | tf_op jit(solution)/shard_map/all_to_all | solution.py:29
  60.8 7.0 %all-to-all-start.1 = ((bf16[32,272,128]{2,1,0:T(8,128)(2,1)}), bf16[32,272,128]{2,1,0:T(8,128)(2,1)S(1)}, u32[]{:S(2)}, u32[]{:S(2)}) async-start(bf16[32,272,128]{2,1,0:T(8,128)(2,1)} %cross_heads.1), calls=%async_computation.1 | async-start | bytes 4456448 | tf_op jit(solution)/shard_map/all_to_all | solution.py:29
  67.8 1.2 slice.3
  69.0 0.6 collective-permute-start.3
  69.6 22.6 %self_attention.1.own = bf16[32,128,128]{2,1,0:T(8,128)(2,1)S(1)} custom-call(bf16[32,480,128]{2,1,0:T(8,128)(2,1)} %all-to-all-done.q_ref.k_ref.v_ref.qkv_ref, bf16[32,480,128]{2,1,0:T(8,128)(2,1)} %all-to-all-done.q_ref.k_ref.v_ref.qkv_ref, bf16[32,480,128]{2,1,0:T(8,128)(2,1)} %all-to-all-done.q_ref.k_ref.v_ref.qkv_ref), custom_call_target="tpu_custom_call" | custom-call | flops 17179869184 | bytes 4194304 | tf_op jit(solution)/shard_map/self_attention/pallas_call | solution.py:417
  92.2 0.0 copy-start
  92.2 1.0 copy-done
  93.2 0.0 collective-permute-done.3.other_ref
  93.2 2.3 %projected.1 = (bf16[1120,128]{1,0:T(8,128)(2,1)S(1)}, bf16[1120,128]{1,0:T(8,128)(2,1)S(1)}) custom-call(s32[2]{0:T(128)S(1)} %add_multiply_fusion.place_ref, bf16[32,480,128]{2,1,0:T(8,128)(2,1)} %all-to-all-done.q_ref.k_ref.v_ref.qkv_ref, bf16[32,96,128]{2,1,0:T(8,128)(2,1)S(1)} %collective-permute-done.3.other_ref, bf16[768,256]{1,0:T(8,128)(2,1)S(1)} %bitcast.12), custom_call_target="tpu_custom_call" | custom-call | flops 402653184 | bytes 2539520 | tf_op jit(solution)/shard_map/projected/pallas_call | solution.py:206
  95.5 1.7 %all-to-all-done.1.got = bf16[32,272,128]{2,1,0:T(8,128)(2,1)S(1)} async-done(((bf16[32,272,128]{2,1,0:T(8,128)(2,1)}), bf16[32,272,128]{2,1,0:T(8,128)(2,1)S(1)}, u32[]{:S(2)}, u32[]{:S(2)}) %all-to-all-start.1) | async-done | bytes 2228256 | tf_op jit(solution)/shard_map/all_to_all | solution.py:29
  97.2 0.0 copy-start.1
  97.2 1.2 copy-done.1
  98.4 4.6 %cross_attention.1 = (bf16[32,224,128]{2,1,0:T(8,128)(2,1)S(1)}, bf16[32,96,128]{2,1,0:T(8,128)(2,1)S(1)}, bf16[32,96,128]{2,1,0:T(8,128)(2,1)S(1)}) custom-call(s32[2]{0:T(128)S(1)} %add_multiply_fusion.place_ref, bf16[32,272,128]{2,1,0:T(8,128)(2,1)S(1)} %all-to-all-done.1.got, bf16[32,128,128]{2,1,0:T(8,128)(2,1)S(1)} %copy-done.1, ...), custom_call_target="tpu_custom_call" | custom-call | flops 1073741824 | bytes 6815744 | tf_op jit(solution)/shard_map/cross_attention/pallas_call | solution.py:321
  103.0 2.6 %collective-permute-start.4 = (bf16[32,96,128]{2,1,0:T(8,128)(2,1)S(1)}, bf16[32,96,128]{2,1,0:T(8,128)(2,1)S(1)}, u32[]{:S(2)}, u32[]{:S(2)}) collective-permute-start(bf16[32,96,128]{2,1,0:T(8,128)(2,1)S(1)} %get-tuple-element.27), channel_id=1, source_target_pairs={{0,8},{8,0},{16,24},{24,16},{32,40},{40,32},{48,56},{56,48},{64,72... | collective-permute-start | bytes 2359304 | tf_op jit(solution)/shard_map/ppermute | solution.py:48
  105.6 1.9 %collective-permute-done.4 = bf16[32,96,128]{2,1,0:T(8,128)(2,1)S(1)} collective-permute-done((bf16[32,96,128]{2,1,0:T(8,128)(2,1)S(1)}, bf16[32,96,128]{2,1,0:T(8,128)(2,1)S(1)}, u32[]{:S(2)}, u32[]{:S(2)}) %collective-permute-start.4) | collective-permute-done | bytes 786464 | tf_op jit(solution)/shard_map/ppermute | solution.py:48
  107.5 0.3 fusion
  107.8 28.7 %all_to_all.15.got_ref = bf16[32,224,128]{2,1,0:T(8,128)(2,1)S(1)} all-to-all(bf16[32,224,128]{2,1,0:T(8,128)(2,1)S(1)} %fusion), channel_id=1, replica_groups=mesh['seq'=32,'fsdp'=8] {'seq'}, dimensions={0} | all-to-all | bytes 3670016 | tf_op jit(solution)/shard_map/all_to_all | solution.py:29
  136.5 1.2 arrived.1
  (7 shorter events, 0.1 us)
Async XLA Ops:
  4.5 8.7 %copy-start.2 = (bf16[96,128]{1,0:T(8,128)(2,1)S(1)}, bf16[96,128]{1,0:T(8,128)(2,1)}, u32[]{:S(2)}) copy-start(bf16[96,128]{1,0:T(8,128)(2,1)} %param.16) | copy-start | bytes 73732
  4.5 8.7 %copy-start.3 = (bf16[96,128]{1,0:T(8,128)(2,1)S(1)}, bf16[96,128]{1,0:T(8,128)(2,1)}, u32[]{:S(2)}) copy-start(bf16[96,128]{1,0:T(8,128)(2,1)} %param.15) | copy-start | bytes 73732
  4.5 56.2 %all-to-all-start = ((bf16[32,480,128]{2,1,0:T(8,128)(2,1)}), bf16[32,480,128]{2,1,0:T(8,128)(2,1)}, u32[]{:S(2)}, u32[]{:S(2)}) async-start(bf16[32,480,128]{2,1,0:T(8,128)(2,1)} %self_heads.1), calls=%async_computation | async-start | bytes 7864320 | tf_op jit(solution)/shard_map/all_to_all | solution.py:29
  13.2 3.6 %collective-permute-start = (bf16[1,96,256]{2,1,0:T(8,128)(2,1)S(1)}, bf16[1,96,256]{2,1,0:T(8,128)(2,1)S(1)}, u32[]{:S(2)}, u32[]{:S(2)}) collective-permute-start(bf16[1,96,256]{2,1,0:T(8,128)(2,1)S(1)} %maximum_bitcast_fusion), channel_id=1, source_target_pairs={{0,1},{1,0},{2,3},{3,2},{4,5},{5,4},{6,7},{7,6},{8,9},{9,8},{10,11... | collective-permute-start | bytes 147464 | tf_op jit(solution)/shard_map/ppermute | solution.py:37
  16.9 5.5 %collective-permute-start.1 = (bf16[2,96,256]{2,1,0:T(8,128)(2,1)S(1)}, bf16[2,96,256]{2,1,0:T(8,128)(2,1)S(1)}, u32[]{:S(2)}, u32[]{:S(2)}) collective-permute-start(bf16[2,96,256]{2,1,0:T(8,128)(2,1)S(1)} %pad_maximum_fusion.2), channel_id=1, source_target_pairs={{0,2},{1,3},{2,0},{3,1},{4,6},{5,7},{6,4},{7,5},{8,10},{9,11},{10,... | collective-permute-start | bytes 294920 | tf_op jit(solution)/shard_map/ppermute | solution.py:37
  22.4 16.3 %collective-permute-start.2 = (bf16[4,96,256]{2,1,0:T(8,128)(2,1)S(1)}, bf16[4,96,256]{2,1,0:T(8,128)(2,1)S(1)}, u32[]{:S(2)}, u32[]{:S(2)}) collective-permute-start(bf16[4,96,256]{2,1,0:T(8,128)(2,1)S(1)} %pad_maximum_fusion.1), channel_id=1, source_target_pairs={{0,4},{1,5},{2,6},{3,7},{4,0},{5,1},{6,2},{7,3},{8,12},{9,13},{10,... | collective-permute-start | bytes 589832 | tf_op jit(solution)/shard_map/ppermute | solution.py:37
  60.8 36.4 %all-to-all-start.1 = ((bf16[32,272,128]{2,1,0:T(8,128)(2,1)}), bf16[32,272,128]{2,1,0:T(8,128)(2,1)S(1)}, u32[]{:S(2)}, u32[]{:S(2)}) async-start(bf16[32,272,128]{2,1,0:T(8,128)(2,1)} %cross_heads.1), calls=%async_computation.1 | async-start | bytes 4456448 | tf_op jit(solution)/shard_map/all_to_all | solution.py:29
  69.0 24.2 %collective-permute-start.3 = (bf16[32,96,128]{2,1,0:T(8,128)(2,1)S(1)}, bf16[32,96,128]{2,1,0:T(8,128)(2,1)S(1)}, u32[]{:S(2)}, u32[]{:S(2)}) collective-permute-start(bf16[32,96,128]{2,1,0:T(8,128)(2,1)S(1)} %slice.3), channel_id=1, source_target_pairs={{0,8},{8,0},{16,24},{24,16},{32,40},{40,32},{48,56},{56,48},{64,72... | collective-permute-start | bytes 2359304 | tf_op jit(solution)/shard_map/ppermute | solution.py:48
  92.2 1.0 copy-start
  97.2 1.2 copy-start.1
  103.0 4.5 %collective-permute-start.4 = (bf16[32,96,128]{2,1,0:T(8,128)(2,1)S(1)}, bf16[32,96,128]{2,1,0:T(8,128)(2,1)S(1)}, u32[]{:S(2)}, u32[]{:S(2)}) collective-permute-start(bf16[32,96,128]{2,1,0:T(8,128)(2,1)S(1)} %get-tuple-element.27), channel_id=1, source_target_pairs={{0,8},{8,0},{16,24},{24,16},{32,40},{40,32},{48,56},{56,48},{64,72... | collective-permute-start | bytes 2359304 | tf_op jit(solution)/shard_map/ppermute | solution.py:48
